TPU v7x, 32 devices: a whole 2x2x4 slice. The times are simulated.
32 devices in a mesh: section: 2 (over core), dp: 16 (over z, y, x).
Axes of the slice: x: 2, y: 2, z: 4, core: 2. Of those that a mesh axis runs over, the one named last changes fastest.
Arguments:
- enc_in: bfloat16 [32, 512, 768], P('dp'), may hold values from -6 to 6
- dec_in: bfloat16 [128, 768], P('dp'), may hold values from -6 to 6
- segment: int32 [32, 512], P('dp'), may hold values from 0 to 3, never falling along the last dimension, each value on 1 to 256 neighbouring positions
- d_out: bfloat16 [128, 768], P('dp'), may hold values from -6 to 6
- attn_gain: bfloat16 [2, 768], P('section', 'dp'), may hold values from 0.5 to 1.5
- w_query: bfloat16 [2, 768, 768], P('section', 'dp'), may hold values from -0.0390625 to 0.0390625
- w_key: bfloat16 [2, 768, 768], P('section', 'dp'), may hold values from -0.21875 to 0.21875
- w_value: bfloat16 [2, 768, 768], P('section', 'dp'), may hold values from -0.21875 to 0.21875
- w_out: bfloat16 [2, 768, 768], P('section', 'dp'), may hold values from -0.625 to 0.625
- ffn_gain: bfloat16 [2, 768], P('section', 'dp'), may hold values from 0.5 to 1.5
- w_in: bfloat16 [2, 768, 3072], P('section', 'dp'), may hold values from -0.21875 to 0.21875
- w_back: bfloat16 [2, 3072, 768], P('section', 'dp'), may hold values from -0.109375 to 0.109375
- self_gain: bfloat16 [768], P(('section', 'dp')), may hold values from 0.5 to 1.5
- self_value: bfloat16 [768, 768], P(('section', 'dp')), may hold values from -0.21875 to 0.21875
- self_out: bfloat16 [768, 768], P(('section', 'dp')), may hold values from -0.21875 to 0.21875
- rel_table: float32 [32, 12], replicated, may hold values from -4 to 4
Outputs:
- dec_out: bfloat16 [128, 768], P('dp', 'section')
- enc_in_grad: bfloat16 [32, 512, 768], P('dp', None, 'section')
- dec_in_grad: bfloat16 [128, 768], P('dp', 'section')
- g_attn_gain: float32 [2, 768], P('section', 'dp')
- g_w_query: float32 [2, 768, 768], P('section', 'dp')
- g_w_key: float32 [2, 768, 768], P('section', 'dp')
- g_w_value: float32 [2, 768, 768], P('section', 'dp')
- g_w_out: float32 [2, 768, 768], P('section', 'dp')
- g_ffn_gain: float32 [2, 768], P('section', 'dp')
- g_w_in: float32 [2, 768, 3072], P('section', 'dp')
- g_w_back: float32 [2, 3072, 768], P('section', 'dp')
- g_self_gain: float32 [768], P(('section', 'dp'))
- g_self_value: float32 [768, 768], P(('section', 'dp'))
- g_self_out: float32 [768, 768], P(('section', 'dp'))
- g_rel_table: float32 [32, 12], replicated
Inputs may be any that keep to these rules, and one draw needn't show every extreme that they name: `segment`: in each row the pair numbers never fall along the tokens, each of the 4 numbers covers 1 to 256 tokens, and one covers exactly 256.
All inputs are finite; a program needn't handle non-finite values.
Results may differ from a plain program's by a relative error of at most 0.025.
The roundings to bfloat16 on the way count: a program that leaves them out, or rounds other values in their place, can miss the bound.
Values may be sent and summed in bfloat16 or wider, within the bound.
No kernel may reach another device: no remote copies, remote signals or barrier semaphores. Data moves between devices by JAX's collectives and lax.ppermute only.
A program may use at most 448 MiB of HBM per device.

v0:
```python
import jax
import jax.numpy as jnp
import numpy as np
from jax import lax
from jax.sharding import PartitionSpec as P

D = 768
HEADS = 12
HEAD_DIM = 64
FF = 3072
BUCKETS = 32
MAX_DIST = 128
ROW_LEN = 512
SEGS = 4


epsilon = 1e-06
masked_score = -1000000000.0


def passed_along(value, axis, steps):
    count = lax.axis_size(axis)
    leading, last = (max(0, -steps), min(count, count - steps))
    return lax.ppermute(value, axis, [(source, source + steps) for source in range(leading, last)])


def bucket_matrix(length, buckets, reach_max):
    half_count = buckets // 2
    exact_count = half_count // 2
    exponent = half_count - exact_count
    growth = reach_max // exact_count
    by_distance = []
    for distance in range(length):
        if distance < exact_count:
            by_distance.append(distance)
        else:
            levels = 0
            while (
                levels < exponent
                and exact_count**exponent * growth ** (levels + 1) <= distance**exponent
            ):
                levels += 1
            by_distance.append(min(exact_count + levels, half_count - 1))
    by_distance = np.array(by_distance, dtype=np.int32)
    places = np.arange(length)
    offset = places[None, :] - places[:, None]
    return (np.where(offset > 0, half_count, 0) + by_distance[np.abs(offset)]).astype(np.int32)


def offset_onehot():
    full_table = bucket_matrix(ROW_LEN, BUCKETS, MAX_DIST)
    by_offset = np.concatenate([full_table[ROW_LEN - 1, :], full_table[0, 1:]]).astype(np.int32)
    labels = jnp.arange(BUCKETS, dtype=jnp.int32)
    return (jnp.asarray(by_offset)[None, :] == labels[:, None]).astype(jnp.float32)


def spread_offsets(per_offset):
    length = (per_offset.shape[1] + 1) // 2
    tiled = jnp.tile(per_offset, (1, length))
    window = tiled[:, length - 1 : length - 1 + length * (2 * length - 2)]
    return window.reshape(per_offset.shape[0], length, 2 * length - 2)[:, :, :length]


def bias_from_table(table):
    per_offset = jnp.dot(table.T, offset_onehot(), precision=lax.Precision.HIGHEST)
    return spread_offsets(per_offset)


def table_from_scores(score_sum):
    anchor = jnp.zeros((HEADS, 2 * ROW_LEN - 1), jnp.float32)
    primal, puller = jax.vjp(spread_offsets, anchor)
    per_offset = puller(score_sum)[0]
    return jnp.dot(offset_onehot(), per_offset.T, precision=lax.Precision.HIGHEST)


def rms_gain(values, gain):
    return values * lax.rsqrt(jnp.mean(values * values, axis=-1, keepdims=True) + epsilon) * gain


def gelu_tanh(pre_act):
    return jax.nn.gelu(pre_act, approximate=True)


def norm_back(values, gain, grad_out):
    primal, puller = jax.vjp(rms_gain, values, gain)
    return puller(grad_out)


def gelu_back(pre_act, grad_out):
    primal, puller = jax.vjp(gelu_tanh, pre_act)
    return puller(grad_out)[0]


def matmul(left_arr, right_arr):
    return jnp.dot(left_arr, right_arr, preferred_element_type=jnp.float32)


def times_transpose(grad_rows, weight):
    return lax.dot_general(
        grad_rows, weight, (((1,), (1,)), ((), ())), preferred_element_type=jnp.float32
    )


def weight_grad(act_rows, grad_rows):
    return lax.dot_general(
        act_rows, grad_rows, (((0,), (0,)), ((), ())), preferred_element_type=jnp.float32
    )


def split_heads(flat, row_count):
    return flat.reshape(row_count, flat.shape[0] // row_count, HEADS, HEAD_DIM)


def zeros_of(specs):
    return tuple((jnp.zeros(shape_spec, kind) for shape_spec, kind in specs))


def enc_blank(row_count):
    tokens = row_count * ROW_LEN
    flat_bf = ((tokens, D), jnp.bfloat16)
    kept = zeros_of(
        [
            flat_bf,
            flat_bf,
            flat_bf,
            flat_bf,
            ((row_count, HEADS, ROW_LEN), jnp.float32),
            flat_bf,
            ((tokens, D), jnp.float32),
            flat_bf,
            ((tokens, FF), jnp.float32),
            ((tokens, FF), jnp.bfloat16),
        ]
    )
    return (jnp.zeros((row_count, ROW_LEN, D), jnp.bfloat16), kept)


def dec_blank(row_count):
    pair_rows = row_count * SEGS
    tokens = row_count * ROW_LEN
    pair_bf = ((pair_rows, D), jnp.bfloat16)
    pair_fl = ((pair_rows, D), jnp.float32)
    token_bf = ((tokens, D), jnp.bfloat16)
    kept = zeros_of(
        [
            pair_bf,
            pair_bf,
            pair_fl,
            pair_bf,
            pair_bf,
            token_bf,
            token_bf,
            ((row_count, HEADS, SEGS), jnp.float32),
            pair_bf,
            pair_fl,
            pair_bf,
            ((pair_rows, FF), jnp.float32),
            ((pair_rows, FF), jnp.bfloat16),
        ]
    )
    return (jnp.zeros((pair_rows, D), jnp.bfloat16), kept)


def block_blank():
    return zeros_of(
        [
            ((1, D), jnp.float32),
            ((1, D, D), jnp.float32),
            ((1, D, D), jnp.float32),
            ((1, D, D), jnp.float32),
            ((1, D, D), jnp.float32),
            ((1, D), jnp.float32),
            ((1, D, FF), jnp.float32),
            ((1, FF, D), jnp.float32),
        ]
    )


def self_blank():
    return zeros_of([((D,), jnp.float32), ((D, D), jnp.float32), ((D, D), jnp.float32)])


def add_onto(totals, fresh):
    return tuple((total_part + fresh_part[None] for total_part, fresh_part in zip(totals, fresh)))


def self_scores(row_query, row_key, row_seg, score_bias):
    scores = (
        jnp.einsum("ihd,jhd->hij", row_query, row_key, preferred_element_type=jnp.float32)
        + score_bias
    )
    same_pair = row_seg[:, None] == row_seg[None, :]
    return jnp.where(same_pair[None], scores, masked_score)


def cross_scores(query_heads, key_heads, seg_rows):
    scores = jnp.einsum(
        "nshd,njhd->nhsj", query_heads, key_heads, preferred_element_type=jnp.float32
    )
    owner_mask = seg_rows[:, None, :] == jnp.arange(SEGS, dtype=jnp.int32)[None, :, None]
    return jnp.where(owner_mask[:, None], scores, masked_score)


def encode_forward(rows_in, seg_rows, weights, score_bias):
    attn_g, w_q, w_k, w_v, w_o, ffn_g, w_i, w_b = weights
    row_count = rows_in.shape[0]
    tokens = row_count * rows_in.shape[1]
    flat_in = rows_in.reshape(tokens, rows_in.shape[2]).astype(jnp.float32)
    normed = rms_gain(flat_in, attn_g.astype(jnp.float32)).astype(jnp.bfloat16)
    queries = matmul(normed, w_q).astype(jnp.bfloat16)
    key_rows = matmul(normed, w_k).astype(jnp.bfloat16)
    value_rows = matmul(normed, w_v).astype(jnp.bfloat16)

    def attend(pieces):
        row_query, row_key, row_value, row_seg = pieces
        scores = self_scores(row_query, row_key, row_seg, score_bias)
        row_max = jnp.max(scores, axis=-1, keepdims=True)
        exp_scores = jnp.exp(scores - row_max)
        row_total = jnp.sum(exp_scores, axis=-1, keepdims=True)
        attn_probs = (exp_scores / row_total).astype(jnp.bfloat16)
        row_context = jnp.einsum(
            "hij,jhd->ihd", attn_probs, row_value, preferred_element_type=jnp.float32
        )
        return (row_context.astype(jnp.bfloat16), (row_max + jnp.log(row_total))[:, :, 0])

    context, log_total = lax.map(
        attend,
        (
            split_heads(queries, row_count),
            split_heads(key_rows, row_count),
            split_heads(value_rows, row_count),
            seg_rows,
        ),
    )
    context = context.reshape(tokens, -1)
    residual = flat_in + matmul(context, w_o)
    normed_two = rms_gain(residual, ffn_g.astype(jnp.float32)).astype(jnp.bfloat16)
    pre_act = matmul(normed_two, w_i)
    hidden = gelu_tanh(pre_act).astype(jnp.bfloat16)
    encoded = (residual + matmul(hidden, w_b)).astype(jnp.bfloat16).reshape(rows_in.shape)
    return (
        encoded,
        (
            normed,
            queries,
            key_rows,
            value_rows,
            log_total,
            context,
            residual,
            normed_two,
            pre_act,
            hidden,
        ),
    )


def encode_backward(rows_in, seg_rows, weights, score_bias, kept, grad_enc, block_acc, table_acc):
    attn_g, w_q, w_k, w_v, w_o, ffn_g, w_i, w_b = weights
    (
        normed,
        queries,
        key_rows,
        value_rows,
        log_total,
        context,
        residual,
        normed_two,
        pre_act,
        hidden,
    ) = kept
    row_count = rows_in.shape[0]
    tokens = row_count * rows_in.shape[1]
    flat_in = rows_in.reshape(tokens, rows_in.shape[2]).astype(jnp.float32)
    grad_top = grad_enc.reshape(tokens, -1)
    g_back = weight_grad(hidden, grad_top)
    grad_pre = gelu_back(pre_act, times_transpose(grad_top, w_b)).astype(jnp.bfloat16)
    g_in = weight_grad(normed_two, grad_pre)
    grad_norm_two, g_ffn = norm_back(
        residual, ffn_g.astype(jnp.float32), times_transpose(grad_pre, w_i)
    )
    grad_residual = grad_top.astype(jnp.float32) + grad_norm_two
    grad_branch = grad_residual.astype(jnp.bfloat16)
    g_out = weight_grad(context, grad_branch)
    grad_context = times_transpose(grad_branch, w_o).astype(jnp.bfloat16)

    def attend_back(score_sum, pieces):
        row_query, row_key, row_value, row_seg, row_log, row_grad = pieces
        scores = self_scores(row_query, row_key, row_seg, score_bias)
        attn_probs = jnp.exp(scores - row_log[:, :, None])
        grad_value = jnp.einsum(
            "hij,ihd->jhd",
            attn_probs.astype(jnp.bfloat16),
            row_grad,
            preferred_element_type=jnp.float32,
        ).astype(jnp.bfloat16)
        grad_probs = jnp.einsum(
            "ihd,jhd->hij", row_grad, row_value, preferred_element_type=jnp.float32
        )
        inner_sum = jnp.sum(attn_probs * grad_probs, axis=-1, keepdims=True)
        grad_scores = (attn_probs * (grad_probs - inner_sum)).astype(jnp.bfloat16)
        grad_query = jnp.einsum(
            "hij,jhd->ihd", grad_scores, row_key, preferred_element_type=jnp.float32
        ).astype(jnp.bfloat16)
        grad_key = jnp.einsum(
            "hij,ihd->jhd", grad_scores, row_query, preferred_element_type=jnp.float32
        ).astype(jnp.bfloat16)
        return (score_sum + grad_scores.astype(jnp.float32), (grad_query, grad_key, grad_value))

    score_init = jnp.zeros((HEADS, ROW_LEN, ROW_LEN), jnp.float32)
    score_sum, grads_qkv = lax.scan(
        attend_back,
        score_init,
        (
            split_heads(queries, row_count),
            split_heads(key_rows, row_count),
            split_heads(value_rows, row_count),
            seg_rows,
            log_total,
            split_heads(grad_context, row_count),
        ),
    )
    grad_query = grads_qkv[0].reshape(tokens, -1)
    grad_key = grads_qkv[1].reshape(tokens, -1)
    grad_value = grads_qkv[2].reshape(tokens, -1)
    g_query = weight_grad(normed, grad_query)
    g_key = weight_grad(normed, grad_key)
    g_value = weight_grad(normed, grad_value)
    grad_normed = (
        times_transpose(grad_query, w_q)
        + times_transpose(grad_key, w_k)
        + times_transpose(grad_value, w_v)
    )
    grad_norm_one, g_attn = norm_back(flat_in, attn_g.astype(jnp.float32), grad_normed)
    grad_in = (grad_residual + grad_norm_one).astype(jnp.bfloat16).reshape(rows_in.shape)
    table_next = table_acc + table_from_scores(score_sum)
    blocks = add_onto(block_acc, (g_attn, g_query, g_key, g_value, g_out, g_ffn, g_in, g_back))
    return (grad_in, blocks, table_next)


def decode_forward(enc_rows, seg_rows, dec_rows, weights, self_weights):
    attn_g, w_q, w_k, w_v, w_o, ffn_g, w_i, w_b = weights
    self_g, self_v, self_o = self_weights
    row_count = enc_rows.shape[0]
    dec_flat = dec_rows.astype(jnp.float32)
    normed_self = rms_gain(dec_flat, self_g.astype(jnp.float32)).astype(jnp.bfloat16)
    self_vals = matmul(normed_self, self_v).astype(jnp.bfloat16)
    after_self = dec_flat + matmul(self_vals, self_o)
    normed_cross = rms_gain(after_self, attn_g.astype(jnp.float32)).astype(jnp.bfloat16)
    cross_query = matmul(normed_cross, w_q).astype(jnp.bfloat16)
    enc_flat = enc_rows.reshape(-1, enc_rows.shape[2])
    cross_key = matmul(enc_flat, w_k).astype(jnp.bfloat16)
    cross_value = matmul(enc_flat, w_v).astype(jnp.bfloat16)
    scores = cross_scores(
        split_heads(cross_query, row_count), split_heads(cross_key, row_count), seg_rows
    )
    row_max = jnp.max(scores, axis=-1, keepdims=True)
    exp_scores = jnp.exp(scores - row_max)
    row_total = jnp.sum(exp_scores, axis=-1, keepdims=True)
    attn_probs = (exp_scores / row_total).astype(jnp.bfloat16)
    context = (
        jnp.einsum(
            "nhsj,njhd->nshd",
            attn_probs,
            split_heads(cross_value, row_count),
            preferred_element_type=jnp.float32,
        )
        .astype(jnp.bfloat16)
        .reshape(dec_flat.shape[0], -1)
    )
    log_total = (row_max + jnp.log(row_total))[..., 0]
    after_cross = after_self + matmul(context, w_o)
    normed_ffn = rms_gain(after_cross, ffn_g.astype(jnp.float32)).astype(jnp.bfloat16)
    pre_act = matmul(normed_ffn, w_i)
    hidden = gelu_tanh(pre_act).astype(jnp.bfloat16)
    result = (after_cross + matmul(hidden, w_b)).astype(jnp.bfloat16)
    return (
        result,
        (
            normed_self,
            self_vals,
            after_self,
            normed_cross,
            cross_query,
            cross_key,
            cross_value,
            log_total,
            context,
            after_cross,
            normed_ffn,
            pre_act,
            hidden,
        ),
    )


def decode_backward(enc_rows, seg_rows, dec_rows, weights, self_weights, kept, grad_out, block_acc):
    attn_g, w_q, w_k, w_v, w_o, ffn_g, w_i, w_b = weights
    self_g, self_v, self_o = self_weights
    (
        normed_self,
        self_vals,
        after_self,
        normed_cross,
        cross_query,
        cross_key,
        cross_value,
        log_total,
        context,
        after_cross,
        normed_ffn,
        pre_act,
        hidden,
    ) = kept
    row_count = enc_rows.shape[0]
    width = dec_rows.shape[1]
    dec_flat = dec_rows.astype(jnp.float32)
    g_back = weight_grad(hidden, grad_out)
    grad_pre = gelu_back(pre_act, times_transpose(grad_out, w_b)).astype(jnp.bfloat16)
    g_in = weight_grad(normed_ffn, grad_pre)
    grad_norm_ffn, g_ffn = norm_back(
        after_cross, ffn_g.astype(jnp.float32), times_transpose(grad_pre, w_i)
    )
    grad_cross_res = grad_out.astype(jnp.float32) + grad_norm_ffn
    grad_branch = grad_cross_res.astype(jnp.bfloat16)
    g_out = weight_grad(context, grad_branch)
    grad_context = split_heads(times_transpose(grad_branch, w_o).astype(jnp.bfloat16), row_count)
    query_heads = split_heads(cross_query, row_count)
    key_heads = split_heads(cross_key, row_count)
    value_heads = split_heads(cross_value, row_count)
    scores = cross_scores(query_heads, key_heads, seg_rows)
    attn_probs = jnp.exp(scores - log_total[..., None])
    grad_value = (
        jnp.einsum(
            "nhsj,nshd->njhd",
            attn_probs.astype(jnp.bfloat16),
            grad_context,
            preferred_element_type=jnp.float32,
        )
        .astype(jnp.bfloat16)
        .reshape(-1, width)
    )
    grad_probs = jnp.einsum(
        "nshd,njhd->nhsj", grad_context, value_heads, preferred_element_type=jnp.float32
    )
    inner_sum = jnp.sum(attn_probs * grad_probs, axis=-1, keepdims=True)
    grad_scores = (attn_probs * (grad_probs - inner_sum)).astype(jnp.bfloat16)
    grad_query = (
        jnp.einsum("nhsj,njhd->nshd", grad_scores, key_heads, preferred_element_type=jnp.float32)
        .astype(jnp.bfloat16)
        .reshape(-1, width)
    )
    grad_key = (
        jnp.einsum("nhsj,nshd->njhd", grad_scores, query_heads, preferred_element_type=jnp.float32)
        .astype(jnp.bfloat16)
        .reshape(-1, width)
    )
    enc_flat = enc_rows.reshape(-1, width)
    g_query = weight_grad(normed_cross, grad_query)
    g_key = weight_grad(enc_flat, grad_key)
    g_value = weight_grad(enc_flat, grad_value)
    grad_enc = (
        (times_transpose(grad_key, w_k) + times_transpose(grad_value, w_v))
        .astype(jnp.bfloat16)
        .reshape(enc_rows.shape)
    )
    grad_norm_cross, g_attn = norm_back(
        after_self, attn_g.astype(jnp.float32), times_transpose(grad_query, w_q)
    )
    grad_self_res = grad_cross_res + grad_norm_cross
    grad_self_branch = grad_self_res.astype(jnp.bfloat16)
    g_self_out = weight_grad(self_vals, grad_self_branch)
    grad_self_vals = times_transpose(grad_self_branch, self_o).astype(jnp.bfloat16)
    g_self_value = weight_grad(normed_self, grad_self_vals)
    grad_norm_self, g_self_gain = norm_back(
        dec_flat, self_g.astype(jnp.float32), times_transpose(grad_self_vals, self_v)
    )
    grad_dec = (grad_self_res + grad_norm_self).astype(jnp.bfloat16)
    blocks = add_onto(block_acc, (g_attn, g_query, g_key, g_value, g_out, g_ffn, g_in, g_back))
    self_next = (g_self_gain, g_self_value, g_self_out)
    return (grad_enc, grad_dec, blocks, self_next)


def spread_block(blocks):
    attn_part, query_part, key_part, value_part, out_part, ffn_part, in_part, back_part = blocks
    return (
        lax.psum_scatter(attn_part, "dp", scatter_dimension=1, tiled=True),
        lax.psum_scatter(query_part, "dp", scatter_dimension=1, tiled=True),
        lax.psum_scatter(key_part, "dp", scatter_dimension=1, tiled=True),
        lax.psum_scatter(value_part, "dp", scatter_dimension=1, tiled=True),
        lax.psum_scatter(out_part, "dp", scatter_dimension=1, tiled=True),
        lax.psum_scatter(ffn_part, "dp", scatter_dimension=1, tiled=True),
        lax.psum_scatter(in_part, "dp", scatter_dimension=1, tiled=True),
        lax.psum_scatter(back_part, "dp", scatter_dimension=1, tiled=True),
    )


def per_device(
    enc_in,
    dec_in,
    segment,
    d_out,
    attn_gain,
    w_query,
    w_key,
    w_value,
    w_out,
    ffn_gain,
    w_in,
    w_back,
    self_gain,
    self_value,
    self_out,
    rel_table,
):
    section_index = lax.axis_index("section")
    gathered = (
        lax.all_gather(attn_gain, "dp", axis=1, tiled=True),
        lax.all_gather(w_query, "dp", axis=1, tiled=True),
        lax.all_gather(w_key, "dp", axis=1, tiled=True),
        lax.all_gather(w_value, "dp", axis=1, tiled=True),
        lax.all_gather(w_out, "dp", axis=1, tiled=True),
        lax.all_gather(ffn_gain, "dp", axis=1, tiled=True),
        lax.all_gather(w_in, "dp", axis=1, tiled=True),
        lax.all_gather(w_back, "dp", axis=1, tiled=True),
    )
    weights = tuple((part_full[0] for part_full in gathered))
    self_weights = (
        lax.all_gather(self_gain, ("section", "dp"), axis=0, tiled=True),
        lax.all_gather(self_value, ("section", "dp"), axis=0, tiled=True),
        lax.all_gather(self_out, ("section", "dp"), axis=0, tiled=True),
    )
    score_bias = bias_from_table(rel_table)
    groups = 1
    per_group = enc_in.shape[0] // groups
    half_width = enc_in.shape[2] // 2
    enc_kept = []
    dec_kept = []
    arrived = []
    dec_results = []
    for moment in range(groups + 1):

        def enc_side():
            if moment < groups:
                enc_pack = encode_forward(enc_in, segment, weights, score_bias)
            else:
                enc_pack = enc_blank(per_group)
            return (enc_pack, dec_blank(per_group))

        def dec_side():
            if moment >= 1:
                dec_pack = decode_forward(
                    arrived[moment - 1], segment, dec_in, weights, self_weights
                )
            else:
                dec_pack = dec_blank(per_group)
            return (enc_blank(per_group), dec_pack)

        enc_pack, dec_pack = lax.cond(section_index == 0, enc_side, dec_side)
        if moment < groups:
            enc_kept.append(enc_pack[1])
            arrived.append(passed_along(enc_pack[0], "section", 1))
        if moment >= 1:
            dec_results.append(dec_pack[0])
            dec_kept.append(dec_pack[1])
    shares = tuple(
        (
            jnp.zeros(part_arg.shape, jnp.float32)
            for part_arg in (attn_gain, w_query, w_key, w_value, w_out, ffn_gain, w_in, w_back)
        )
    )
    block_total = block_blank()
    self_total = self_blank()
    table_total = jnp.zeros(rel_table.shape, jnp.float32)
    returned = []
    out_left = []
    grad_left = []
    own_grads = []
    in_grads = []
    for moment in range(groups + 1):
        block_acc = block_total

        def dec_work():
            if moment < groups:
                grad_enc, grad_dec, blocks, self_next = decode_backward(
                    arrived[moment],
                    segment,
                    dec_in,
                    weights,
                    self_weights,
                    dec_kept[moment],
                    d_out,
                    block_acc,
                )
            else:
                grad_enc = jnp.zeros((per_group, ROW_LEN, D), jnp.bfloat16)
                grad_dec = jnp.zeros((per_group * SEGS, D), jnp.bfloat16)
                blocks = block_acc
                self_next = self_total
            return (
                grad_enc,
                grad_dec,
                jnp.zeros((per_group, ROW_LEN, D), jnp.bfloat16),
                blocks,
                self_next,
                table_total,
            )

        def enc_work():
            if moment >= 1:
                grad_in, blocks, table_next = encode_backward(
                    enc_in,
                    segment,
                    weights,
                    score_bias,
                    enc_kept[moment - 1],
                    returned[moment - 1],
                    block_acc,
                    table_total,
                )
            else:
                grad_in = jnp.zeros((per_group, ROW_LEN, D), jnp.bfloat16)
                blocks = block_acc
                table_next = table_total
            return (
                jnp.zeros((per_group, ROW_LEN, D), jnp.bfloat16),
                jnp.zeros((per_group * SEGS, D), jnp.bfloat16),
                grad_in,
                blocks,
                self_total,
                table_next,
            )

        grad_enc, grad_dec, grad_in, blocks, self_total, table_total = lax.cond(
            section_index == 0, enc_work, dec_work
        )
        if moment < groups:
            arrived_back = passed_along(
                (grad_enc, dec_results[moment][:, :half_width], grad_dec[:, :half_width]),
                "section",
                -1,
            )
            returned.append(arrived_back[0])
            out_left.append(arrived_back[1])
            grad_left.append(arrived_back[2])
            own_grads.append(grad_dec)
        if moment >= 1:
            in_grads.append(grad_in)
        block_total = blocks
    shares = spread_block(block_total)
    self_shares = (
        lax.psum_scatter(self_total[0], ("section", "dp"), scatter_dimension=0, tiled=True),
        lax.psum_scatter(self_total[1], ("section", "dp"), scatter_dimension=0, tiled=True),
        lax.psum_scatter(self_total[2], ("section", "dp"), scatter_dimension=0, tiled=True),
    )
    table_sum = lax.psum(table_total, ("section", "dp"))
    grad_in_all = in_grads[0]
    moved = passed_along(grad_in_all[:, :, half_width:], "section", 1)
    enc_in_grad = jnp.where(section_index == 0, grad_in_all[:, :, :half_width], moved)
    dec_out = jnp.where(section_index == 0, out_left[0], dec_results[0][:, half_width:])
    dec_in_grad = jnp.where(section_index == 0, grad_left[0], own_grads[0][:, half_width:])
    return (dec_out, enc_in_grad, dec_in_grad) + tuple(shares) + tuple(self_shares) + (table_sum,)


def solution(mesh):
    return jax.shard_map(
        per_device,
        mesh=mesh,
        in_specs=(
            P("dp", None, None),
            P("dp", None),
            P("dp", None),
            P("dp", None),
            P("section", "dp"),
            P("section", "dp", None),
            P("section", "dp", None),
            P("section", "dp", None),
            P("section", "dp", None),
            P("section", "dp"),
            P("section", "dp", None),
            P("section", "dp", None),
            P(("section", "dp")),
            P(("section", "dp"), None),
            P(("section", "dp"), None),
            P(),
        ),
        out_specs=(
            P("dp", "section"),
            P("dp", None, "section"),
            P("dp", "section"),
            P("section", "dp"),
            P("section", "dp", None),
            P("section", "dp", None),
            P("section", "dp", None),
            P("section", "dp", None),
            P("section", "dp"),
            P("section", "dp", None),
            P("section", "dp", None),
            P(("section", "dp")),
            P(("section", "dp"), None),
            P(("section", "dp"), None),
            P(),
        ),
        check_vma=False,
    )
```

profile of v0, /device:TPU:0, one launch (start us, length us, event | category | flops | bytes accessed | tf_op | source)
XLA Modules:
  0.0 2393.1 jit_solution(3958814886395219973)
XLA Ops:
  13.6 11.6 tile.4
  25.2 38.3 %tile.10 = f32[12,523776]{1,0:T(8,128)} reshape(f32[12,512,1023]{2,1,0:T(8,128)} %tile.4) | data formatting | bytes 50282496 | tf_op jit(solution)/shard_map/tile | solution.py:59
  63.5 25.6 %slice.32 = f32[12,523264]{1,0:T(8,128)} slice(f32[12,523776]{1,0:T(8,128)} %tile.10), slice={[0:12], [511:523775]} | slice | bytes 50233344 | tf_op jit(solution)/shard_map/slice | solution.py:60
  89.0 42.4 %reshape.410 = f32[12,512,1022]{2,1,0:T(8,128)} reshape(f32[12,523264]{1,0:T(8,128)} %slice.32) | data formatting | bytes 50233344 | tf_op jit(solution)/shard_map/reshape | solution.py:61
  131.4 10.9 slice.33
  144.0 43.6 %all-reduce.7 = (bf16[768]{0:T(1024)(128)(2,1)S(1)}, bf16[768]{0:T(1024)(128)(2,1)S(1)}) all-reduce(bf16[768]{0:T(1024)(128)(2,1)S(1)} %dynamic-update-slice.1, bf16[768]{0:T(1024)(128)(2,1)S(1)} %dynamic-update-slice.2), channel_id=1, replica_groups=mesh['section'=2,'dp'=16] {'dp'}, use_global_device_ids=true, to_apply=%add.3 | all-reduce | flops 1536 | bytes 6144 | tf_op jit(solution)/shard_map/squeeze | solution.py:527
  187.7 55.5 %all-gather.19.cloned.1.call-done = bf16[1,768,768]{2,1,0:T(8,128)(2,1)} async-done(((bf16[1,48,768]{2,1,0:T(8,128)(2,1)}), bf16[1,768,768]{2,1,0:T(8,128)(2,1)}) %all-gather.19.cloned.1.call-update) | async-done | bytes 1179664 | tf_op jit(solution)/shard_map/all_gather | solution.py:522
  243.2 82.0 %all-gather.21.cloned.1.call-done = bf16[1,768,3072]{2,1,0:T(8,128)(2,1)} async-done(((bf16[1,48,3072]{2,1,0:T(8,128)(2,1)}), bf16[1,768,3072]{2,1,0:T(8,128)(2,1)}) %all-gather.21.cloned.1.call-update) | async-done | bytes 4718608 | tf_op jit(solution)/shard_map/all_gather | solution.py:524
  325.2 81.8 %all-gather.23.cloned.1.call-done = bf16[1,3072,768]{2,1,0:T(8,128)(2,1)} async-done(((bf16[1,192,768]{2,1,0:T(8,128)(2,1)}), bf16[1,3072,768]{2,1,0:T(8,128)(2,1)}) %all-gather.23.cloned.1.call-update) | async-done | bytes 4718608 | tf_op jit(solution)/shard_map/all_gather | solution.py:525
  407.0 112.1 %conditional.4 = (bf16[2,512,768]{2,1,0:T(8,128)(2,1)}, bf16[1024,768]{1,0:T(8,128)(2,1)}, bf16[1024,768]{1,0:T(8,128)(2,1)}, bf16[1024,768]{1,0:T(8,128)(2,1)},...) conditional(s32[]{:T(128)} %convert_element_type.218, () %tuple.48, ...), branch_computations={%region_0.0_spmd, %region_1.8_spmd} | conditional | flops 15369893888 | bytes 244616832 | solution.py:559
  444.7 12.8 copy.149
  457.4 26.7 %while.27 = (s32[]{:T(128)}, bf16[2,512,12,64]{1,3,2,0:T(8,128)(2,1)}, f32[2,12,512]{2,1,0:T(8,128)}, bf16[2,512,12,64]{1,3,2,0:T(8,128)(2,1)}, s32[2,512]{1,0:T...) while((s32[]{:T(128)}, ...), condition=%wide.region_6.6_spmd, body=%wide.region_3.5_spmd.sunk | while | flops 831121408 | bytes 54214764 | solution.py:226
  497.2 12.2 fusion.20
  509.4 9.5 add_convert_fusion
  521.8 39.3 %all-reduce.2 = bf16[768]{0:T(1024)(128)(2,1)S(1)} all-reduce(bf16[768]{0:T(1024)(128)(2,1)S(1)} %dynamic-update-slice), channel_id=1, replica_groups=mesh['section'=2,'dp'=16] {'section','dp'}, use_global_device_ids=true, to_apply=%add.2 | all-reduce | flops 768 | bytes 3072
  564.3 16.8 conditional.6
  582.4 93.9 %collective-permute-done.2 = bf16[2,512,768]{2,1,0:T(8,128)(2,1)} collective-permute-done((bf16[2,512,768]{2,1,0:T(8,128)(2,1)S(1)}, bf16[2,512,768]{2,1,0:T(8,128)(2,1)}, u32[]{:S(2)}, u32[]{:S(2)}) %collective-permute-start.2) | collective-permute-done | bytes 1572896 | tf_op jit(solution)/shard_map/ppermute | solution.py:24
  676.4 369.3 %conditional.7 = (bf16[2,512,768]{2,1,0:T(8,128)(2,1)}, f32[1,768]{1,0:T(1,128)}, f32[1,768,768]{1,2,0:T(8,128)}, f32[1,768,768]{1,2,0:T(8,128)}, f32[1,768,768]...) conditional(s32[]{:T(128)} %convert_element_type.218, ...), branch_computations={%region_27.28_spmd, %region_28.39_spmd} | conditional | flops 31154388992 | bytes 812366464 | solution.py:634
  699.2 15.5 fusion.144
  714.7 10.7 bitcast_add_fusion.1
  725.4 7.9 multiply_reduce_fusion.11
  749.1 11.2 bitcast_add_fusion.2
  760.3 12.7 copy.155
  773.0 91.1 %while.28 = (s32[]{:T(128)}, f32[12,512,512]{1,2,0:T(8,128)}, bf16[2,512,12,64]{1,3,2,0:T(8,128)(2,1)}, bf16[2,512,12,64]{1,3,2,0:T(8,128)(2,1)}, bf16[2,512,12,...) while((s32[]{:T(128)}, f32[12,512,512]{1,2,0:T(8,128)}, ...), condition=%wide.region_33.33_spmd.clone, body=%wide.region_31.32_spmd.clone.sunk | while | flops 2052450304 | bytes 203558272 | solution.py:311
  777.4 10.3 multiply_reduce_fusion.15
  787.6 7.5 fusion.274
  795.1 13.9 select_add_fusion.2
  820.3 10.2 multiply_reduce_fusion.15
  830.6 7.5 fusion.274
  838.1 18.5 select_add_fusion.2
  895.3 12.6 copy.173
  907.9 14.4 pad.4.clone
  922.3 47.0 %reshape.407 = f32[12,523264]{1,0:T(8,128)} reshape(f32[12,512,1022]{2,1,0:T(8,128)} %pad.4.clone) | data formatting | bytes 50233344 | tf_op jit(solution)/shard_map/cond/branch_1_fun/transpose(jvp())/reshape | solution.py:61
  969.4 25.6 %pad.5 = f32[12,523776]{1,0:T(8,128)} pad(f32[12,523264]{1,0:T(8,128)} %reshape.407, f32[]{:T(128)} %constant.170.clone), padding=0_0x511_1 | pad | bytes 50257924 | tf_op jit(solution)/shard_map/cond/branch_1_fun/transpose(jvp())/pad | solution.py:60
  995.0 41.3 %reshape.408 = f32[12,512,1023]{2,1,0:T(8,128)} reshape(f32[12,523776]{1,0:T(8,128)} %pad.5) | data formatting | bytes 50282496 | tf_op jit(solution)/shard_map/cond/branch_1_fun/transpose(jvp())/reshape | solution.py:59
  1036.3 9.0 reduce_sum.241
  1069.6 9.7 copy.161
  1086.9 39.2 %all-reduce.6 = (f32[768]{0:T(1024)S(1)}, f32[32,12]{0,1:T(8,128)}) all-reduce(f32[768]{0:T(1024)S(1)} %copy-done.76, f32[32,12]{0,1:T(8,128)S(1)} %copy-done.68), channel_id=10, replica_groups=mesh['section'=2,'dp'=16] {'section','dp'}, use_global_device_ids=true, to_apply=%region_47.48.clone | all-reduce | flops 1152 | bytes 9216
  1126.7 41.8 %reduce-scatter.31.cloned.1.call-done = f32[48,1]{1,0:T(8,128)} async-done(((f32[768,1]{1,0:T(8,128)}), f32[48,1]{1,0:T(8,128)}) %reduce-scatter.31.cloned.1.call-update) | async-done | bytes 208
  1169.8 124.5 %reduce-scatter.33.cloned.1.call-done = f32[48,1]{1,0:T(8,128)} async-done(((f32[768,1]{1,0:T(8,128)}), f32[48,1]{1,0:T(8,128)}) %reduce-scatter.33.cloned.1.call-update) | async-done | bytes 208
  1297.9 100.6 %reduce-scatter.27.cloned.1.call-done = f32[24,768]{1,0:T(8,128)} async-done(((f32[768,768]{1,0:T(8,128)}), f32[24,768]{1,0:T(8,128)}) %reduce-scatter.27.cloned.1.call-update) | async-done | bytes 73744 | tf_op jit(solution)/shard_map/reduce_scatter | solution.py:653
  1398.5 104.7 %reduce-scatter.29.cloned.1.call-done = f32[24,768]{1,0:T(8,128)} async-done(((f32[768,768]{1,0:T(8,128)}), f32[24,768]{1,0:T(8,128)}) %reduce-scatter.29.cloned.1.call-update) | async-done | bytes 73744 | tf_op jit(solution)/shard_map/reduce_scatter | solution.py:654
  1503.1 132.0 %reduce-scatter.15.cloned.1.call-done = f32[1,48,768]{2,1,0:T(8,128)} async-done(((f32[1,768,768]{2,1,0:T(8,128)}), f32[1,48,768]{2,1,0:T(8,128)}) %reduce-scatter.15.cloned.1.call-update) | async-done | bytes 147472 | tf_op jit(solution)/shard_map/reduce_scatter | solution.py:488
  1635.1 132.9 %reduce-scatter.17.cloned.1.call-done = f32[1,48,768]{2,1,0:T(8,128)} async-done(((f32[1,768,768]{2,1,0:T(8,128)}), f32[1,48,768]{2,1,0:T(8,128)}) %reduce-scatter.17.cloned.1.call-update) | async-done | bytes 147472 | tf_op jit(solution)/shard_map/reduce_scatter | solution.py:489
  1768.1 132.0 %reduce-scatter.19.cloned.1.call-done = f32[1,48,768]{2,1,0:T(8,128)} async-done(((f32[1,768,768]{2,1,0:T(8,128)}), f32[1,48,768]{2,1,0:T(8,128)}) %reduce-scatter.19.cloned.1.call-update) | async-done | bytes 147472 | tf_op jit(solution)/shard_map/reduce_scatter | solution.py:490
  1900.1 132.9 %reduce-scatter.21.cloned.1.call-done = f32[1,48,768]{2,1,0:T(8,128)} async-done(((f32[1,768,768]{2,1,0:T(8,128)}), f32[1,48,768]{2,1,0:T(8,128)}) %reduce-scatter.21.cloned.1.call-update) | async-done | bytes 147472 | tf_op jit(solution)/shard_map/reduce_scatter | solution.py:491
  2032.9 176.3 %reduce-scatter.25.cloned.1.call-done = f32[1,192,768]{2,1,0:T(8,128)} async-done(((f32[1,3072,768]{2,1,0:T(8,128)}), f32[1,192,768]{2,1,0:T(8,128)}) %reduce-scatter.25.cloned.1.call-update) | async-done | bytes 589840 | tf_op jit(solution)/shard_map/reduce_scatter | solution.py:494
  2209.2 176.8 %reduce-scatter.23.cloned.1.call-done = f32[1,48,3072]{2,1,0:T(8,128)} async-done(((f32[1,768,3072]{2,1,0:T(8,128)}), f32[1,48,3072]{2,1,0:T(8,128)}) %reduce-scatter.23.cloned.1.call-update) | async-done | bytes 589840 | tf_op jit(solution)/shard_map/reduce_scatter | solution.py:493
  (351 shorter events, 236.7 us)
Async XLA Ops:
  7.2 180.4 %all-gather.13.cloned.1.call-start = ((), (), s32[]{:S(2)}) async-start(), calls=%async_computation.12 | async-start | bytes 1253376 | tf_op jit(solution)/shard_map/all_gather | solution.py:519
  7.9 179.7 %all-gather.15.cloned.1.call-start = ((), (), s32[]{:S(2)}) async-start(), calls=%async_computation.13 | async-start | bytes 1253376 | tf_op jit(solution)/shard_map/all_gather | solution.py:520
  8.7 179.0 %all-gather.17.cloned.1.call-start = ((), (), s32[]{:S(2)}) async-start(), calls=%async_computation.14 | async-start | bytes 1253376 | tf_op jit(solution)/shard_map/all_gather | solution.py:521
  9.4 233.7 %all-gather.19.cloned.1.call-start = ((), (), s32[]{:S(2)}) async-start(), calls=%async_computation.15 | async-start | bytes 1253376 | tf_op jit(solution)/shard_map/all_gather | solution.py:522
  10.0 315.2 %all-gather.21.cloned.1.call-start = ((), (), s32[]{:S(2)}) async-start(), calls=%async_computation.16 | async-start | bytes 5013504 | tf_op jit(solution)/shard_map/all_gather | solution.py:524
  10.6 396.4 %all-gather.23.cloned.1.call-start = ((), (), s32[]{:S(2)}) async-start(), calls=%async_computation.17 | async-start | bytes 5013504 | tf_op jit(solution)/shard_map/all_gather | solution.py:525
  11.2 549.9 %all-gather.9.cloned.1.call-start = ((), (), s32[]{:S(2)}) async-start(), calls=%async_computation.10 | async-start | bytes 1216512 | tf_op jit(solution)/shard_map/all_gather | solution.py:530
  11.9 549.1 %all-gather.11.cloned.1.call-start = ((), (), s32[]{:S(2)}) async-start(), calls=%async_computation.11 | async-start | bytes 1216512 | tf_op jit(solution)/shard_map/all_gather | solution.py:531
  12.7 1155.9 %reduce-scatter.31.cloned.1.call-start = ((), (), s32[]{:S(2)}) async-start(), calls=%async_computation.26 | async-start | bytes 417792
  131.4 275.5 %copy-start.5 = (bf16[2,512,768]{2,1,0:T(8,128)(2,1)S(1)}, bf16[2,512,768]{2,1,0:T(8,128)(2,1)}, u32[]{:S(2)}) copy-start(bf16[2,512,768]{2,1,0:T(8,128)(2,1)} %param.30) | copy-start | bytes 4718596
  187.6 219.4 %copy-start.65 = (bf16[768]{0:T(1024)(128)(2,1)}, bf16[768]{0:T(1024)(128)(2,1)S(1)}, u32[]{:S(2)}) copy-start(bf16[768]{0:T(1024)(128)(2,1)S(1)} %get-tuple-element.810) | copy-start | bytes 4612
  187.6 219.4 %copy-start.66 = (bf16[768]{0:T(1024)(128)(2,1)}, bf16[768]{0:T(1024)(128)(2,1)S(1)}, u32[]{:S(2)}) copy-start(bf16[768]{0:T(1024)(128)(2,1)S(1)} %get-tuple-element.811) | copy-start | bytes 4612
  407.0 114.6 %copy-start.90 = (bf16[24]{0:T(256)(128)(2,1)S(1)}, bf16[24]{0:T(256)(128)(2,1)}, u32[]{:S(2)}) copy-start(bf16[24]{0:T(256)(128)(2,1)} %param.42) | copy-start | bytes 148
  407.0 154.1 %copy-start.38 = (bf16[8,768]{1,0:T(8,128)(2,1)S(1)}, bf16[8,768]{1,0:T(8,128)(2,1)}, u32[]{:S(2)}) copy-start(bf16[8,768]{1,0:T(8,128)(2,1)} %param.31) | copy-start | bytes 36868
  444.7 12.8 copy-start.42
  484.1 13.1 slice-start
  488.9 20.5 slice-start.4
  519.1 41.9 %collective-permute-start = (bf16[2,512,768]{2,1,0:T(8,128)(2,1)}, bf16[2,512,768]{2,1,0:T(8,128)(2,1)}, u32[]{:S(2)}, u32[]{:S(2)}) collective-permute-start(bf16[2,512,768]{2,1,0:T(8,128)(2,1)} %get-tuple-element.447), channel_id=1, source_target_pairs={{0,16},{1,17},{2,18},{3,19},{4,20},{5,21},{6,22},{7,23},{8,24},{9,... | collective-permute-start | bytes 4718600 | tf_op jit(solution)/shard_map/ppermute | solution.py:24
  581.1 95.3 %copy-start.23 = (f32[1,768,768]{1,2,0:T(8,128)}, f32[1,768,768]{1,2,0:T(8,128)S(1)}, u32[]{:S(2)}) copy-start(f32[1,768,768]{1,2,0:T(8,128)S(1)} %get-tuple-element.464) | copy-start | bytes 7077892
  581.1 95.3 %copy-start.69 = (f32[1,768]{1,0:T(1,128)}, f32[1,768]{1,0:T(1,128)S(1)}, u32[]{:S(2)}) copy-start(f32[1,768]{1,0:T(1,128)S(1)} %get-tuple-element.467) | copy-start | bytes 9220
  581.1 95.3 %copy-start.72 = (f32[1,768]{1,0:T(1,128)}, f32[1,768]{1,0:T(1,128)S(1)}, u32[]{:S(2)}) copy-start(f32[1,768]{1,0:T(1,128)S(1)} %get-tuple-element.462) | copy-start | bytes 9220
  581.1 95.3 %copy-start.75 = (f32[768]{0:T(1024)}, f32[768]{0:T(1024)S(1)}, u32[]{:S(2)}) copy-start(f32[768]{0:T(1024)S(1)} %get-tuple-element.491) | copy-start | bytes 9220
  581.1 95.3 %copy-start.13 = (f32[768,768]{0,1:T(8,128)}, f32[768,768]{0,1:T(8,128)S(1)}, u32[]{:S(2)}) copy-start(f32[768,768]{0,1:T(8,128)S(1)} %get-tuple-element.493) | copy-start | bytes 7077892
  581.1 95.3 %copy-start.15 = (f32[768,768]{0,1:T(8,128)}, f32[768,768]{0,1:T(8,128)S(1)}, u32[]{:S(2)}) copy-start(f32[768,768]{0,1:T(8,128)S(1)} %get-tuple-element.492) | copy-start | bytes 7077892
  581.1 95.3 %copy-start.57 = (bf16[8,768]{1,0:T(8,128)(2,1)}, bf16[8,768]{1,0:T(8,128)(2,1)S(1)}, u32[]{:S(2)}) copy-start(bf16[8,768]{1,0:T(8,128)(2,1)S(1)} %get-tuple-element.482) | copy-start | bytes 36868
  581.1 95.2 %collective-permute-start.2 = (bf16[2,512,768]{2,1,0:T(8,128)(2,1)S(1)}, bf16[2,512,768]{2,1,0:T(8,128)(2,1)}, u32[]{:S(2)}, u32[]{:S(2)}) collective-permute-start(bf16[2,512,768]{2,1,0:T(8,128)(2,1)S(1)} %get-tuple-element.470), channel_id=1, source_target_pairs={{16,0},{17,1},{18,2},{19,3},{20,4},{21,5},{22,6},{23,7},{24,8},{25... | collective-permute-start | bytes 4718600 | tf_op jit(solution)/shard_map/ppermute | solution.py:24
  697.7 27.7 %slice-start.2 = ((s8[4718592]{0:T(1024)(128)(4,1)}), s8[524288]{0:T(1024)(128)(4,1)S(1)}, s32[]{:S(2)}) async-start(s8[4718592]{0:T(1024)(128)(4,1)} %bitcast.350), calls=%async_computation.30 | async-start | bytes 1048576 | tf_op jit(solution)/shard_map/cond
  699.2 26.2 %slice-start.3 = ((s8[4718592]{0:T(1024)(128)(4,1)}), s8[4194304]{0:T(1024)(128)(4,1)S(1)}, s32[]{:S(2)}) async-start(s8[4718592]{0:T(1024)(128)(4,1)} %bitcast.350), calls=%async_computation.31 | async-start | bytes 8388608 | tf_op jit(solution)/shard_map/cond
  760.3 12.7 copy-start.43
  795.1 13.9 copy-start.3
  795.1 13.9 copy-start.27
  795.1 18.9 copy-start.30
  838.1 18.5 copy-start.3
  838.1 18.5 copy-start.27
  838.1 23.5 copy-start.30
  1047.4 247.0 %reduce-scatter.33.cloned.1.call-start = ((), (), s32[]{:S(2)}) async-start(), calls=%async_computation.27 | async-start | bytes 417792
  1049.1 349.4 %reduce-scatter.27.cloned.1.call-start = ((), (), s32[]{:S(2)}) async-start(), calls=%async_computation.24 | async-start | bytes 2433024 | tf_op jit(solution)/shard_map/reduce_scatter | solution.py:653
  1052.3 450.9 %reduce-scatter.29.cloned.1.call-start = ((), (), s32[]{:S(2)}) async-start(), calls=%async_computation.25 | async-start | bytes 2433024 | tf_op jit(solution)/shard_map/reduce_scatter | solution.py:654
  1055.9 579.3 %reduce-scatter.15.cloned.1.call-start = ((), (), s32[]{:S(2)}) async-start(), calls=%async_computation.18 | async-start | bytes 2506752 | tf_op jit(solution)/shard_map/reduce_scatter | solution.py:488
  1059.0 709.1 %reduce-scatter.17.cloned.1.call-start = ((), (), s32[]{:S(2)}) async-start(), calls=%async_computation.19 | async-start | bytes 2506752 | tf_op jit(solution)/shard_map/reduce_scatter | solution.py:489
  1062.6 837.4 %reduce-scatter.19.cloned.1.call-start = ((), (), s32[]{:S(2)}) async-start(), calls=%async_computation.20 | async-start | bytes 2506752 | tf_op jit(solution)/shard_map/reduce_scatter | solution.py:490
  1065.8 967.2 %reduce-scatter.21.cloned.1.call-start = ((), (), s32[]{:S(2)}) async-start(), calls=%async_computation.21 | async-start | bytes 2506752 | tf_op jit(solution)/shard_map/reduce_scatter | solution.py:491
  1068.9 1140.3 %reduce-scatter.25.cloned.1.call-start = ((), (), s32[]{:S(2)}) async-start(), calls=%async_computation.23 | async-start | bytes 10027008 | tf_op jit(solution)/shard_map/reduce_scatter | solution.py:494
  1069.5 1316.5 %reduce-scatter.23.cloned.1.call-start = ((), (), s32[]{:S(2)}) async-start(), calls=%async_computation.22 | async-start | bytes 10027008 | tf_op jit(solution)/shard_map/reduce_scatter | solution.py:493
  1079.3 1306.7 %copy-start.1 = (f32[32,12]{0,1:T(8,128)S(1)}, f32[32,12]{0,1:T(8,128)}, u32[]{:S(2)}) copy-start(f32[32,12]{0,1:T(8,128)} %param.45) | copy-start | bytes 4612
  1080.5 215.2 %collective-permute-start.3 = (bf16[2,512,384]{2,1,0:T(8,128)(2,1)S(1)}, bf16[2,512,384]{2,1,0:T(8,128)(2,1)S(1)}, u32[]{:S(2)}, u32[]{:S(2)}) collective-permute-start(bf16[2,512,384]{2,1,0:T(8,128)(2,1)S(1)} %slice.29), channel_id=1, source_target_pairs={{0,16},{1,17},{2,18},{3,19},{4,20},{5,21},{6,22},{7,23},{8,24},{9,... | collective-permute-start | bytes 2359304 | tf_op jit(solution)/shard_map/ppermute | solution.py:24
  1081.9 3.1 collective-permute-start.1
  1083.2 3.1 collective-permute-start.4
  (51 other events, 223.5 us)
Sparse Core Ops, SparseCore 0:
  10.8 58.8 all-gather.12
  72.5 54.9 all-gather.14
  130.3 55.1 all-gather.16
  188.2 54.9 all-gather.18
  245.8 79.3 all-gather.20
  327.8 79.0 all-gather.22
  409.9 52.6 all-gather.8
  465.4 53.0 all-gather.10
  1047.5 120.9 reduce-scatter.30
  1173.7 120.6 reduce-scatter.32
  1300.2 98.1 reduce-scatter.26
  1405.0 98.0 reduce-scatter.28
  1508.6 126.4 reduce-scatter.14
  1641.2 126.7 reduce-scatter.16
  1773.4 126.6 reduce-scatter.18
  1906.2 126.7 reduce-scatter.20
  2039.0 170.1 reduce-scatter.24
  2216.3 169.6 reduce-scatter.22
where the time goes:
time: 2400 us; the launch traced here: 2390 us
  waiting for transfers between devices  1570 us (65%)
  local copies, waits for them, and re-layouts  416 us (17%)
  matrix products  185 us (8%)
  blocking collectives  122 us (5%)
  other arithmetic  66.2 us (3%)
    reduce_scatter x1, waiting for transfers between devices, spread_block(): lax.psum_scatter(in_part, 'dp', scatter_dimension=1, tiled=True)  177 us
    reduce_scatter x1, waiting for transfers between devices, spread_block(): lax.psum_scatter(back_part, 'dp', scatter_dimension=1, tiled=True)  176 us
    unnamed x20, waiting for transfers between devices  172 us
    reduce_scatter x1, waiting for transfers between devices, spread_block(): lax.psum_scatter(key_part, 'dp', scatter_dimension=1, tiled=True)  133 us
    reduce_scatter x1, waiting for transfers between devices, spread_block(): lax.psum_scatter(out_part, 'dp', scatter_dimension=1, tiled=True)  133 us
    reduce_scatter x1, waiting for transfers between devices, spread_block(): lax.psum_scatter(query_part, 'dp', scatter_dimension=1, tiled=True)  132 us
    reduce_scatter x1, waiting for transfers between devices, spread_block(): lax.psum_scatter(value_part, 'dp', scatter_dimension=1, tiled=True)  132 us
    reduce_scatter x1, waiting for transfers between devices, per_device(): lax.psum_scatter(self_total[2], ('section', 'dp'), scatter_dimension=0, t...  105 us
  transfers between devices with their start and end apart: 23, of which 16 were waited for; matrix products, arithmetic and copies ran while one was open for 12% of the time, Pallas kernels for 0%

commit v1 on v0

v1 whole, which is shorter than its diff:
```python
import functools

import jax
import jax.numpy as jnp
import numpy as np
from jax import lax
from jax.experimental import pallas as pl
from jax.experimental.pallas import tpu as pltpu
from jax.sharding import PartitionSpec as P

D = 768
HEADS = 12
HEAD_DIM = 64
FF = 3072
BUCKETS = 32
MAX_DIST = 128
ROW_LEN = 512
SEGS = 4
GROUP = 48
GROUPS = D // GROUP
TILE = 128
EPS = 1e-06
MASKED = -1000000000.0
BF = jnp.bfloat16
F32 = jnp.float32
VMEM_LIMIT = 58 * 1024 * 1024


def bucket_of(offset):
    half, exact = BUCKETS // 2, BUCKETS // 4
    exponent, growth = half - exact, MAX_DIST // exact
    distance = abs(offset)
    if distance < exact:
        level = distance
    else:
        k = 0
        while k < exponent and exact**exponent * growth ** (k + 1) <= distance**exponent:
            k += 1
        level = min(exact + k, half - 1)
    return (half if offset > 0 else 0) + level


def window_onehots():
    table = np.zeros((2, 3, 2 * TILE, BUCKETS), np.float32)
    for d in range(3):
        for t in range(2 * TILE):
            table[0, d, t, bucket_of(TILE * (d - 1) - TILE + t)] = 1.0
            table[1, d, t, bucket_of(TILE * (d - 1) + TILE - t)] = 1.0
    return table


def diagonal_onehots():
    table = np.zeros((5, 2 * TILE, BUCKETS), np.float32)
    table[1:4] = window_onehots()[1]
    table[0, :, bucket_of(-TILE - 1)] = 1.0
    table[4, :, bucket_of(TILE + 1)] = 1.0
    return table


def across(value):
    return lax.ppermute(value, "section", [(0, 1), (1, 0)])


def along(value, bit):
    count = lax.axis_size("dp")
    return lax.ppermute(value, "dp", [(i, i ^ (1 << bit)) for i in range(count)])


def bit_of(index, bit):
    return lax.rem(lax.div(index, 1 << bit), 2)


def low_bits(rows):
    count = 0
    while rows < GROUP:
        rows *= 2
        count += 1
    return count


def filled(piece, pre, chip, axis):
    for bit in range(pre):
        other = along(piece, bit)
        upper = bit_of(chip, bit) == 1
        first = jnp.where(upper, other, piece)
        second = jnp.where(upper, piece, other)
        piece = jnp.concatenate([first, second], axis=axis)
    return piece


def narrowed(total, pre, chip):
    for bit in reversed(range(pre)):
        length = total.shape[0] // 2
        upper = bit_of(chip, bit)
        kept = lax.dynamic_slice_in_dim(total, upper * length, length, 0)
        sent = lax.dynamic_slice_in_dim(total, (1 - upper) * length, length, 0)
        total = added(kept, along(sent.astype(BF), bit), F32)
    return total


def gather_groups(piece, order, pre):
    held = [(piece[None], [0])]
    for bit in order:
        held += [(along(part, bit + pre), [g ^ (1 << bit) for g in ids]) for part, ids in held]
        slots = sum(len(ids) for part, ids in held)
        if slots <= 4:
            merged = jnp.concatenate([part for part, ids in held], axis=0)
            held = [(merged, sum([ids for part, ids in held], []))]
    return held


def on_both(held):
    return [(part, ids, 0) for part, ids in held] + [(across(part), ids, 1) for part, ids in held]


def added(left, right, kind=BF):
    return (left.astype(F32) + right.astype(F32)).astype(kind)


def scatter_groups(mine, theirs, order, pre):
    got = across(theirs)
    half = GROUPS // 2
    keep, send = added(mine[:half], got[:half]), added(mine[half:], got[half:])
    for bit in order:
        got = along(send, bit + pre)
        half = keep.shape[0] // 2
        if half:
            keep, send = added(keep[:half], got[:half]), added(keep[half:], got[half:])
        else:
            total = added(keep[0], got[0], F32)
    return total


def nn(a, b):
    return lax.dot_general(a, b, (((1,), (0,)), ((), ())), preferred_element_type=F32)


def nt(a, b):
    return lax.dot_general(a, b, (((1,), (1,)), ((), ())), preferred_element_type=F32)


def tn(a, b):
    return lax.dot_general(a, b, (((0,), (0,)), ((), ())), preferred_element_type=F32)


def rms(v, gain):
    return v * lax.rsqrt(jnp.mean(v * v, axis=-1, keepdims=True) + EPS) * gain


def rms_back(v, gain, dy):
    r = lax.rsqrt(jnp.mean(v * v, axis=-1, keepdims=True) + EPS)
    dgain = jnp.sum(dy * v * r, axis=0, keepdims=True)
    dyg = dy * gain
    dv = r * dyg - v * (r * r * r) * jnp.mean(v * dyg, axis=-1, keepdims=True)
    return dv, dgain


def gelu_both(u):
    c = 0.7978845608028654
    t = jnp.tanh(c * (u + 0.044715 * u * u * u))
    value = 0.5 * u * (1.0 + t)
    slope = 0.5 * (1.0 + t) + (0.5 * c) * u * (1.0 - t * t) * (1.0 + 3 * 0.044715 * u * u)
    return value, slope


def square_row(core, b, g):
    return (core * 2 + b) * D + GROUP * g


def back_row(core, b, g):
    return 4 * GROUP * g + GROUP * (2 * core + b)


def self_row(core, b, g):
    return b * D + core * (D // 2) + GROUP * g


def start_fetch(meta, refs, plan, dst, row_of, sem, which=0):
    me, core = meta[which], meta[2]
    for ref, (ids, other) in zip(refs, plan):
        source = 1 - core if other else core
        for slot, rel in enumerate(ids):
            group = jnp.bitwise_xor(me, rel)
            for b in range(ref.shape[1]):
                off = pl.multiple_of(row_of(source, b, group), 16)
                pltpu.make_async_copy(ref.at[slot, b], dst.at[pl.ds(off, GROUP)], sem).start()


def drain(ref, sem):
    pltpu.make_async_copy(ref, ref, sem).wait()


def slot_of(meta, group, order):
    rel = jnp.bitwise_xor(meta[0], group)
    slot = 0
    for k, bit in enumerate(order):
        slot = slot + bit_of(rel, bit) * (1 << (len(order) - 1 - k))
    return slot


def start_store(meta, src, group, core, b, mine, theirs, order, sem):
    slot = slot_of(meta, group, order)

    @pl.when(meta[2] == core)
    def _():
        pltpu.make_async_copy(src, mine.at[slot, b], sem).start()

    @pl.when(meta[2] != core)
    def _():
        pltpu.make_async_copy(src, theirs.at[slot, b], sem).start()


def head_lanes(h):
    lane = lax.broadcasted_iota(jnp.int32, (1, D), 1)
    return (lane >= h * HEAD_DIM) & (lane < (h + 1) * HEAD_DIM)


def pair_lanes(hh):
    lane = lax.broadcasted_iota(jnp.int32, (1, TILE), 1)
    return (lane < HEAD_DIM) if hh == 0 else (lane >= HEAD_DIM)


def masked(value, lanes):
    return jnp.where(lanes, value, jnp.zeros_like(value))


def fill_bias(window_ref, tiles, transposed):
    part = 1 if transposed else 0

    def one(h, carry):
        for d in range(3):
            row = jnp.broadcast_to(window_ref[h, pl.ds(part * 3 + d, 1), :], (TILE, 2 * TILE))
            rolled = pltpu.roll(row, TILE, 1, stride=1, stride_axis=0)
            tiles[h, d + 1] = rolled[:, :TILE]
        low = window_ref[h, pl.ds(0, 1), pl.ds(0, 1)]
        high = window_ref[h, pl.ds(2, 1), pl.ds(2 * TILE - 1, 1)]
        tiles[h, 0] = jnp.broadcast_to(low, (TILE, TILE))
        tiles[h, 4] = jnp.broadcast_to(high, (TILE, TILE))
        return carry

    lax.fori_loop(0, HEADS, one, 0)


def whole(space=pltpu.VMEM):
    return pl.BlockSpec(memory_space=space)


def call(body, name, ins, spaces, outs, out_spaces, scratch, flops=0, bytes_=0):
    return pl.pallas_call(
        body,
        name=name,
        in_specs=[whole(s) for s in spaces],
        out_specs=[whole(s) for s in out_spaces],
        out_shape=[jax.ShapeDtypeStruct(s, k) for s, k in outs],
        scratch_shapes=scratch,
        compiler_params=pltpu.CompilerParams(vmem_limit_bytes=VMEM_LIMIT),
        cost_estimate=pl.CostEstimate(flops=int(flops), bytes_accessed=int(bytes_), transcendentals=0),
    )(*ins)


VM, SM, ANY = pltpu.VMEM, pltpu.SMEM, pl.ANY


def plan_of(sets):
    return [part for part, ids, other in sets], [(ids, other) for part, ids, other in sets]


def enc_attention(meta, x, gains, segr, segc, windows, sets):
    arrays, plan = plan_of(sets)
    n = len(arrays)

    def body(meta, x, gains, segr, segc, windows, *rest):
        parts, rest = rest[:n], rest[n:]
        n1, q, k, v, c, h1, n2, lse, w, tiles, lcol, sem = rest
        start_fetch(meta, parts, plan, w, square_row, sem)
        fill_bias(windows, tiles, False)
        xf = x[...].astype(F32)
        n1[...] = rms(xf, gains[0:1, :]).astype(BF)
        drain(w, sem)
        for ref, at in ((q, 0), (k, 2), (v, 3)):
            ref[...] = nn(n1[...], w[at * D : (at + 1) * D, :]).astype(BF)
        lane = lax.broadcasted_iota(jnp.int32, (1, TILE), 1)
        lcol[...] = jnp.zeros_like(lcol)

        def pair(pr, carry):
            cols = pl.ds(pl.multiple_of(pr * TILE, TILE), TILE)
            kp, vp = k[:, cols], v[:, cols]
            for ib in range(ROW_LEN // TILE):
                rows = slice(ib * TILE, (ib + 1) * TILE)
                same = segc[rows, :] == segr[...]
                qp = q[rows, cols]
                total = jnp.zeros((TILE, TILE), F32)
                for hh in range(2):
                    h = 2 * pr + hh
                    lanes = pair_lanes(hh)
                    bias = jnp.concatenate(
                        [tiles[h, min(max(jb - ib, -2), 2) + 2] for jb in range(ROW_LEN // TILE)], axis=1
                    )
                    s = jnp.where(same, nt(masked(qp, lanes), kp) + bias, MASKED)
                    top = jnp.max(s, axis=-1, keepdims=True)
                    ex = jnp.exp(s - top)
                    tot = jnp.sum(ex, axis=-1, keepdims=True)
                    p = (ex * (1.0 / tot)).astype(BF)
                    total = total + nn(p, masked(vp, lanes))
                    lcol[rows, :] = jnp.where(lane == h, top + jnp.log(tot), lcol[rows, :])
                c[rows, cols] = total.astype(BF)
            return carry

        lax.fori_loop(0, HEADS // 2, pair, 0)
        lse[...] = lcol[...].T
        res = x[...].astype(F32) + nn(c[...], w[D : 2 * D, :])
        h1[...] = res
        n2[...] = rms(res, gains[1:2, :]).astype(BF)

    rows = (ROW_LEN, D)
    return call(
        body, "enc_attention", [meta, x, gains, segr, segc, windows, *arrays],
        [SM, VM, VM, VM, VM, VM] + [ANY] * n,
        [(rows, BF)] * 5 + [(rows, F32), (rows, BF), ((TILE, ROW_LEN), F32)], [VM] * 8,
        [pltpu.VMEM((4 * D, D), BF), pltpu.VMEM((HEADS, 5, TILE, TILE), F32),
         pltpu.VMEM((ROW_LEN, TILE), F32), pltpu.SemaphoreType.DMA],
        flops=4e9, bytes_=12e6,
    )


def enc_ffn(meta, h1, n2, in_sets, back_sets):
    in_arrays, in_plan = plan_of(in_sets)
    back_arrays, back_plan = plan_of(back_sets)
    n = len(in_arrays)

    def body(meta, h1, n2, *rest):
        ins, backs, rest = rest[:n], rest[n : 2 * n], rest[2 * n :]
        f, slope, e, w_in, w_back, acc, sems = rest
        start_fetch(meta, ins, in_plan, w_in, square_row, sems.at[0])
        start_fetch(meta, backs, back_plan, w_back, back_row, sems.at[1])
        acc[...] = h1[...]
        drain(w_in, sems.at[0])
        drain(w_back, sems.at[1])

        def block(b, carry):
            rows = pl.ds(pl.multiple_of(b * D, D), D)
            value, grad = gelu_both(nn(n2[...], w_in[rows, :]))
            fb = value.astype(BF)
            f[:, rows] = fb
            slope[:, rows] = grad.astype(BF)
            acc[...] += nn(fb, w_back[rows, :])
            return carry

        lax.fori_loop(0, FF // D, block, 0)
        e[...] = acc[...].astype(BF)

    return call(
        body, "enc_ffn", [meta, h1, n2, *in_arrays, *back_arrays], [SM, VM, VM] + [ANY] * (2 * n),
        [((ROW_LEN, FF), BF), ((ROW_LEN, FF), BF), ((ROW_LEN, D), BF)], [VM] * 3,
        [pltpu.VMEM((FF, D), BF), pltpu.VMEM((FF, D), BF), pltpu.VMEM((ROW_LEN, D), F32),
         pltpu.SemaphoreType.DMA((2,))],
        flops=5e9, bytes_=18e6,
    )


def enc_ffn_back_out(meta, de, f, slope, back_sets, order):
    arrays, plan = plan_of(back_sets)
    n = len(arrays)

    def body(meta, de, f, slope, *rest):
        parts, rest = rest[:n], rest[n:]
        du, mine, theirs, w, buf, sems = rest
        start_fetch(meta, parts, plan, w, back_row, sems.at[0])
        drain(w, sems.at[0])
        for b in range(FF // D):
            cols = slice(b * D, (b + 1) * D)
            du[:, cols] = (slope[:, cols].astype(F32) * nt(de[...], w[cols, :])).astype(BF)
            at = b % 2
            if b >= 2:
                drain(buf.at[at], sems.at[1 + at])
            buf[at] = tn(f[:, cols], de[...]).astype(BF)
            for k in range(D // GROUP):
                group, piece = b * (D // GROUP // 4) + k // 4, k % 4
                start_store(meta, buf.at[at, pl.ds(k * GROUP, GROUP)], group, piece // 2, piece % 2,
                            mine, theirs, order, sems.at[1 + at])
        drain(buf.at[0], sems.at[1])
        drain(buf.at[1], sems.at[2])

    part = (GROUPS, 2, GROUP, D)
    return call(
        body, "enc_ffn_back_out", [meta, de, f, slope, *arrays], [SM, VM, VM, VM] + [ANY] * n,
        [((ROW_LEN, FF), BF), (part, BF), (part, BF)], [VM, ANY, ANY],
        [pltpu.VMEM((FF, D), BF), pltpu.VMEM((2, D, D), BF), pltpu.SemaphoreType.DMA((3,))],
        flops=5e9, bytes_=18e6,
    )


def enc_ffn_back_in(meta, du, n2, h1, de, gains, in_sets, order):
    arrays, plan = plan_of(in_sets)
    n = len(arrays)

    def body(meta, du, n2, h1, de, gains, *rest):
        parts, rest = rest[:n], rest[n:]
        dh1, da, dgain, mine, theirs, w, buf, acc, sems = rest
        start_fetch(meta, parts, plan, w, square_row, sems.at[0])
        drain(w, sems.at[0])
        for b in range(FF // D):
            cols = slice(b * D, (b + 1) * D)
            at = b % 2
            if b >= 2:
                drain(buf.at[at], sems.at[1 + at])
            buf[at] = tn(n2[...], du[:, cols]).astype(BF)
            for g in range(GROUPS):
                start_store(meta, buf.at[at, pl.ds(g * GROUP, GROUP)], g, b // 2, b % 2,
                            mine, theirs, order, sems.at[1 + at])
            part = nt(du[:, cols], w[cols, :])
            acc[...] = part if b == 0 else acc[...] + part
        dv, dg = rms_back(h1[...], gains[1:2, :], acc[...])
        total = de[...].astype(F32) + dv
        dh1[...] = total
        da[...] = total.astype(BF)
        dgain[...] = dg
        drain(buf.at[0], sems.at[1])
        drain(buf.at[1], sems.at[2])

    part, rows = (GROUPS, 2, GROUP, D), (ROW_LEN, D)
    return call(
        body, "enc_ffn_back_in", [meta, du, n2, h1, de, gains, *arrays], [SM, VM, VM, VM, VM, VM] + [ANY] * n,
        [(rows, F32), (rows, BF), ((1, D), F32), (part, BF), (part, BF)], [VM, VM, VM, ANY, ANY],
        [pltpu.VMEM((FF, D), BF), pltpu.VMEM((2, D, D), BF), pltpu.VMEM(rows, F32), pltpu.SemaphoreType.DMA((3,))],
        flops=5e9, bytes_=18e6,
    )


def enc_attention_back(meta, da, c, q, k, v, lse, segr, segc, windows, sets):
    arrays, plan = plan_of(sets)
    n = len(arrays)
    wide = 2 * TILE

    def body(meta, da, c, q, k, v, lse, segr, segc, windows, *rest):
        parts, rest = rest[:n], rest[n:]
        g_out, dq, dk, dv, diag, w, dc, tiles, sums, kacc, vacc, sem = rest
        start_fetch(meta, parts, plan, w, square_row, sem)
        fill_bias(windows, tiles, True)
        g_out[...] = tn(c[...], da[...]).astype(BF)
        drain(w, sem)
        dc[...] = nt(da[...], w[D : 2 * D, :]).astype(BF)
        row = lax.broadcasted_iota(jnp.int32, (TILE, TILE), 0)
        col = lax.broadcasted_iota(jnp.int32, (TILE, TILE), 1)
        flip = (row + col == TILE - 1).astype(F32)

        def pair(pr, carry):
            cols = pl.ds(pl.multiple_of(pr * TILE, TILE), TILE)
            for hh in range(2):
                h = 2 * pr + hh
                lanes = pair_lanes(hh)
                km, vm = masked(k[:, cols], lanes), masked(v[:, cols], lanes)
                sums[...] = jnp.zeros_like(sums)
                for ib in range(ROW_LEN // wide):
                    rows = slice(ib * wide, (ib + 1) * wide)
                    same = segc[...] == segr[:, rows]
                    qp, dcp = q[rows, cols], dc[rows, cols]
                    bias = jnp.concatenate([
                        jnp.concatenate([
                            tiles[h, min(max(jb - (2 * ib + i), -2), 2) + 2] for i in range(2)
                        ], axis=1) for jb in range(ROW_LEN // TILE)
                    ], axis=0)
                    s = jnp.where(same, nt(km, qp) + bias, MASKED)
                    prob = jnp.exp(s - lse[pl.ds(h, 1), rows])
                    dprob = nt(vm, dcp)
                    inner = jnp.sum(prob * dprob, axis=0, keepdims=True)
                    ds = (prob * (dprob - inner)).astype(BF)
                    dvp = nn(prob.astype(BF), masked(dcp, lanes))
                    dkp = nn(ds, masked(qp, lanes))
                    dqp = tn(ds, km)
                    if hh == 0 and ib == 0:
                        vacc[...], kacc[...] = dvp, dkp
                    else:
                        vacc[...] += dvp
                        kacc[...] += dkp
                    if hh == 0:
                        dq[rows, cols] = dqp.astype(BF)
                    else:
                        dq[rows, cols] = dq[rows, cols] + dqp.astype(BF)
                    for jb in range(ROW_LEN // TILE):
                        for i in range(2):
                            d = min(max(jb - (2 * ib + i), -2), 2) + 2
                            sums[d] += ds[jb * TILE : (jb + 1) * TILE, i * TILE : (i + 1) * TILE].astype(F32)
                for d in range(5):
                    if d in (0, 4):
                        line = jnp.sum(sums[d], axis=0, keepdims=True)
                        diag[h, d : d + 1, :] = jnp.concatenate([line, jnp.zeros_like(line)], axis=1)
                    else:
                        turned = lax.dot_general(
                            flip, sums[d], (((1,), (0,)), ((), ())),
                            precision=lax.Precision.HIGHEST, preferred_element_type=F32,
                        )
                        wider = jnp.concatenate([turned, jnp.zeros_like(turned)], axis=1)
                        rolled = pltpu.roll(wider, 1, 1, stride=1, stride_axis=0)
                        diag[h, d : d + 1, :] = jnp.sum(rolled, axis=0, keepdims=True)
            dk[:, cols] = kacc[...].astype(BF)
            dv[:, cols] = vacc[...].astype(BF)
            return carry

        lax.fori_loop(0, HEADS // 2, pair, 0)

    rows = (ROW_LEN, D)
    return call(
        body, "enc_attention_back", [meta, da, c, q, k, v, lse, segr, segc, windows, *arrays],
        [SM] + [VM] * 9 + [ANY] * n,
        [((D, D), BF), (rows, BF), (rows, BF), (rows, BF), ((HEADS, 5, 2 * TILE), F32)], [VM] * 5,
        [pltpu.VMEM((4 * D, D), BF), pltpu.VMEM(rows, BF), pltpu.VMEM((HEADS, 5, TILE, TILE), F32),
         pltpu.VMEM((5, TILE, TILE), F32), pltpu.VMEM((ROW_LEN, TILE), F32), pltpu.VMEM((ROW_LEN, TILE), F32),
         pltpu.SemaphoreType.DMA],
        flops=6e9, bytes_=12e6,
    )


def enc_square_grads(meta, n1, dq, dk, dv, g_out, order):
    def body(meta, n1, dq, dk, dv, g_out, mine, theirs, buf, sem):
        for at, (grad, core, b) in enumerate(((dq, 0, 0), (dk, 1, 0), (dv, 1, 1))):
            buf[at] = tn(n1[...], grad[...]).astype(BF)
            for g in range(GROUPS):
                start_store(meta, buf.at[at, pl.ds(g * GROUP, GROUP)], g, core, b, mine, theirs, order, sem)
        for g in range(GROUPS):
            start_store(meta, g_out.at[pl.ds(g * GROUP, GROUP)], g, 0, 1, mine, theirs, order, sem)
        drain(buf, sem)
        drain(g_out, sem)

    part = (GROUPS, 2, GROUP, D)
    return call(
        body, "enc_square_grads", [meta, n1, dq, dk, dv, g_out], [SM] + [VM] * 5,
        [(part, BF), (part, BF)], [ANY, ANY],
        [pltpu.VMEM((3, D, D), BF), pltpu.SemaphoreType.DMA],
        flops=2e9, bytes_=8e6,
    )


def enc_input_grad(meta, dq, dk, dv, x, dh1, gains, sets):
    arrays, plan = plan_of(sets)
    n = len(arrays)

    def body(meta, dq, dk, dv, x, dh1, gains, *rest):
        parts, rest = rest[:n], rest[n:]
        keep, send, dgain, w, sem = rest
        start_fetch(meta, parts, plan, w, square_row, sem)
        drain(w, sem)
        total = nt(dq[...], w[0:D, :]) + nt(dk[...], w[2 * D : 3 * D, :]) + nt(dv[...], w[3 * D :, :])
        dx, dg = rms_back(x[...].astype(F32), gains[0:1, :], total)
        out = (dh1[...] + dx).astype(BF)
        dgain[...] = dg
        half = D // 2

        @pl.when(meta[2] == 0)
        def _():
            keep[...] = out[:, :half]
            send[...] = out[:, half:]

        @pl.when(meta[2] != 0)
        def _():
            keep[...] = out[:, half:]
            send[...] = out[:, :half]

    return call(
        body, "enc_input_grad", [meta, dq, dk, dv, x, dh1, gains, *arrays], [SM] + [VM] * 6 + [ANY] * n,
        [((ROW_LEN, D // 2), BF), ((ROW_LEN, D // 2), BF), ((1, D), F32)], [VM] * 3,
        [pltpu.VMEM((4 * D, D), BF), pltpu.SemaphoreType.DMA],
        flops=2e9, bytes_=10e6,
    )


def spread_heads(value):
    return jnp.concatenate([masked(value, head_lanes(h)) for h in range(HEADS)], axis=0)


def join_heads(value):
    total = jnp.zeros((8, D), F32)
    for h in range(HEADS):
        total = total + masked(value[8 * h : 8 * h + 8, :], head_lanes(h))
    return total


def own_rows(meta):
    row = lax.broadcasted_iota(jnp.int32, (8, 1), 0)
    return (row >= 4 * meta[2]) & (row < 4 * meta[2] + 4)


def dec_before(meta, z, gains, self_sets, sets):
    self_arrays, self_plan = plan_of(self_sets)
    arrays, plan = plan_of(sets)
    n0, n = len(self_arrays), len(arrays)

    def body(meta, z, gains, *rest):
        selfs, parts, rest = rest[:n0], rest[n0 : n0 + n], rest[n0 + n :]
        m1, sv, z1, m2, qc, qk, w_self, w, sems = rest
        start_fetch(meta, selfs, self_plan, w_self, self_row, sems.at[0], 1)
        start_fetch(meta, parts, plan, w, square_row, sems.at[1])
        zf = z[...].astype(F32)
        m1v = rms(zf, gains[4:5, :]).astype(BF)
        drain(w_self, sems.at[0])
        drain(w, sems.at[1])
        svv = nn(m1v, w_self[0:D, :]).astype(BF)
        z1v = zf + nn(svv, w_self[D:, :])
        m2v = rms(z1v, gains[2:3, :]).astype(BF)
        qcv = nn(m2v, w[0:D, :]).astype(BF)
        qk[...] = nt(spread_heads(qcv), w[2 * D : 3 * D, :]).astype(BF)
        m1[...], sv[...], z1[...], m2[...], qc[...] = m1v, svv, z1v, m2v, qcv

    rows = (8, D)
    return call(
        body, "dec_before", [meta, z, gains, *self_arrays, *arrays], [SM, VM, VM] + [ANY] * (n0 + n),
        [(rows, BF), (rows, BF), (rows, F32), (rows, BF), (rows, BF), ((8 * HEADS, D), BF)], [VM] * 6,
        [pltpu.VMEM((2 * D, D), BF), pltpu.VMEM((4 * D, D), BF), pltpu.SemaphoreType.DMA((2,))],
        flops=1e9, bytes_=8e6,
    )


def dec_grad_hidden(meta, g, sets):
    arrays, plan = plan_of(sets)
    n = len(arrays)

    def body(meta, g, *rest):
        parts, rest = rest[:n], rest[n:]
        gm, gw, w, sem = rest
        start_fetch(meta, parts, plan, w, back_row, sem)
        own = jnp.where(own_rows(meta), g[...].astype(F32), 0.0).astype(BF)
        gm[...] = own
        drain(w, sem)
        for b in range(FF // D):
            gw[:, b * D : (b + 1) * D] = nt(own, w[b * D : (b + 1) * D, :])

    return call(
        body, "dec_grad_hidden", [meta, g, *arrays], [SM, VM] + [ANY] * n,
        [((8, D), BF), ((8, FF), F32)], [VM] * 2,
        [pltpu.VMEM((FF, D), BF), pltpu.SemaphoreType.DMA],
        flops=1e9, bytes_=5e6,
    )


def dec_core(meta, e, segr, qk, z1, g, gw, gains, sets, in_sets):
    arrays, plan = plan_of(sets)
    in_arrays, in_plan = plan_of(in_sets)
    n, n2 = len(arrays), len(in_arrays)

    def body(meta, e, segr, qk, z1, g, gw, gains, *rest):
        parts, ins, rest = rest[:n], rest[n : n + n2], rest[n + n2 :]
        de, cc, z2, m3, fc, duc, da2, dz2, dcc, edt, ebar, dgain, w, w_in, sems = rest
        start_fetch(meta, parts, plan, w, square_row, sems.at[0])
        start_fetch(meta, ins, in_plan, w_in, square_row, sems.at[1])
        pairs = lax.broadcasted_iota(jnp.int32, (8 * HEADS, 1), 0)
        owner = segr[...] == jnp.bitwise_and(pairs, 7) - 4 * meta[2]
        t = jnp.where(owner, nt(qk[...], e[...]), MASKED)
        ex = jnp.where(owner, jnp.exp(t - jnp.max(t, axis=-1, keepdims=True)), 0.0)
        tot = jnp.sum(ex, axis=-1, keepdims=True)
        prob = ex * (1.0 / jnp.where(tot > 0.0, tot, 1.0))
        pc = prob.astype(BF)
        ebv = nn(pc, e[...]).astype(BF)
        ebar[...] = ebv
        drain(w, sems.at[0])
        ccv = join_heads(nn(ebv, w[3 * D :, :])).astype(BF)
        z2v = z1[...] + nn(ccv, w[D : 2 * D, :])
        m3v = rms(z2v, gains[3:4, :]).astype(BF)
        drain(w_in, sems.at[1])
        dm3 = jnp.zeros((8, D), F32)
        for b in range(FF // D):
            cols = slice(b * D, (b + 1) * D)
            value, slope = gelu_both(nn(m3v, w_in[cols, :]))
            fc[:, cols] = value.astype(BF)
            ducv = (slope * gw[:, cols]).astype(BF)
            duc[:, cols] = ducv
            dm3 = dm3 + nt(ducv, w_in[cols, :])
        back, dg = rms_back(z2v, gains[3:4, :], dm3)
        dz2v = g[...].astype(F32) + back
        da2v = dz2v.astype(BF)
        dccv = nt(da2v, w[D : 2 * D, :]).astype(BF)
        dvw = nt(spread_heads(dccv), w[3 * D :, :]).astype(BF)
        dprob = nt(dvw, e[...])
        dt = (prob * (dprob - jnp.sum(prob * dprob, axis=-1, keepdims=True))).astype(BF)
        de[...] = tn(jnp.concatenate([pc, dt], axis=0), jnp.concatenate([dvw, qk[...]], axis=0)).astype(BF)
        edt[...] = nn(dt, e[...]).astype(BF)
        cc[...], z2[...], m3[...], da2[...], dz2[...], dcc[...], dgain[...] = ccv, z2v, m3v, da2v, dz2v, dccv, dg

    rows, spread = (8, D), (8 * HEADS, D)
    return call(
        body, "dec_core", [meta, e, segr, qk, z1, g, gw, gains, *arrays, *in_arrays],
        [SM] + [VM] * 7 + [ANY] * (n + n2),
        [((ROW_LEN, D), BF), (rows, BF), (rows, F32), (rows, BF), ((8, FF), BF), ((8, FF), BF), (rows, BF),
         (rows, F32), (rows, BF), (spread, BF), (spread, BF), ((1, D), F32)], [VM] * 12,
        [pltpu.VMEM((4 * D, D), BF), pltpu.VMEM((FF, D), BF), pltpu.SemaphoreType.DMA((2,))],
        flops=4e9, bytes_=12e6,
    )


def dec_after(meta, z, sv, z1, z2, dz2, qc, dcc, edt, ebar, fc, gains, self_sets, sets, back_sets, order):
    self_arrays, self_plan = plan_of(self_sets)
    arrays, plan = plan_of(sets)
    back_arrays, back_plan = plan_of(back_sets)
    n0, n, n2 = len(self_arrays), len(arrays), len(back_arrays)

    def body(meta, z, sv, z1, z2, dz2, qc, dcc, edt, ebar, fc, gains, *rest):
        selfs, parts, backs = rest[:n0], rest[n0 : n0 + n], rest[n0 + n : n0 + n + n2]
        dqc, ds1, dsv, dec_grad, dec_out, dg_attn, dg_self, mine, theirs, w_self, w, w_back, buf, sems = rest[n0 + n + n2 :]
        start_fetch(meta, parts, plan, w, square_row, sems.at[1])
        start_fetch(meta, selfs, self_plan, w_self, self_row, sems.at[0], 1)
        start_fetch(meta, backs, back_plan, w_back, back_row, sems.at[2])
        buf[0] = tn(edt[...], spread_heads(qc[...])).astype(BF)
        buf[1] = tn(ebar[...], spread_heads(dcc[...])).astype(BF)
        for at in range(2):
            for grp in range(GROUPS):
                start_store(meta, buf.at[at, pl.ds(grp * GROUP, GROUP)], grp, at, 0, mine, theirs, order, sems.at[3])
        drain(w, sems.at[1])
        dqv = join_heads(nn(edt[...], w[2 * D : 3 * D, :])).astype(BF)
        back, dg = rms_back(z1[...], gains[2:3, :], nt(dqv, w[0:D, :]))
        dz1 = dz2[...] + back
        ds1v = dz1.astype(BF)
        drain(w_self, sems.at[0])
        dsvv = nt(ds1v, w_self[D:, :]).astype(BF)
        back0, dg0 = rms_back(z[...].astype(F32), gains[4:5, :], nt(dsvv, w_self[0:D, :]))
        own = own_rows(meta)
        dec_grad[...] = jnp.where(own, dz1 + back0, 0.0).astype(BF)
        drain(w_back, sems.at[2])
        y = z2[...]
        for b in range(FF // D):
            cols = slice(b * D, (b + 1) * D)
            y = y + nn(fc[:, cols], w_back[cols, :])
        dec_out[...] = jnp.where(own, y, 0.0).astype(BF)
        dqc[...], ds1[...], dsv[...], dg_attn[...], dg_self[...] = dqv, ds1v, dsvv, dg, dg0
        drain(buf, sems.at[3])

    rows, part = (8, D), (GROUPS, 1, GROUP, D)
    return call(
        body, "dec_after",
        [meta, z, sv, z1, z2, dz2, qc, dcc, edt, ebar, fc, gains, *self_arrays, *arrays, *back_arrays],
        [SM] + [VM] * 11 + [ANY] * (n0 + n + n2),
        [(rows, BF)] * 5 + [((1, D), F32)] * 2 + [(part, BF)] * 2, [VM] * 7 + [ANY] * 2,
        [pltpu.VMEM((2 * D, D), BF), pltpu.VMEM((4 * D, D), BF), pltpu.VMEM((FF, D), BF), pltpu.VMEM((2, D, D), BF),
         pltpu.SemaphoreType.DMA((4,))],
        flops=2e9, bytes_=14e6,
    )


def halves(w_query, w_key, w_value, w_out, w_in, w_back):
    ins = [w_in[:, b * D : (b + 1) * D] for b in range(4)]
    backs = [w_back[b * GROUP : (b + 1) * GROUP] for b in range(4)]
    first = [w_query, w_out, ins[0], ins[1], backs[0], backs[1]]
    second = [w_key, w_value, ins[2], ins[3], backs[2], backs[3]]
    return jnp.stack(first), jnp.stack(second)


def per_device(
    enc_in, dec_in, segment, d_out, attn_gain, w_query, w_key, w_value, w_out, ffn_gain, w_in, w_back,
    self_gain, self_value, self_out, rel_table,
):
    core, chip = lax.axis_index("section"), lax.axis_index("dp")
    chips = lax.axis_size("dp")
    rows = w_query.shape[1]
    first = core == 0
    meta = jnp.stack([chip >> low_bits(rows), chip >> low_bits(self_value.shape[0]), core]).astype(jnp.int32)

    small = jnp.stack([
        jnp.pad(v.astype(BF), (0, TILE - v.shape[0])) for v in (attn_gain[0], ffn_gain[0], self_gain)
    ])
    gathered = small[None]
    bits = chips.bit_length() - 1
    for bit in range(bits):
        gathered = jnp.concatenate([gathered, along(gathered, bit)], axis=0)
    places = jnp.bitwise_xor(jnp.arange(chips), chip)
    gathered = jnp.take(gathered, places, axis=0)
    both = jnp.stack([gathered, across(gathered)])
    both = jnp.where(first, both, both[::-1])
    attn_all, ffn_all = both[:, :, 0, :rows].reshape(2, D), both[:, :, 1, :rows].reshape(2, D)
    self_all = both[:, :, 2, : self_gain.shape[0]].reshape(1, D)
    gains = jnp.concatenate(
        [attn_all[0:1], ffn_all[0:1], attn_all[1:2], ffn_all[1:2], self_all, jnp.zeros((3, D), BF)]
    ).astype(F32)

    pre = low_bits(rows)
    own_first, own_second = halves(
        *[filled(w[0], pre, chip, 0) for w in (w_query, w_key, w_value, w_out, w_in, w_back)]
    )
    swapped = across(jnp.where(first, own_second, own_first))
    enc_blocks = jnp.where(first, own_first, swapped)
    dec_blocks = jnp.where(first, swapped, own_second)
    zzxy, zzyx = (2, 3, 0, 1), (2, 3, 1, 0)

    def gather(blocks, order, pre=pre):
        return on_both(gather_groups(blocks, order, pre))

    enc_square = gather(enc_blocks[0:2], zzxy)
    enc_w_in = gather(enc_blocks[2:4], zzyx)
    enc_w_back = gather(enc_blocks[4:6], zzxy)
    self_pre = low_bits(self_value.shape[0])
    self_own = filled(jnp.stack([self_value, self_out]), self_pre, chip, 1)
    self_sets = gather(self_own, (1, 2, 0), self_pre)
    dec_square = gather(dec_blocks[0:2], zzyx)
    dec_w_in = gather(dec_blocks[2:4], zzxy)
    dec_w_back = gather(dec_blocks[4:6], zzyx)

    windows = jnp.einsum(
        "adtb,bh->hadt", window_onehots(), rel_table, precision=lax.Precision.HIGHEST
    ).reshape(HEADS, 6, 2 * TILE)

    x = lax.dynamic_index_in_dim(enc_in, core, 0, False)
    seg = lax.dynamic_index_in_dim(segment, core, 0, False)
    segr, segc = seg[None, :], seg[:, None]

    n1, q, k, v, c, h1, n2, lse = enc_attention(meta, x, gains, segr, segc, windows, enc_square)
    f, slope, e = enc_ffn(meta, h1, n2, enc_w_in, enc_w_back)

    m1, sv, z1, m2, qc, qk = dec_before(meta, dec_in, gains, self_sets, dec_square)
    gm, gw = dec_grad_hidden(meta, d_out, dec_w_back)
    de, cc, z2, m3, fc, duc, da2, dz2, dcc, edt, ebar, dg_ffn1 = dec_core(
        meta, e, segr, qk, z1, gm, gw, gains, dec_square, dec_w_in
    )

    du, back_mine, back_theirs = enc_ffn_back_out(meta, de, f, slope, enc_w_back, zzxy[::-1])
    dh1, da, dg_ffn0, in_mine, in_theirs = enc_ffn_back_in(meta, du, n2, h1, de, gains, enc_w_in, zzyx[::-1])
    dqc, ds1, dsv, dec_grad, dec_out, dg_attn1, dg_self, kv_mine, kv_theirs = dec_after(
        meta, dec_in, sv, z1, z2, dz2, qc, dcc, edt, ebar, fc, gains, self_sets, dec_square, dec_w_back, zzxy[::-1]
    )
    g_out, dq, dk, dv, diag = enc_attention_back(meta, da, c, q, k, v, lse, segr, segc, windows, enc_square)
    sq_mine, sq_theirs = enc_square_grads(meta, n1, dq, dk, dv, g_out, zzyx[::-1])
    keep, send, dg_attn0 = enc_input_grad(meta, dq, dk, dv, x, dh1, gains, enc_square)

    back_sum = scatter_groups(back_mine, back_theirs, zzxy[::-1], pre)
    in_sum = scatter_groups(in_mine, in_theirs, zzyx[::-1], pre)
    kv_sum = scatter_groups(kv_mine, kv_theirs, zzxy[::-1], pre)
    sq_sum = scatter_groups(sq_mine, sq_theirs, zzyx[::-1], pre)

    own = (jnp.arange(8)[:, None] // 4) == core
    acts = jnp.concatenate([m1, sv, m2, cc, m3, dsv, ds1, dqc, da2, fc, gm, duc], axis=1)
    acts = jnp.where(own, acts, jnp.zeros_like(acts))
    acts = acts + across(acts)
    width = acts.shape[1] // 2
    part = lax.dynamic_slice_in_dim(acts, core * width, width, 1)
    for bit in range(bits):
        part = jnp.concatenate([part, along(part, bit)], axis=0)
    other = across(part)
    acts = jnp.concatenate([jnp.where(first, part, other), jnp.where(first, other, part)], axis=1)
    a_m1, a_sv, a_m2, a_cc, a_m3, a_dsv, a_ds1, a_dqc, a_da2 = [acts[:, i * D : (i + 1) * D] for i in range(9)]
    a_fc, a_g, a_duc = acts[:, 9 * D : 13 * D], acts[:, 13 * D : 14 * D], acts[:, 14 * D :]

    def grad_rows(left, right, at, count):
        return tn(lax.dynamic_slice_in_dim(left, at, count, 1), right)

    mine = chip * rows
    dec_q = grad_rows(a_m2, a_dqc, mine, rows)
    dec_o = grad_rows(a_cc, a_da2, mine, rows)
    dec_i = grad_rows(a_m3, a_duc, mine, rows)
    dec_b = grad_rows(a_fc, a_g, 4 * mine, 4 * rows)
    own_self = self_value.shape[0]
    at_self = (core * chips + chip) * own_self
    g_self_value = grad_rows(a_m1, a_dsv, at_self, own_self)
    g_self_out = grad_rows(a_sv, a_ds1, at_self, own_self)

    table = jnp.einsum("hdt,dtb->bh", diag, diagonal_onehots(), precision=lax.Precision.HIGHEST)
    little = jnp.concatenate([
        dg_attn0, dg_ffn0, dg_attn1, dg_ffn1, dg_self,
        jnp.pad(table.reshape(1, -1), ((0, 0), (0, D - BUCKETS * HEADS))), jnp.zeros((2, D), F32),
    ])
    little = little + across(little)
    for bit in range(bits):
        little = little + along(little, bit)
    g_rel_table = little[5, : BUCKETS * HEADS].reshape(BUCKETS, HEADS)

    def cut(index, at, count):
        return lax.dynamic_slice_in_dim(little[index], at, count, 0)

    g_attn_gain = cut(jnp.where(first, 0, 2), mine, rows)[None]
    g_ffn_gain = cut(jnp.where(first, 1, 3), mine, rows)[None]
    g_self_gain = cut(4, at_self, own_self)

    enc_share = jnp.concatenate([sq_sum, in_sum, back_sum]).astype(BF)
    got = across(enc_share)
    got_kv = across(kv_sum)

    def placed(enc_value, dec_value):
        return jnp.where(first, narrowed(enc_value, pre, chip), dec_value)[None]

    g_w_query = placed(sq_sum[0], dec_q)
    g_w_out = placed(sq_sum[1], dec_o)
    g_w_key = narrowed(jnp.where(first, got[0].astype(F32), got_kv[0]), pre, chip)[None]
    g_w_value = narrowed(jnp.where(first, got[1].astype(F32), kv_sum[0]), pre, chip)[None]
    wide = jnp.concatenate([in_sum[0], in_sum[1], got[2].astype(F32), got[3].astype(F32)], axis=1)
    g_w_in = placed(wide, dec_i)
    tall = jnp.concatenate([back_sum[0], back_sum[1], got[4].astype(F32), got[5].astype(F32)], axis=0)
    g_w_back = placed(tall, dec_b)

    other_half = across(send)
    enc_in_grad = jnp.where(first, jnp.stack([keep, other_half]), jnp.stack([other_half, keep]))
    dec_out = dec_out + across(dec_out)
    dec_grad = dec_grad + across(dec_grad)
    half = D // 2
    dec_out = jnp.where(first, dec_out[:, :half], dec_out[:, half:])
    dec_in_grad = jnp.where(first, dec_grad[:, :half], dec_grad[:, half:])
    return (
        dec_out, enc_in_grad, dec_in_grad, g_attn_gain, g_w_query, g_w_key, g_w_value, g_w_out, g_ffn_gain,
        g_w_in, g_w_back, g_self_gain, g_self_value, g_self_out, g_rel_table,
    )


def solution(mesh):
    return jax.shard_map(
        per_device,
        mesh=mesh,
        in_specs=(
            P("dp", None, None),
            P("dp", None),
            P("dp", None),
            P("dp", None),
            P("section", "dp"),
            P("section", "dp", None),
            P("section", "dp", None),
            P("section", "dp", None),
            P("section", "dp", None),
            P("section", "dp"),
            P("section", "dp", None),
            P("section", "dp", None),
            P(("section", "dp")),
            P(("section", "dp"), None),
            P(("section", "dp"), None),
            P(),
        ),
        out_specs=(
            P("dp", "section"),
            P("dp", None, "section"),
            P("dp", "section"),
            P("section", "dp"),
            P("section", "dp", None),
            P("section", "dp", None),
            P("section", "dp", None),
            P("section", "dp", None),
            P("section", "dp"),
            P("section", "dp", None),
            P("section", "dp", None),
            P(("section", "dp")),
            P(("section", "dp"), None),
            P(("section", "dp"), None),
            P(),
        ),
        check_vma=False,
    )
```

time: 2400 us -> 611 us (0.25)
  waiting for transfers between devices: 1570 us -> 332 us
  local copies, waits for them, and re-layouts: 416 us -> 26.1 us
  matrix products: 185 us -> 8.34 us
  Pallas kernels: 0 us -> 133 us
  blocking collectives: 122 us -> 0 us
  starting transfers between devices: 8.42 us -> 77.2 us
  other arithmetic: 66.2 us -> 24.9 us
    reduce_scatter x8 -> x0, waiting for transfers between devices: 1090 us -> none  [the longest x1 177 us: spread_block(): lax.psum_scatter(in_part, 'dp', scatter_dimension=1, tiled=True)]
    ppermute x5 -> x102, waiting for transfers between devices: 95.1 us -> 332 us  [the longest x62 330 us: along(): return lax.ppermute(value, 'dp', [(i, i ^ 1 << bit) for i in range(count)])]
    all_gather x8 -> x0, waiting for transfers between devices: 219 us -> none  [the longest x1 82 us: per_device(): lax.all_gather(w_in, 'dp', axis=1, tiled=True)]
    dot_general x34 -> x8, matrix products: 185 us -> 8.34 us  [the longest x6 6.04 us: tn(): lax.dot_general(a, b, (((0,), (0,)), ((), ())), preferred_element_type=F32)]
    unnamed x20 -> x0, waiting for transfers between devices: 172 us -> none
    reshape x10 -> x2, local copies, waits for them, and re-layouts: 150 us -> 0.8 us  [the longest x1 0.69 us: per_device(): windows = jnp.einsum('adtb,bh->hadt', window_onehots(), rel_table, precis...]
    pallas_call x0 -> x11, Pallas kernels: none -> 133 us  [call(): pl.pallas_call(body, name=name, in_specs=[whole(s) for s in spaces], out_...]
    another operation x31 -> x5, local copies, waits for them, and re-layouts: 89.2 us -> 1.82 us  [the longest x1 0.93 us: halves(): return (jnp.stack(first), jnp.stack(second))]
  transfers between devices with their start and end apart: 23 -> 102, of which waited for: 16 -> 52; matrix products, arithmetic and copies ran while one was open for 12% -> 7% of each run, Pallas kernels for 0% -> 9%
where the time goes in v1:
time: 611 us; the launch traced here: 603 us
  waiting for transfers between devices  332 us (54%)
  Pallas kernels  133 us (22%)
  starting transfers between devices  77.2 us (13%)
  local copies, waits for them, and re-layouts  26.1 us (4%)
  other arithmetic  24.9 us (4%)
  matrix products  8.34 us (1%)
    ppermute x62, waiting for transfers between devices, along(): return lax.ppermute(value, 'dp', [(i, i ^ 1 << bit) for i in range(count)])  330 us
    pallas_call x11, Pallas kernels, call(): pl.pallas_call(body, name=name, in_specs=[whole(s) for s in spaces], out_...  133 us
    ppermute x62, starting transfers between devices, along(): return lax.ppermute(value, 'dp', [(i, i ^ 1 << bit) for i in range(count)])  69 us
    unnamed x146, local copies, waits for them, and re-layouts  16.2 us
    convert_element_type x16, other arithmetic, added(): return (left.astype(F32) + right.astype(F32)).astype(kind)  12.5 us
  transfers between devices with their start and end apart: 102, of which 52 were waited for; matrix products, arithmetic and copies ran while one was open for 7% of the time, Pallas kernels for 9%

profile of v1, /device:TPU:0, one launch (start us, length us, event | category | flops | bytes accessed | tf_op | source)
XLA Modules:
  0.0 603.4 jit_solution(15056602853986930959)
XLA Ops:
  19.4 3.1 collective-permute-start.3
  27.8 3.1 collective-permute-done.6
  31.0 4.5 collective-permute-start.7
  40.1 3.9 collective-permute-done.7
  51.7 5.1 collective-permute-done.39
  68.9 24.7 %collective-permute-done.49 = bf16[2,2,48,768]{3,2,1,0:T(8,128)(2,1)S(1)} collective-permute-done((bf16[2,2,48,768]{3,2,1,0:T(8,128)(2,1)S(1)}, bf16[2,2,48,768]{3,2,1,0:T(8,128)(2,1)S(1)}, u32[]{:S(2)}, u32[]{:S(2)}) %collective-permute-start.49) | collective-permute-done | bytes 294944 | tf_op jit(solution)/shard_map/ppermute | solution.py:66
  93.5 9.5 %collective-permute-done.58 = bf16[2,2,48,768]{3,2,1,0:T(8,128)(2,1)S(1)} collective-permute-done((bf16[2,2,48,768]{3,2,1,0:T(8,128)(2,1)S(1)}, bf16[2,2,48,768]{3,2,1,0:T(8,128)(2,1)S(1)}, u32[]{:S(2)}, u32[]{:S(2)}) %collective-permute-start.58) | collective-permute-done | bytes 294944 | tf_op jit(solution)/shard_map/ppermute | solution.py:66
  103.1 9.4 %collective-permute-done.40 = bf16[2,2,48,768]{3,2,1,0:T(8,128)(2,1)S(1)} collective-permute-done((bf16[2,2,48,768]{3,2,1,0:T(8,128)(2,1)S(1)}, bf16[2,2,48,768]{3,2,1,0:T(8,128)(2,1)S(1)}, u32[]{:S(2)}, u32[]{:S(2)}) %collective-permute-start.40) | collective-permute-done | bytes 294944 | tf_op jit(solution)/shard_map/ppermute | solution.py:66
  112.5 6.3 %collective-permute-done.31 = bf16[2,2,48,768]{3,2,1,0:T(8,128)(2,1)S(1)} collective-permute-done((bf16[2,2,48,768]{3,2,1,0:T(8,128)(2,1)S(1)}, bf16[2,2,48,768]{3,2,1,0:T(8,128)(2,1)S(1)}, u32[]{:S(2)}, u32[]{:S(2)}) %collective-permute-start.31) | collective-permute-done | bytes 294944 | tf_op jit(solution)/shard_map/ppermute | solution.py:66
  120.4 3.1 collective-permute-done.22
  130.7 6.2 %collective-permute-done.51.rest_2_.rest_14_ = bf16[4,2,48,768]{3,2,1,0:T(8,128)(2,1)} collective-permute-done((bf16[4,2,48,768]{3,2,1,0:T(8,128)(2,1)S(1)}, bf16[4,2,48,768]{3,2,1,0:T(8,128)(2,1)}, u32[]{:S(2)}, u32[]{:S(2)}) %collective-permute-start.51) | collective-permute-done | bytes 589856 | tf_op jit(solution)/shard_map/ppermute | solution.py:66
  138.6 11.0 %collective-permute-done.59.rest_9_ = bf16[4,2,48,768]{3,2,1,0:T(8,128)(2,1)} collective-permute-done((bf16[4,2,48,768]{3,2,1,0:T(8,128)(2,1)S(1)}, bf16[4,2,48,768]{3,2,1,0:T(8,128)(2,1)}, u32[]{:S(2)}, u32[]{:S(2)}) %collective-permute-start.59) | collective-permute-done | bytes 589856 | tf_op jit(solution)/shard_map/ppermute | solution.py:66
  151.2 11.0 %collective-permute-done.41.rest_9_.rest_1_ = bf16[4,2,48,768]{3,2,1,0:T(8,128)(2,1)} collective-permute-done((bf16[4,2,48,768]{3,2,1,0:T(8,128)(2,1)S(1)}, bf16[4,2,48,768]{3,2,1,0:T(8,128)(2,1)}, u32[]{:S(2)}, u32[]{:S(2)}) %collective-permute-start.41) | collective-permute-done | bytes 589856 | tf_op jit(solution)/shard_map/ppermute | solution.py:66
  165.4 9.3 %collective-permute-done.33.rest_2_ = bf16[4,2,48,768]{3,2,1,0:T(8,128)(2,1)S(1)} collective-permute-done((bf16[4,2,48,768]{3,2,1,0:T(8,128)(2,1)S(1)}, bf16[4,2,48,768]{3,2,1,0:T(8,128)(2,1)S(1)}, u32[]{:S(2)}, u32[]{:S(2)}) %collective-permute-start.33) | collective-permute-done | bytes 589856 | tf_op jit(solution)/shard_map/ppermute | solution.py:66
  177.2 7.4 %collective-permute-done.23.rest_1_ = bf16[4,2,48,768]{3,2,1,0:T(8,128)(2,1)} collective-permute-done((bf16[4,2,48,768]{3,2,1,0:T(8,128)(2,1)S(1)}, bf16[4,2,48,768]{3,2,1,0:T(8,128)(2,1)}, u32[]{:S(2)}, u32[]{:S(2)}) %collective-permute-start.23) | collective-permute-done | bytes 589856 | tf_op jit(solution)/shard_map/ppermute | solution.py:66
  186.8 5.9 collective-permute-done.60.rest_10_
  193.1 11.4 %collective-permute-done.14.rest_5_.rest_1_ = bf16[4,2,48,768]{3,2,1,0:T(8,128)(2,1)S(1)} collective-permute-done((bf16[4,2,48,768]{3,2,1,0:T(8,128)(2,1)S(1)}, bf16[4,2,48,768]{3,2,1,0:T(8,128)(2,1)S(1)}, u32[]{:S(2)}, u32[]{:S(2)}) %collective-permute-start.14) | collective-permute-done | bytes 589856 | tf_op jit(solution)/shard_map/ppermute | solution.py:66
  213.5 8.0 %collective-permute-done.61.rest_11_ = bf16[4,2,48,768]{3,2,1,0:T(8,128)(2,1)} collective-permute-done((bf16[4,2,48,768]{3,2,1,0:T(8,128)(2,1)}, bf16[4,2,48,768]{3,2,1,0:T(8,128)(2,1)}, u32[]{:S(2)}, u32[]{:S(2)}) %collective-permute-start.61) | collective-permute-done | bytes 589856 | tf_op jit(solution)/shard_map/ppermute | solution.py:66
  223.1 11.1 %collective-permute-done.43.rest_11_.rest_3_ = bf16[4,2,48,768]{3,2,1,0:T(8,128)(2,1)} collective-permute-done((bf16[4,2,48,768]{3,2,1,0:T(8,128)(2,1)}, bf16[4,2,48,768]{3,2,1,0:T(8,128)(2,1)}, u32[]{:S(2)}, u32[]{:S(2)}) %collective-permute-start.43) | collective-permute-done | bytes 589856 | tf_op jit(solution)/shard_map/ppermute | solution.py:66
  238.6 7.4 %collective-permute-done.25.rest_3_ = bf16[4,2,48,768]{3,2,1,0:T(8,128)(2,1)} collective-permute-done((bf16[4,2,48,768]{3,2,1,0:T(8,128)(2,1)}, bf16[4,2,48,768]{3,2,1,0:T(8,128)(2,1)}, u32[]{:S(2)}, u32[]{:S(2)}) %collective-permute-start.25) | collective-permute-done | bytes 589856 | tf_op jit(solution)/shard_map/ppermute | solution.py:66
  248.4 6.0 dec_before.1
  254.7 7.3 %collective-permute-done.34.rest_3_ = bf16[4,2,48,768]{3,2,1,0:T(8,128)(2,1)} collective-permute-done((bf16[4,2,48,768]{3,2,1,0:T(8,128)(2,1)}, bf16[4,2,48,768]{3,2,1,0:T(8,128)(2,1)}, u32[]{:S(2)}, u32[]{:S(2)}) %collective-permute-start.34) | collective-permute-done | bytes 589856 | tf_op jit(solution)/shard_map/ppermute | solution.py:66
  264.6 20.9 %enc_attention.1 = (bf16[512,768]{1,0:T(8,128)(2,1)}, bf16[512,768]{1,0:T(8,128)(2,1)}, bf16[512,768]{1,0:T(8,128)(2,1)}, bf16[512,768]{1,0:T(8,128)(2,1)}, bf16...) custom-call(s32[3]{0:T(128)} %pad_add_fusion.meta, ...), custom_call_target="tpu_custom_call" | custom-call | flops 4000000000 | bytes 12000000 | tf_op jit(solution)/shard_map/enc_attention/pallas_call | solution.py:249
  286.9 5.1 dec_grad_hidden.1
  292.1 16.1 %enc_ffn.1 = (bf16[512,3072]{1,0:T(8,128)(2,1)}, bf16[512,3072]{1,0:T(8,128)(2,1)}, bf16[512,768]{1,0:T(8,128)(2,1)}) custom-call(s32[3]{0:T(128)} %pad_add_fusion.meta, f32[512,768]{1,0:T(8,128)} %get-tuple-element.75.h1, bf16[512,768]{1,0:T(8,128)(2,1)} %get-tuple-element.76.n2, bf16[4,2,48,768]{3,2,1,0:T(8,128)(2,1)} %copy-done.24, ...), custom_call_target="tpu_custom_call" | custom-call | flops 5000000000 | bytes 18000000 | tf_op jit(solution)/shard_map/enc_ffn/pallas_call | solution.py:249
  309.7 10.0 %dec_core.1 = (bf16[512,768]{1,0:T(8,128)(2,1)}, bf16[8,768]{1,0:T(8,128)(2,1)}, f32[8,768]{1,0:T(8,128)}, bf16[8,768]{1,0:T(8,128)(2,1)}, bf16[8,3072]{1,0:T(8,...) custom-call(s32[3]{0:T(128)} %pad_add_fusion.meta, ...), custom_call_target="tpu_custom_call" | custom-call | flops 4000000000 | bytes 12000000 | tf_op jit(solution)/shard_map/dec_core/pallas_call | solution.py:249
  321.2 8.0 %dec_after.1 = (bf16[8,768]{1,0:T(8,128)(2,1)}, bf16[8,768]{1,0:T(8,128)(2,1)}, bf16[8,768]{1,0:T(8,128)(2,1)}, bf16[8,768]{1,0:T(8,128)(2,1)}, bf16[8,768]{1,0:...) custom-call(s32[3]{0:T(128)} %pad_add_fusion.meta, ...), custom_call_target="tpu_custom_call" | custom-call | flops 2000000000 | bytes 14000000 | tf_op jit(solution)/shard_map/dec_after/pallas_call | solution.py:249
  331.4 14.2 %enc_ffn_back_out.1 = (bf16[512,3072]{1,0:T(8,128)(2,1)}, bf16[16,2,48,768]{3,2,1,0:T(8,128)(2,1)}, bf16[16,2,48,768]{3,2,1,0:T(8,128)(2,1)}) custom-call(s32[3]{0:T(128)} %pad_add_fusion.meta, bf16[512,768]{1,0:T(8,128)(2,1)} %get-tuple-element.89.de, bf16[512,3072]{1,0:T(8,128)(2,1)} %get-tuple-element.90.f, bf16[512,3072]{1,0:T(8,128)(2,1)} %get-tuple-element.91.slope, ...), custom_call_target="tpu_custom_call" | custom-call | flops 5000000000 | bytes 18000000 | tf_op jit(solution)/shard_map/enc_ffn_back_out/pallas_call | solution.py:249
  345.6 13.2 %enc_ffn_back_in.1 = (f32[512,768]{1,0:T(8,128)}, bf16[512,768]{1,0:T(8,128)(2,1)}, f32[1,768]{1,0:T(1,128)}, bf16[16,2,48,768]{3,2,1,0:T(8,128)(2,1)}, bf16[16,2,48,768]{3,2,1,0:T(8,128)(2,1)}) custom-call(s32[3]{0:T(128)} %pad_add_fusion.meta, bf16[512,3072]{1,0:T(8,128)(2,1)} %get-tuple-element.92.du, bf16[512,768]{1,0:T(8,128)(2,1)} %get-tuple-element.76.n2, ...), custom_call_target="tpu_custom_call" | custom-call | flops 5000000000 | bytes 18000000 | tf_op jit(solution)/shard_map/enc_ffn_back_in/pallas_call | solution.py:249
  358.8 24.8 %enc_attention_back.1 = (bf16[768,768]{1,0:T(8,128)(2,1)}, bf16[512,768]{1,0:T(8,128)(2,1)}, bf16[512,768]{1,0:T(8,128)(2,1)}, bf16[512,768]{1,0:T(8,128)(2,1)}, f32[12,5,256]{2,1,0:T(8,128)}) custom-call(s32[3]{0:T(128)} %pad_add_fusion.meta, bf16[512,768]{1,0:T(8,128)(2,1)} %get-tuple-element.93.da, bf16[512,768]{1,0:T(8,128)(2,1)} %get-tuple-element.94.c, ...), custom_call_target="tpu_custom_call" | custom-call | flops 6000000000 | bytes 12000000 | tf_op jit(solution)/shard_map/enc_attention_back/pallas_call | solution.py:249
  385.0 8.5 %enc_input_grad.1 = (bf16[512,384]{1,0:T(8,128)(2,1)}, bf16[512,384]{1,0:T(8,128)(2,1)}, f32[1,768]{1,0:T(1,128)}) custom-call(s32[3]{0:T(128)} %pad_add_fusion.meta, bf16[512,768]{1,0:T(8,128)(2,1)} %get-tuple-element.99.dq, bf16[512,768]{1,0:T(8,128)(2,1)} %get-tuple-element.100.dk, bf16[512,768]{1,0:T(8,128)(2,1)} %get-tuple-element.101.dv, ...), custom_call_target="tpu_custom_call" | custom-call | flops 2000000000 | bytes 10000000 | tf_op jit(solution)/shard_map/enc_input_grad/pallas_call | solution.py:249
  400.8 5.9 enc_square_grads.1
  417.9 4.4 collective-permute-done.80
  423.5 5.9 collective-permute-done.81
  430.4 10.0 %collective-permute-done.82 = bf16[32,6912]{1,0:T(8,128)(2,1)S(1)} collective-permute-done((bf16[32,6912]{1,0:T(8,128)(2,1)S(1)}, bf16[32,6912]{1,0:T(8,128)(2,1)S(1)}, u32[]{:S(2)}, u32[]{:S(2)}) %collective-permute-start.82) | collective-permute-done | bytes 442400 | tf_op jit(solution)/shard_map/ppermute | solution.py:66
  443.7 11.7 %collective-permute-done.97 = bf16[8,1,48,768]{3,2,1,0:T(8,128)(2,1)S(1)} collective-permute-done((bf16[8,1,48,768]{3,2,1,0:T(8,128)(2,1)S(1)}, bf16[8,1,48,768]{3,2,1,0:T(8,128)(2,1)S(1)}, u32[]{:S(2)}, u32[]{:S(2)}) %collective-permute-start.97) | collective-permute-done | bytes 589856 | tf_op jit(solution)/shard_map/ppermute | solution.py:66
  455.6 24.2 %collective-permute-done.83 = bf16[64,6912]{1,0:T(8,128)(2,1)S(1)} collective-permute-done((bf16[64,6912]{1,0:T(8,128)(2,1)S(1)}, bf16[64,6912]{1,0:T(8,128)(2,1)S(1)}, u32[]{:S(2)}, u32[]{:S(2)}) %collective-permute-start.83) | collective-permute-done | bytes 884768 | tf_op jit(solution)/shard_map/ppermute | solution.py:66
  495.5 4.1 collective-permute-done.99
  500.7 14.4 %collective-permute-done.86 = bf16[8,2,48,768]{3,2,1,0:T(8,128)(2,1)} collective-permute-done((bf16[8,2,48,768]{3,2,1,0:T(8,128)(2,1)}, bf16[8,2,48,768]{3,2,1,0:T(8,128)(2,1)}, u32[]{:S(2)}, u32[]{:S(2)}) %collective-permute-start.86) | collective-permute-done | bytes 1179680 | tf_op jit(solution)/shard_map/ppermute | solution.py:66
  519.3 21.0 %collective-permute-done.75 = bf16[8,2,48,768]{3,2,1,0:T(8,128)(2,1)} collective-permute-done((bf16[8,2,48,768]{3,2,1,0:T(8,128)(2,1)}, bf16[8,2,48,768]{3,2,1,0:T(8,128)(2,1)}, u32[]{:S(2)}, u32[]{:S(2)}) %collective-permute-start.75) | collective-permute-done | bytes 1179680 | tf_op jit(solution)/shard_map/ppermute | solution.py:66
  546.9 5.0 collective-permute-done.92
  552.1 3.2 collective-permute-done.76
  555.6 18.1 %collective-permute-done.88 = bf16[2,2,48,768]{3,2,1,0:T(8,128)(2,1)S(1)} collective-permute-done((bf16[2,2,48,768]{3,2,1,0:T(8,128)(2,1)S(1)}, bf16[2,2,48,768]{3,2,1,0:T(8,128)(2,1)S(1)}, u32[]{:S(2)}, u32[]{:S(2)}) %collective-permute-start.88) | collective-permute-done | bytes 294944 | tf_op jit(solution)/shard_map/ppermute | solution.py:66
  573.8 6.3 %collective-permute-done.93 = bf16[2,2,48,768]{3,2,1,0:T(8,128)(2,1)S(1)} collective-permute-done((bf16[2,2,48,768]{3,2,1,0:T(8,128)(2,1)S(1)}, bf16[2,2,48,768]{3,2,1,0:T(8,128)(2,1)S(1)}, u32[]{:S(2)}, u32[]{:S(2)}) %collective-permute-start.93) | collective-permute-done | bytes 294944 | tf_op jit(solution)/shard_map/ppermute | solution.py:66
  580.2 6.1 %collective-permute-done.77 = bf16[2,2,48,768]{3,2,1,0:T(8,128)(2,1)S(1)} collective-permute-done((bf16[2,2,48,768]{3,2,1,0:T(8,128)(2,1)S(1)}, bf16[2,2,48,768]{3,2,1,0:T(8,128)(2,1)S(1)}, u32[]{:S(2)}, u32[]{:S(2)}) %collective-permute-start.77) | collective-permute-done | bytes 294944 | tf_op jit(solution)/shard_map/ppermute | solution.py:66
  586.4 3.0 collective-permute-done.89
  589.5 3.1 collective-permute-done.94
  592.7 3.0 collective-permute-done.78
  (429 shorter events, 156.0 us)
Async XLA Ops:
  7.4 28.1 %collective-permute-start.11 = (bf16[6,48,768]{2,1,0:T(8,128)(2,1)S(1)}, bf16[6,48,768]{2,1,0:T(8,128)(2,1)S(1)}, u32[]{:S(2)}, u32[]{:S(2)}) collective-permute-start(bf16[6,48,768]{2,1,0:T(8,128)(2,1)S(1)} %broadcast_select_fusion.4), channel_id=1, source_target_pairs={{0,16},{16,0},{1,17},{17,1},{2,18},{18,2},{3,19},{19,3},{4,20},{20... | collective-permute-start | bytes 1327112 | tf_op jit(solution)/shard_map/ppermute | solution.py:61
  27.8 38.1 %collective-permute-start.4 = (bf16[16,3,128]{2,1,0:T(4,128)(2,1)S(1)}, bf16[16,3,128]{2,1,0:T(4,128)(2,1)S(1)}, u32[]{:S(2)}, u32[]{:S(2)}) collective-permute-start(bf16[16,3,128]{2,1,0:T(4,128)(2,1)S(1)} %broadcast_select_fusion.8), channel_id=1, source_target_pairs={{0,16},{16,0},{1,17},{17,1},{2,18},{18,2},{3,19},{19,3},{4,20},{20... | collective-permute-start | bytes 36872 | tf_op jit(solution)/shard_map/ppermute | solution.py:61
  56.8 36.7 %collective-permute-start.49 = (bf16[2,2,48,768]{3,2,1,0:T(8,128)(2,1)S(1)}, bf16[2,2,48,768]{3,2,1,0:T(8,128)(2,1)S(1)}, u32[]{:S(2)}, u32[]{:S(2)}) collective-permute-start(bf16[2,2,48,768]{3,2,1,0:T(8,128)(2,1)S(1)} %pad_maximum_fusion.15), channel_id=1, source_target_pairs={{0,8},{1,9},{2,10},{3,11},{4,12},{5,13},{6,14},{7,15},{8,0},{9,1},... | collective-permute-start | bytes 884744 | tf_op jit(solution)/shard_map/ppermute | solution.py:66
  60.7 42.3 %collective-permute-start.58 = (bf16[2,2,48,768]{3,2,1,0:T(8,128)(2,1)S(1)}, bf16[2,2,48,768]{3,2,1,0:T(8,128)(2,1)S(1)}, u32[]{:S(2)}, u32[]{:S(2)}) collective-permute-start(bf16[2,2,48,768]{3,2,1,0:T(8,128)(2,1)S(1)} %pad_maximum_fusion.16), channel_id=1, source_target_pairs={{0,8},{1,9},{2,10},{3,11},{4,12},{5,13},{6,14},{7,15},{8,0},{9,1},... | collective-permute-start | bytes 884744 | tf_op jit(solution)/shard_map/ppermute | solution.py:66
  64.2 62.6 %collective-permute-start.8 = (bf16[4,2,48,768]{3,2,1,0:T(8,128)(2,1)S(1)}, bf16[4,2,48,768]{3,2,1,0:T(8,128)(2,1)S(1)}, u32[]{:S(2)}, u32[]{:S(2)}) collective-permute-start(bf16[4,2,48,768]{3,2,1,0:T(8,128)(2,1)S(1)} %pad_maximum_fusion.1.rest_0_), channel_id=1, source_target_pairs={{0,2},{1,3},{2,0},{3,1},{4,6},{5,7},{6,4},{7,5},{8,10},{9,11},{10,... | collective-permute-start | bytes 1769480 | tf_op jit(solution)/shard_map/ppermute | solution.py:66
  65.8 46.7 %collective-permute-start.40 = (bf16[2,2,48,768]{3,2,1,0:T(8,128)(2,1)S(1)}, bf16[2,2,48,768]{3,2,1,0:T(8,128)(2,1)S(1)}, u32[]{:S(2)}, u32[]{:S(2)}) collective-permute-start(bf16[2,2,48,768]{3,2,1,0:T(8,128)(2,1)S(1)} %pad_maximum_fusion.14), channel_id=1, source_target_pairs={{0,8},{1,9},{2,10},{3,11},{4,12},{5,13},{6,14},{7,15},{8,0},{9,1},... | collective-permute-start | bytes 884744 | tf_op jit(solution)/shard_map/ppermute | solution.py:66
  65.9 52.9 %collective-permute-start.31 = (bf16[2,2,48,768]{3,2,1,0:T(8,128)(2,1)S(1)}, bf16[2,2,48,768]{3,2,1,0:T(8,128)(2,1)S(1)}, u32[]{:S(2)}, u32[]{:S(2)}) collective-permute-start(bf16[2,2,48,768]{3,2,1,0:T(8,128)(2,1)S(1)} %pad_maximum_fusion.13), channel_id=1, source_target_pairs={{0,8},{1,9},{2,10},{3,11},{4,12},{5,13},{6,14},{7,15},{8,0},{9,1},... | collective-permute-start | bytes 884744 | tf_op jit(solution)/shard_map/ppermute | solution.py:66
  93.5 30.0 %collective-permute-start.22 = (bf16[2,2,48,768]{3,2,1,0:T(8,128)(2,1)S(1)}, bf16[2,2,48,768]{3,2,1,0:T(8,128)(2,1)S(1)}, u32[]{:S(2)}, u32[]{:S(2)}) collective-permute-start(bf16[2,2,48,768]{3,2,1,0:T(8,128)(2,1)S(1)} %pad_maximum_fusion.12), channel_id=1, source_target_pairs={{0,8},{1,9},{2,10},{3,11},{4,12},{5,13},{6,14},{7,15},{8,0},{9,1},... | collective-permute-start | bytes 884744 | tf_op jit(solution)/shard_map/ppermute | solution.py:66
  103.0 23.7 %collective-permute-start.13 = (bf16[2,2,48,768]{3,2,1,0:T(8,128)(2,1)S(1)}, bf16[2,2,48,768]{3,2,1,0:T(8,128)(2,1)S(1)}, u32[]{:S(2)}, u32[]{:S(2)}) collective-permute-start(bf16[2,2,48,768]{3,2,1,0:T(8,128)(2,1)S(1)} %pad_maximum_fusion.11), channel_id=1, source_target_pairs={{0,8},{1,9},{2,10},{3,11},{4,12},{5,13},{6,14},{7,15},{8,0},{9,1},... | collective-permute-start | bytes 884744 | tf_op jit(solution)/shard_map/ppermute | solution.py:66
  126.8 22.8 %collective-permute-start.59 = (bf16[4,2,48,768]{3,2,1,0:T(8,128)(2,1)S(1)}, bf16[4,2,48,768]{3,2,1,0:T(8,128)(2,1)}, u32[]{:S(2)}, u32[]{:S(2)}) collective-permute-start(bf16[4,2,48,768]{3,2,1,0:T(8,128)(2,1)S(1)} %pad_maximum_fusion.7.rest_8_), channel_id=1, source_target_pairs={{0,1},{1,0},{2,3},{3,2},{4,5},{5,4},{6,7},{7,6},{8,9},{9,8},{10,11... | collective-permute-start | bytes 1769480 | tf_op jit(solution)/shard_map/ppermute | solution.py:66
  128.7 33.5 %collective-permute-start.41 = (bf16[4,2,48,768]{3,2,1,0:T(8,128)(2,1)S(1)}, bf16[4,2,48,768]{3,2,1,0:T(8,128)(2,1)}, u32[]{:S(2)}, u32[]{:S(2)}) collective-permute-start(bf16[4,2,48,768]{3,2,1,0:T(8,128)(2,1)S(1)} %pad_maximum_fusion.5.rest_8_.rest_0_), channel_id=1, source_target_pairs={{0,1},{1,0},{2,3},{3,2},{4,5},{5,4},{6,7},{7,6},{8,9},{9,8},{10,11... | collective-permute-start | bytes 1769480 | tf_op jit(solution)/shard_map/ppermute | solution.py:66
  129.2 33.0 %collective-permute-start.42 = (bf16[4,2,48,768]{3,2,1,0:T(8,128)(2,1)S(1)}, bf16[4,2,48,768]{3,2,1,0:T(8,128)(2,1)S(1)}, u32[]{:S(2)}, u32[]{:S(2)}) collective-permute-start(bf16[4,2,48,768]{3,2,1,0:T(8,128)(2,1)S(1)} %pad_maximum_fusion.5.rest_8_.rest_0_), channel_id=1, source_target_pairs={{0,2},{1,3},{2,0},{3,1},{4,6},{5,7},{6,4},{7,5},{8,10},{9,11},{10,... | collective-permute-start | bytes 1769480 | tf_op jit(solution)/shard_map/ppermute | solution.py:66
  136.9 27.0 %collective-permute-start.44 = (bf16[4,2,48,768]{3,2,1,0:T(8,128)(2,1)S(1)}, bf16[4,2,48,768]{3,2,1,0:T(8,128)(2,1)S(1)}, u32[]{:S(2)}, u32[]{:S(2)}) collective-permute-start(bf16[4,2,48,768]{3,2,1,0:T(8,128)(2,1)S(1)} %pad_maximum_fusion.5.rest_8_.rest_0_), channel_id=1, source_target_pairs={{0,16},{16,0},{1,17},{17,1},{2,18},{18,2},{3,19},{19,3},{4,20},{20... | collective-permute-start | bytes 1769480 | tf_op jit(solution)/shard_map/ppermute | solution.py:61
  136.9 28.5 %collective-permute-start.32 = (bf16[4,2,48,768]{3,2,1,0:T(8,128)(2,1)S(1)}, bf16[4,2,48,768]{3,2,1,0:T(8,128)(2,1)}, u32[]{:S(2)}, u32[]{:S(2)}) collective-permute-start(bf16[4,2,48,768]{3,2,1,0:T(8,128)(2,1)S(1)} %pad_maximum_fusion.4.rest_0_), channel_id=1, source_target_pairs={{0,2},{1,3},{2,0},{3,1},{4,6},{5,7},{6,4},{7,5},{8,10},{9,11},{10,... | collective-permute-start | bytes 1769480 | tf_op jit(solution)/shard_map/ppermute | solution.py:66
  149.6 25.2 %collective-permute-start.33 = (bf16[4,2,48,768]{3,2,1,0:T(8,128)(2,1)S(1)}, bf16[4,2,48,768]{3,2,1,0:T(8,128)(2,1)S(1)}, u32[]{:S(2)}, u32[]{:S(2)}) collective-permute-start(bf16[4,2,48,768]{3,2,1,0:T(8,128)(2,1)S(1)} %pad_maximum_fusion.4.rest_0_), channel_id=1, source_target_pairs={{0,1},{1,0},{2,3},{3,2},{4,5},{5,4},{6,7},{7,6},{8,9},{9,8},{10,11... | collective-permute-start | bytes 1769480 | tf_op jit(solution)/shard_map/ppermute | solution.py:66
  162.2 22.4 %collective-permute-start.23 = (bf16[4,2,48,768]{3,2,1,0:T(8,128)(2,1)S(1)}, bf16[4,2,48,768]{3,2,1,0:T(8,128)(2,1)}, u32[]{:S(2)}, u32[]{:S(2)}) collective-permute-start(bf16[4,2,48,768]{3,2,1,0:T(8,128)(2,1)S(1)} %pad_maximum_fusion.3.rest_0_), channel_id=1, source_target_pairs={{0,1},{1,0},{2,3},{3,2},{4,5},{5,4},{6,7},{7,6},{8,9},{9,8},{10,11... | collective-permute-start | bytes 1769480 | tf_op jit(solution)/shard_map/ppermute | solution.py:66
  163.9 22.3 %collective-permute-start.24 = (bf16[4,2,48,768]{3,2,1,0:T(8,128)(2,1)S(1)}, bf16[4,2,48,768]{3,2,1,0:T(8,128)(2,1)}, u32[]{:S(2)}, u32[]{:S(2)}) collective-permute-start(bf16[4,2,48,768]{3,2,1,0:T(8,128)(2,1)S(1)} %pad_maximum_fusion.3.rest_0_), channel_id=1, source_target_pairs={{0,2},{1,3},{2,0},{3,1},{4,6},{5,7},{6,4},{7,5},{8,10},{9,11},{10,... | collective-permute-start | bytes 1769480 | tf_op jit(solution)/shard_map/ppermute | solution.py:66
  176.5 28.1 %collective-permute-start.14 = (bf16[4,2,48,768]{3,2,1,0:T(8,128)(2,1)S(1)}, bf16[4,2,48,768]{3,2,1,0:T(8,128)(2,1)S(1)}, u32[]{:S(2)}, u32[]{:S(2)}) collective-permute-start(bf16[4,2,48,768]{3,2,1,0:T(8,128)(2,1)S(1)} %pad_maximum_fusion.2.rest_4_.rest_0_), channel_id=1, source_target_pairs={{0,2},{1,3},{2,0},{3,1},{4,6},{5,7},{6,4},{7,5},{8,10},{9,11},{10,... | collective-permute-start | bytes 1769480 | tf_op jit(solution)/shard_map/ppermute | solution.py:66
  206.6 27.6 %collective-permute-start.43 = (bf16[4,2,48,768]{3,2,1,0:T(8,128)(2,1)}, bf16[4,2,48,768]{3,2,1,0:T(8,128)(2,1)}, u32[]{:S(2)}, u32[]{:S(2)}) collective-permute-start(bf16[4,2,48,768]{3,2,1,0:T(8,128)(2,1)} %collective-permute-done.41.rest_9_.rest_1_), channel_id=1, source_target_pairs={{0,2},{1,3},{2,0},{3,1},{4,6},{5,7},{6,4},{7,5},{8,10},{9,11},{10,... | collective-permute-start | bytes 1769480 | tf_op jit(solution)/shard_map/ppermute | solution.py:66
  210.2 24.1 %collective-permute-start.16 = (bf16[4,2,48,768]{3,2,1,0:T(8,128)(2,1)S(1)}, bf16[4,2,48,768]{3,2,1,0:T(8,128)(2,1)S(1)}, u32[]{:S(2)}, u32[]{:S(2)}) collective-permute-start(bf16[4,2,48,768]{3,2,1,0:T(8,128)(2,1)S(1)} %collective-permute-done.14.rest_5_.rest_1_), channel_id=1, source_target_pairs={{0,1},{1,0},{2,3},{3,2},{4,5},{5,4},{6,7},{7,6},{8,9},{9,8},{10,11... | collective-permute-start | bytes 1769480 | tf_op jit(solution)/shard_map/ppermute | solution.py:66
  213.0 25.5 %collective-permute-start.45 = (bf16[4,2,48,768]{3,2,1,0:T(8,128)(2,1)}, bf16[4,2,48,768]{3,2,1,0:T(8,128)(2,1)}, u32[]{:S(2)}, u32[]{:S(2)}) collective-permute-start(bf16[4,2,48,768]{3,2,1,0:T(8,128)(2,1)} %collective-permute-done.41.rest_9_.rest_1_), channel_id=1, source_target_pairs={{0,16},{16,0},{1,17},{17,1},{2,18},{18,2},{3,19},{19,3},{4,20},{20... | collective-permute-start | bytes 1769480 | tf_op jit(solution)/shard_map/ppermute | solution.py:61
  213.1 32.9 %collective-permute-start.18 = (bf16[4,2,48,768]{3,2,1,0:T(8,128)(2,1)S(1)}, bf16[4,2,48,768]{3,2,1,0:T(8,128)(2,1)}, u32[]{:S(2)}, u32[]{:S(2)}) collective-permute-start(bf16[4,2,48,768]{3,2,1,0:T(8,128)(2,1)S(1)} %collective-permute-done.14.rest_5_.rest_1_), channel_id=1, source_target_pairs={{0,16},{16,0},{1,17},{17,1},{2,18},{18,2},{3,19},{19,3},{4,20},{20... | collective-permute-start | bytes 1769480 | tf_op jit(solution)/shard_map/ppermute | solution.py:61
  221.6 24.4 %collective-permute-start.25 = (bf16[4,2,48,768]{3,2,1,0:T(8,128)(2,1)}, bf16[4,2,48,768]{3,2,1,0:T(8,128)(2,1)}, u32[]{:S(2)}, u32[]{:S(2)}) collective-permute-start(bf16[4,2,48,768]{3,2,1,0:T(8,128)(2,1)} %collective-permute-done.23.rest_1_), channel_id=1, source_target_pairs={{0,2},{1,3},{2,0},{3,1},{4,6},{5,7},{6,4},{7,5},{8,10},{9,11},{10,... | collective-permute-start | bytes 1769480 | tf_op jit(solution)/shard_map/ppermute | solution.py:66
  238.5 23.6 %collective-permute-start.27 = (bf16[4,2,48,768]{3,2,1,0:T(8,128)(2,1)}, bf16[4,2,48,768]{3,2,1,0:T(8,128)(2,1)S(1)}, u32[]{:S(2)}, u32[]{:S(2)}) collective-permute-start(bf16[4,2,48,768]{3,2,1,0:T(8,128)(2,1)} %collective-permute-done.23.rest_1_), channel_id=1, source_target_pairs={{0,16},{16,0},{1,17},{17,1},{2,18},{18,2},{3,19},{19,3},{4,20},{20... | collective-permute-start | bytes 1769480 | tf_op jit(solution)/shard_map/ppermute | solution.py:61
  254.4 31.0 %collective-permute-start.36 = (bf16[4,2,48,768]{3,2,1,0:T(8,128)(2,1)}, bf16[4,2,48,768]{3,2,1,0:T(8,128)(2,1)S(1)}, u32[]{:S(2)}, u32[]{:S(2)}) collective-permute-start(bf16[4,2,48,768]{3,2,1,0:T(8,128)(2,1)} %collective-permute-done.32.rest_1_), channel_id=1, source_target_pairs={{0,16},{16,0},{1,17},{17,1},{2,18},{18,2},{3,19},{19,3},{4,20},{20... | collective-permute-start | bytes 1769480 | tf_op jit(solution)/shard_map/ppermute | solution.py:61
  262.1 23.7 %collective-permute-start.37 = (bf16[4,2,48,768]{3,2,1,0:T(8,128)(2,1)S(1)}, bf16[4,2,48,768]{3,2,1,0:T(8,128)(2,1)S(1)}, u32[]{:S(2)}, u32[]{:S(2)}) collective-permute-start(bf16[4,2,48,768]{3,2,1,0:T(8,128)(2,1)S(1)} %copy-done.48), channel_id=1, source_target_pairs={{0,16},{16,0},{1,17},{17,1},{2,18},{18,2},{3,19},{19,3},{4,20},{20... | collective-permute-start | bytes 1769480 | tf_op jit(solution)/shard_map/ppermute | solution.py:61
  262.1 24.0 %collective-permute-start.56 = (bf16[4,2,48,768]{3,2,1,0:T(8,128)(2,1)S(1)}, bf16[4,2,48,768]{3,2,1,0:T(8,128)(2,1)S(1)}, u32[]{:S(2)}, u32[]{:S(2)}) collective-permute-start(bf16[4,2,48,768]{3,2,1,0:T(8,128)(2,1)S(1)} %copy-done.17), channel_id=1, source_target_pairs={{0,16},{16,0},{1,17},{17,1},{2,18},{18,2},{3,19},{19,3},{4,20},{20... | collective-permute-start | bytes 1769480 | tf_op jit(solution)/shard_map/ppermute | solution.py:61
  262.6 23.7 %collective-permute-start.47 = (bf16[4,2,48,768]{3,2,1,0:T(8,128)(2,1)}, bf16[4,2,48,768]{3,2,1,0:T(8,128)(2,1)}, u32[]{:S(2)}, u32[]{:S(2)}) collective-permute-start(bf16[4,2,48,768]{3,2,1,0:T(8,128)(2,1)} %collective-permute-done.43.rest_11_.rest_3_), channel_id=1, source_target_pairs={{0,16},{16,0},{1,17},{17,1},{2,18},{18,2},{3,19},{19,3},{4,20},{20... | collective-permute-start | bytes 1769480 | tf_op jit(solution)/shard_map/ppermute | solution.py:61
  263.5 28.6 %collective-permute-start.38 = (bf16[4,2,48,768]{3,2,1,0:T(8,128)(2,1)}, bf16[4,2,48,768]{3,2,1,0:T(8,128)(2,1)}, u32[]{:S(2)}, u32[]{:S(2)}) collective-permute-start(bf16[4,2,48,768]{3,2,1,0:T(8,128)(2,1)} %collective-permute-done.34.rest_3_), channel_id=1, source_target_pairs={{0,16},{16,0},{1,17},{17,1},{2,18},{18,2},{3,19},{19,3},{4,20},{20... | collective-permute-start | bytes 1769480 | tf_op jit(solution)/shard_map/ppermute | solution.py:61
  285.5 22.7 %collective-permute-start.62 = (bf16[4,2,48,768]{3,2,1,0:T(8,128)(2,1)S(1)}, bf16[4,2,48,768]{3,2,1,0:T(8,128)(2,1)S(1)}, u32[]{:S(2)}, u32[]{:S(2)}) collective-permute-start(bf16[4,2,48,768]{3,2,1,0:T(8,128)(2,1)S(1)} %copy-done.27), channel_id=1, source_target_pairs={{0,16},{16,0},{1,17},{17,1},{2,18},{18,2},{3,19},{19,3},{4,20},{20... | collective-permute-start | bytes 1769480 | tf_op jit(solution)/shard_map/ppermute | solution.py:61
  285.7 22.6 %collective-permute-start.63 = (bf16[4,2,48,768]{3,2,1,0:T(8,128)(2,1)}, bf16[4,2,48,768]{3,2,1,0:T(8,128)(2,1)S(1)}, u32[]{:S(2)}, u32[]{:S(2)}) collective-permute-start(bf16[4,2,48,768]{3,2,1,0:T(8,128)(2,1)} %collective-permute-done.59.rest_9_), channel_id=1, source_target_pairs={{0,16},{16,0},{1,17},{17,1},{2,18},{18,2},{3,19},{19,3},{4,20},{20... | collective-permute-start | bytes 1769480 | tf_op jit(solution)/shard_map/ppermute | solution.py:61
  286.1 22.2 %collective-permute-start.64 = (bf16[4,2,48,768]{3,2,1,0:T(8,128)(2,1)S(1)}, bf16[4,2,48,768]{3,2,1,0:T(8,128)(2,1)S(1)}, u32[]{:S(2)}, u32[]{:S(2)}) collective-permute-start(bf16[4,2,48,768]{3,2,1,0:T(8,128)(2,1)S(1)} %copy-done.52), channel_id=1, source_target_pairs={{0,16},{16,0},{1,17},{17,1},{2,18},{18,2},{3,19},{19,3},{4,20},{20... | collective-permute-start | bytes 1769480 | tf_op jit(solution)/shard_map/ppermute | solution.py:61
  396.1 85.2 %collective-permute-start.85 = (bf16[16,2,48,768]{3,2,1,0:T(8,128)(2,1)}, bf16[16,2,48,768]{3,2,1,0:T(8,128)(2,1)S(1)}, u32[]{:S(2)}, u32[]{:S(2)}) collective-permute-start(bf16[16,2,48,768]{3,2,1,0:T(8,128)(2,1)} %get-tuple-element.126), channel_id=1, source_target_pairs={{0,16},{16,0},{1,17},{17,1},{2,18},{18,2},{3,19},{19,3},{4,20},{20... | collective-permute-start | bytes 7077896 | tf_op jit(solution)/shard_map/ppermute | solution.py:61
  396.6 86.5 %collective-permute-start.90 = (bf16[16,2,48,768]{3,2,1,0:T(8,128)(2,1)}, bf16[16,2,48,768]{3,2,1,0:T(8,128)(2,1)S(1)}, u32[]{:S(2)}, u32[]{:S(2)}) collective-permute-start(bf16[16,2,48,768]{3,2,1,0:T(8,128)(2,1)} %get-tuple-element.128), channel_id=1, source_target_pairs={{0,16},{16,0},{1,17},{17,1},{2,18},{18,2},{3,19},{19,3},{4,20},{20... | collective-permute-start | bytes 7077896 | tf_op jit(solution)/shard_map/ppermute | solution.py:61
  408.0 78.3 %collective-permute-start.74 = (bf16[16,2,48,768]{3,2,1,0:T(8,128)(2,1)}, bf16[16,2,48,768]{3,2,1,0:T(8,128)(2,1)S(1)}, u32[]{:S(2)}, u32[]{:S(2)}) collective-permute-start(bf16[16,2,48,768]{3,2,1,0:T(8,128)(2,1)} %get-tuple-element.115), channel_id=1, source_target_pairs={{0,16},{16,0},{1,17},{17,1},{2,18},{18,2},{3,19},{19,3},{4,20},{20... | collective-permute-start | bytes 7077896 | tf_op jit(solution)/shard_map/ppermute | solution.py:61
  415.5 26.5 %collective-permute-start.96 = (bf16[16,1,48,768]{3,2,1,0:T(8,128)(2,1)}, bf16[16,1,48,768]{3,2,1,0:T(8,128)(2,1)S(1)}, u32[]{:S(2)}, u32[]{:S(2)}) collective-permute-start(bf16[16,1,48,768]{3,2,1,0:T(8,128)(2,1)} %get-tuple-element.130), channel_id=1, source_target_pairs={{0,16},{16,0},{1,17},{17,1},{2,18},{18,2},{3,19},{19,3},{4,20},{20... | collective-permute-start | bytes 3538952 | tf_op jit(solution)/shard_map/ppermute | solution.py:61
  440.5 39.3 %collective-permute-start.83 = (bf16[64,6912]{1,0:T(8,128)(2,1)S(1)}, bf16[64,6912]{1,0:T(8,128)(2,1)S(1)}, u32[]{:S(2)}, u32[]{:S(2)}) collective-permute-start(bf16[64,6912]{1,0:T(8,128)(2,1)S(1)} %pad_maximum_fusion), channel_id=1, source_target_pairs={{0,8},{1,9},{2,10},{3,11},{4,12},{5,13},{6,14},{7,15},{8,0},{9,1},... | collective-permute-start | bytes 2654216 | tf_op jit(solution)/shard_map/ppermute | solution.py:66
  455.4 35.6 %collective-permute-start.67 = (bf16[512,384]{1,0:T(8,128)(2,1)S(1)}, bf16[512,384]{1,0:T(8,128)(2,1)}, u32[]{:S(2)}, u32[]{:S(2)}) collective-permute-start(bf16[512,384]{1,0:T(8,128)(2,1)S(1)} %copy-done.59), channel_id=1, source_target_pairs={{0,16},{16,0},{1,17},{17,1},{2,18},{18,2},{3,19},{19,3},{4,20},{20... | collective-permute-start | bytes 1179656 | tf_op jit(solution)/shard_map/ppermute | solution.py:61
  481.3 61.2 %collective-permute-start.84 = (bf16[128,6912]{1,0:T(8,128)(2,1)}, bf16[128,6912]{1,0:T(8,128)(2,1)}, u32[]{:S(2)}, u32[]{:S(2)}) collective-permute-start(bf16[128,6912]{1,0:T(8,128)(2,1)} %constant_dynamic-update-slice_fusion.21), channel_id=1, source_target_pairs={{0,16},{16,0},{1,17},{17,1},{2,18},{18,2},{3,19},{19,3},{4,20},{20... | collective-permute-start | bytes 5308424 | tf_op jit(solution)/shard_map/ppermute | solution.py:61
  483.1 32.0 %collective-permute-start.86 = (bf16[8,2,48,768]{3,2,1,0:T(8,128)(2,1)}, bf16[8,2,48,768]{3,2,1,0:T(8,128)(2,1)}, u32[]{:S(2)}, u32[]{:S(2)}) collective-permute-start(bf16[8,2,48,768]{3,2,1,0:T(8,128)(2,1)} %get-tuple-element.163), channel_id=1, source_target_pairs={{0,1},{1,0},{2,3},{3,2},{4,5},{5,4},{6,7},{7,6},{8,9},{9,8},{10,11... | collective-permute-start | bytes 3538952 | tf_op jit(solution)/shard_map/ppermute | solution.py:66
  486.3 30.9 %collective-permute-start.91 = (bf16[8,2,48,768]{3,2,1,0:T(8,128)(2,1)}, bf16[8,2,48,768]{3,2,1,0:T(8,128)(2,1)}, u32[]{:S(2)}, u32[]{:S(2)}) collective-permute-start(bf16[8,2,48,768]{3,2,1,0:T(8,128)(2,1)} %get-tuple-element.165), channel_id=1, source_target_pairs={{0,2},{1,3},{2,0},{3,1},{4,6},{5,7},{6,4},{7,5},{8,10},{9,11},{10,... | collective-permute-start | bytes 3538952 | tf_op jit(solution)/shard_map/ppermute | solution.py:66
  489.7 50.7 %collective-permute-start.75 = (bf16[8,2,48,768]{3,2,1,0:T(8,128)(2,1)}, bf16[8,2,48,768]{3,2,1,0:T(8,128)(2,1)}, u32[]{:S(2)}, u32[]{:S(2)}) collective-permute-start(bf16[8,2,48,768]{3,2,1,0:T(8,128)(2,1)} %get-tuple-element.167), channel_id=1, source_target_pairs={{0,1},{1,0},{2,3},{3,2},{4,5},{5,4},{6,7},{7,6},{8,9},{9,8},{10,11... | collective-permute-start | bytes 3538952 | tf_op jit(solution)/shard_map/ppermute | solution.py:66
  500.6 97.3 %collective-permute-start.100 = (bf16[1,1,48,768]{3,2,1,0:T(8,128)(2,1)S(1)}, bf16[1,1,48,768]{3,2,1,0:T(8,128)(2,1)S(1)}, u32[]{:S(2)}, u32[]{:S(2)}) collective-permute-start(bf16[1,1,48,768]{3,2,1,0:T(8,128)(2,1)S(1)} %add_convert_fusion.30), channel_id=1, source_target_pairs={{0,4},{1,5},{2,6},{3,7},{4,0},{5,1},{6,2},{7,3},{8,12},{9,13},{10,... | collective-permute-start | bytes 221192 | tf_op jit(solution)/shard_map/ppermute | solution.py:66
  516.6 30.1 %collective-permute-start.87 = (bf16[4,2,48,768]{3,2,1,0:T(8,128)(2,1)S(1)}, bf16[4,2,48,768]{3,2,1,0:T(8,128)(2,1)S(1)}, u32[]{:S(2)}, u32[]{:S(2)}) collective-permute-start(bf16[4,2,48,768]{3,2,1,0:T(8,128)(2,1)S(1)} %get-tuple-element.173), channel_id=1, source_target_pairs={{0,2},{1,3},{2,0},{3,1},{4,6},{5,7},{6,4},{7,5},{8,10},{9,11},{10,... | collective-permute-start | bytes 1769480 | tf_op jit(solution)/shard_map/ppermute | solution.py:66
  518.7 33.2 %collective-permute-start.92 = (bf16[4,2,48,768]{3,2,1,0:T(8,128)(2,1)S(1)}, bf16[4,2,48,768]{3,2,1,0:T(8,128)(2,1)S(1)}, u32[]{:S(2)}, u32[]{:S(2)}) collective-permute-start(bf16[4,2,48,768]{3,2,1,0:T(8,128)(2,1)S(1)} %get-tuple-element.175), channel_id=1, source_target_pairs={{0,1},{1,0},{2,3},{3,2},{4,5},{5,4},{6,7},{7,6},{8,9},{9,8},{10,11... | collective-permute-start | bytes 1769480 | tf_op jit(solution)/shard_map/ppermute | solution.py:66
  546.8 26.8 %collective-permute-start.88 = (bf16[2,2,48,768]{3,2,1,0:T(8,128)(2,1)S(1)}, bf16[2,2,48,768]{3,2,1,0:T(8,128)(2,1)S(1)}, u32[]{:S(2)}, u32[]{:S(2)}) collective-permute-start(bf16[2,2,48,768]{3,2,1,0:T(8,128)(2,1)S(1)} %get-tuple-element.186), channel_id=1, source_target_pairs={{0,8},{1,9},{2,10},{3,11},{4,12},{5,13},{6,14},{7,15},{8,0},{9,1},... | collective-permute-start | bytes 884744 | tf_op jit(solution)/shard_map/ppermute | solution.py:66
  552.1 28.0 %collective-permute-start.93 = (bf16[2,2,48,768]{3,2,1,0:T(8,128)(2,1)S(1)}, bf16[2,2,48,768]{3,2,1,0:T(8,128)(2,1)S(1)}, u32[]{:S(2)}, u32[]{:S(2)}) collective-permute-start(bf16[2,2,48,768]{3,2,1,0:T(8,128)(2,1)S(1)} %get-tuple-element.188), channel_id=1, source_target_pairs={{0,8},{1,9},{2,10},{3,11},{4,12},{5,13},{6,14},{7,15},{8,0},{9,1},... | collective-permute-start | bytes 884744 | tf_op jit(solution)/shard_map/ppermute | solution.py:66
  555.5 30.8 %collective-permute-start.77 = (bf16[2,2,48,768]{3,2,1,0:T(8,128)(2,1)S(1)}, bf16[2,2,48,768]{3,2,1,0:T(8,128)(2,1)S(1)}, u32[]{:S(2)}, u32[]{:S(2)}) collective-permute-start(bf16[2,2,48,768]{3,2,1,0:T(8,128)(2,1)S(1)} %get-tuple-element.190), channel_id=1, source_target_pairs={{0,8},{1,9},{2,10},{3,11},{4,12},{5,13},{6,14},{7,15},{8,0},{9,1},... | collective-permute-start | bytes 884744 | tf_op jit(solution)/shard_map/ppermute | solution.py:66
  (115 other events, 2051.7 us)

commit v2 on v1

v2 whole, which is shorter than its diff:
```python
import functools

import jax
import jax.numpy as jnp
import numpy as np
from jax import lax
from jax.experimental import pallas as pl
from jax.experimental.pallas import tpu as pltpu
from jax.sharding import PartitionSpec as P

D = 768
HEADS = 12
HEAD_DIM = 64
FF = 3072
BUCKETS = 32
MAX_DIST = 128
ROW_LEN = 512
SEGS = 4
GROUP = 48
GROUPS = D // GROUP
X, Y, Z0, Z1 = 0, 1, 2, 3
TILE = 128
EPS = 1e-06
MASKED = -1000000000.0
BF = jnp.bfloat16
F32 = jnp.float32
VMEM_LIMIT = 58 * 1024 * 1024


def bucket_of(offset):
    half, exact = BUCKETS // 2, BUCKETS // 4
    exponent, growth = half - exact, MAX_DIST // exact
    distance = abs(offset)
    if distance < exact:
        level = distance
    else:
        k = 0
        while k < exponent and exact**exponent * growth ** (k + 1) <= distance**exponent:
            k += 1
        level = min(exact + k, half - 1)
    return (half if offset > 0 else 0) + level


def window_onehots():
    table = np.zeros((2, 3, 2 * TILE, BUCKETS), np.float32)
    for d in range(3):
        for t in range(2 * TILE):
            table[0, d, t, bucket_of(TILE * (d - 1) - TILE + t)] = 1.0
            table[1, d, t, bucket_of(TILE * (d - 1) + TILE - t)] = 1.0
    return table


def diagonal_onehots():
    table = np.zeros((5, 2 * TILE, BUCKETS), np.float32)
    table[1:4] = window_onehots()[1]
    table[0, :, bucket_of(-TILE - 1)] = 1.0
    table[4, :, bucket_of(TILE + 1)] = 1.0
    return table


def across(value):
    return lax.ppermute(value, "section", [(0, 1), (1, 0)])


def along(value, bit):
    count = lax.axis_size("dp")
    return lax.ppermute(value, "dp", [(i, i ^ (1 << bit)) for i in range(count)])


def bit_of(index, bit):
    return lax.rem(lax.div(index, 1 << bit), 2)


def low_bits(rows):
    count = 0
    while rows < GROUP:
        rows *= 2
        count += 1
    return count


def filled(piece, pre, chip, axis):
    for bit in range(pre):
        other = along(piece, bit)
        upper = bit_of(chip, bit) == 1
        first = jnp.where(upper, other, piece)
        second = jnp.where(upper, piece, other)
        piece = jnp.concatenate([first, second], axis=axis)
    return piece


def narrowed(total, pre, chip):
    for bit in reversed(range(pre)):
        length = total.shape[0] // 2
        upper = bit_of(chip, bit)
        kept = lax.dynamic_slice_in_dim(total, upper * length, length, 0)
        sent = lax.dynamic_slice_in_dim(total, (1 - upper) * length, length, 0)
        total = added(kept, along(sent.astype(BF), bit), F32)
    return total


def gate(after, *values):
    out = lax.optimization_barrier((tuple(values), tuple(after)))[0]
    return out[0] if len(values) == 1 else out


class Chain:
    def __init__(self, piece, pre):
        self.held, self.ids, self.pre = piece[None], [0], pre

    def split(self, at):
        parts = []
        for held in (self.held[:, :at], self.held[:, at:]):
            part = Chain(held[0], self.pre)
            part.held, part.ids = held, self.ids
            parts.append(part)
        return parts

    def step(self, bit):
        got = along(self.held, bit + self.pre)
        self.held = jnp.concatenate([self.held, got], axis=0)
        self.ids = self.ids + [g ^ (1 << bit) for g in self.ids]
        return [got]

    def last(self, bit):
        self.last_got = along(self.held, bit + self.pre)
        self.last_ids = [g ^ (1 << bit) for g in self.ids]
        return [self.last_got]

    def cross(self):
        self.other = across(self.held)
        return [self.other]

    def cross_last(self):
        self.other_last = across(self.last_got)
        return [self.other_last]

    def sets(self):
        return [
            (self.held, self.ids, 0), (self.last_got, self.last_ids, 0),
            (self.other, self.ids, 1), (self.other_last, self.last_ids, 1),
        ]


def gate_chains(after, *chains):
    held = lax.optimization_barrier((tuple(c.held for c in chains), tuple(after)))[0]
    for chain, value in zip(chains, held):
        chain.held = value


def added(left, right, kind=BF):
    return (left.astype(F32) + right.astype(F32)).astype(kind)


class Sum:
    def __init__(self, keep, send, pre):
        self.mine, self.send, self.got, self.pre = keep, send, None, pre

    def step(self, bit):
        if self.got is not None:
            half = self.mine.shape[0] // 2
            self.send = added(self.mine[half:], self.got[half:])
            self.mine = added(self.mine[:half], self.got[:half])
        self.got = along(self.send, bit + self.pre)
        return [self.got]

    def total(self):
        return added(self.mine[0], self.got[0], F32)


def merged(sums):
    one = Sum(jnp.concatenate([part.mine for part in sums], axis=1), None, sums[0].pre)
    one.got = jnp.concatenate([part.got for part in sums], axis=1)
    return one


def nn(a, b):
    return lax.dot_general(a, b, (((1,), (0,)), ((), ())), preferred_element_type=F32)


def nt(a, b):
    return lax.dot_general(a, b, (((1,), (1,)), ((), ())), preferred_element_type=F32)


def tn(a, b):
    return lax.dot_general(a, b, (((0,), (0,)), ((), ())), preferred_element_type=F32)


def rms(v, gain):
    return v * lax.rsqrt(jnp.mean(v * v, axis=-1, keepdims=True) + EPS) * gain


def rms_back(v, gain, dy):
    r = lax.rsqrt(jnp.mean(v * v, axis=-1, keepdims=True) + EPS)
    dgain = jnp.sum(dy * v * r, axis=0, keepdims=True)
    dyg = dy * gain
    dv = r * dyg - v * (r * r * r) * jnp.mean(v * dyg, axis=-1, keepdims=True)
    return dv, dgain


def gelu_both(u):
    c = 0.7978845608028654
    t = jnp.tanh(c * (u + 0.044715 * u * u * u))
    value = 0.5 * u * (1.0 + t)
    slope = 0.5 * (1.0 + t) + (0.5 * c) * u * (1.0 - t * t) * (1.0 + 3 * 0.044715 * u * u)
    return value, slope


def square_row(b):
    return lambda core, g: (core * 2 + b) * D + GROUP * g


def back_row(b):
    return lambda core, g: 4 * GROUP * g + GROUP * (2 * core + b)


def in_items(first):
    return [(first + GROUP * b, GROUP, square_row(b), lambda core, g, b=b: 2 * core + b) for b in range(2)]


def back_items(first):
    return [(first, 2 * GROUP, back_row(0), lambda core, g: g // 4)]


def start_fetch(meta, refs, plan, items, dst, sem, only=None):
    if only is not None:
        for other in range(2):
            part = [(ref, entry) for ref, entry in zip(refs, plan) if entry[1] == other]

            @pl.when(jnp.bitwise_xor(meta[1], other) == only)
            def _():
                start_fetch(meta, [r for r, e in part], [e for r, e in part], items, dst, sem)

        return
    me, core = meta[0], meta[1]
    for first, count, row_of, *sem_of in items:
        for ref, (ids, other) in zip(refs, plan):
            source = 1 - core if other else core
            for slot, rel in enumerate(ids):
                group = jnp.bitwise_xor(me, rel)
                off = pl.multiple_of(row_of(source, group), 16)
                at = sem.at[sem_of[0](source, group)] if sem_of else sem
                pltpu.make_async_copy(ref.at[slot, pl.ds(first, count)], dst.at[pl.ds(off, count)], at).start()


def drain(ref, sem):
    pltpu.make_async_copy(ref, ref, sem).wait()


def slot_of(meta, group, b):
    rel = jnp.bitwise_xor(meta[0], group)
    x, y, z0, z1 = [jnp.bitwise_and(rel // (1 << bit), 1) for bit in range(4)]
    return (8 * y + 4 * x if b == 0 else 8 * x + 4 * y) + 2 * z0 + z1


def start_store(meta, src, group, b, keep, send, sem, cols=None):
    slot = slot_of(meta, group, b)
    at = () if cols is None else (slice(None), cols)

    @pl.when(slot < GROUPS // 2)
    def _():
        pltpu.make_async_copy(src, keep.at[(slot,) + at], sem).start()

    @pl.when(slot >= GROUPS // 2)
    def _():
        pltpu.make_async_copy(src, send.at[(slot - GROUPS // 2,) + at], sem).start()


def head_lanes(h):
    lane = lax.broadcasted_iota(jnp.int32, (1, D), 1)
    return (lane >= h * HEAD_DIM) & (lane < (h + 1) * HEAD_DIM)


def pair_lanes(hh):
    lane = lax.broadcasted_iota(jnp.int32, (1, TILE), 1)
    return (lane < HEAD_DIM) if hh == 0 else (lane >= HEAD_DIM)


def masked(value, lanes):
    return jnp.where(lanes, value, jnp.zeros_like(value))


def fill_bias(window_ref, tiles, transposed):
    part = 1 if transposed else 0

    def one(h, carry):
        for d in range(3):
            row = jnp.broadcast_to(window_ref[h, pl.ds(part * 3 + d, 1), :], (TILE, 2 * TILE))
            rolled = pltpu.roll(row, TILE, 1, stride=1, stride_axis=0)
            tiles[h, d + 1] = rolled[:, :TILE]
        low = window_ref[h, pl.ds(0, 1), pl.ds(0, 1)]
        high = window_ref[h, pl.ds(2, 1), pl.ds(2 * TILE - 1, 1)]
        tiles[h, 0] = jnp.broadcast_to(low, (TILE, TILE))
        tiles[h, 4] = jnp.broadcast_to(high, (TILE, TILE))
        return carry

    lax.fori_loop(0, HEADS, one, 0)


def whole(space=pltpu.VMEM):
    return pl.BlockSpec(memory_space=space)


def call(body, name, ins, spaces, outs, out_spaces, scratch, us):
    return pl.pallas_call(
        body,
        name=name,
        in_specs=[whole(s) for s in spaces],
        out_specs=[whole(s) for s in out_spaces],
        out_shape=[jax.ShapeDtypeStruct(s, k) for s, k in outs],
        scratch_shapes=scratch,
        compiler_params=pltpu.CompilerParams(vmem_limit_bytes=VMEM_LIMIT),
        cost_estimate=pl.CostEstimate(flops=int(us * 1.1e9), bytes_accessed=int(us * 1e6), transcendentals=0),
    )(*ins)


VM, SM, ANY = pltpu.VMEM, pltpu.SMEM, pl.ANY


def plan_of(sets):
    return [part for part, ids, other in sets], [(ids, other) for part, ids, other in sets]


def enc_attention(meta, x, gains, segr, segc, windows, a_sets, b_sets):
    a_arrays, a_plan = plan_of(a_sets)
    b_arrays, b_plan = plan_of(b_sets)
    n = len(a_arrays)

    def body(meta, x, gains, segr, segc, windows, *rest):
        a_parts, b_parts, rest = rest[:n], rest[n : 2 * n], rest[2 * n :]
        n1, q, k, v, c, h1, n2, lse, w, tiles, lcol, sems = rest
        start_fetch(meta, a_parts, a_plan, [(0, GROUP, square_row(0))], w, sems.at[0])
        start_fetch(meta, b_parts, b_plan, [(0, GROUP, square_row(1))], w, sems.at[0])
        fill_bias(windows, tiles, False)
        xf = x[...].astype(F32)
        n1[...] = rms(xf, gains[0:1, :]).astype(BF)
        drain(w, sems.at[0])
        for ref, at in ((q, 0), (k, 2), (v, 3)):
            ref[...] = nn(n1[...], w[at * D : (at + 1) * D, :]).astype(BF)
        lane = lax.broadcasted_iota(jnp.int32, (1, TILE), 1)
        lcol[...] = jnp.zeros_like(lcol)

        def pair(pr, carry):
            cols = pl.ds(pl.multiple_of(pr * TILE, TILE), TILE)
            kp, vp = k[:, cols], v[:, cols]
            for ib in range(ROW_LEN // TILE):
                rows = slice(ib * TILE, (ib + 1) * TILE)
                same = segc[rows, :] == segr[...]
                qp = q[rows, cols]
                total = jnp.zeros((TILE, TILE), F32)
                for hh in range(2):
                    h = 2 * pr + hh
                    lanes = pair_lanes(hh)
                    bias = jnp.concatenate(
                        [tiles[h, min(max(jb - ib, -2), 2) + 2] for jb in range(ROW_LEN // TILE)], axis=1
                    )
                    s = jnp.where(same, nt(masked(qp, lanes), kp) + bias, MASKED)
                    top = jnp.max(s, axis=-1, keepdims=True)
                    ex = jnp.exp(s - top)
                    tot = jnp.sum(ex, axis=-1, keepdims=True)
                    p = (ex * (1.0 / tot)).astype(BF)
                    total = total + nn(p, masked(vp, lanes))
                    lcol[rows, :] = jnp.where(lane == h, top + jnp.log(tot), lcol[rows, :])
                c[rows, cols] = total.astype(BF)
            return carry

        lax.fori_loop(0, HEADS // 2, pair, 0)
        lse[...] = lcol[...].T
        res = x[...].astype(F32) + nn(c[...], w[D : 2 * D, :])
        h1[...] = res
        n2[...] = rms(res, gains[1:2, :]).astype(BF)

    rows = (ROW_LEN, D)
    return call(
        body, "enc_attention", [meta, x, gains, segr, segc, windows, *a_arrays, *b_arrays],
        [SM, VM, VM, VM, VM, VM] + [ANY] * (2 * n),
        [(rows, BF)] * 5 + [(rows, F32), (rows, BF), ((TILE, ROW_LEN), F32), ], [VM] * 8,
        [pltpu.VMEM((4 * D, D), BF), pltpu.VMEM((HEADS, 5, TILE, TILE), F32), pltpu.VMEM((ROW_LEN, TILE), F32), pltpu.SemaphoreType.DMA((2,))],
        us=20,
    )


def enc_ffn(meta, h1, n2, in_sets, back_sets):
    in_arrays, in_plan = plan_of(in_sets)
    back_arrays, back_plan = plan_of(back_sets)
    n = len(in_arrays)

    def body(meta, h1, n2, *rest):
        ins, backs, rest = rest[:n], rest[n : 2 * n], rest[2 * n :]
        f, slope, e, w_in, w_back, acc, sems = rest
        start_fetch(meta, ins, in_plan, in_items(0), w_in, sems)
        start_fetch(meta, backs, back_plan, back_items(0), w_back, sems.at[pl.ds(4, 4)])
        acc[...] = h1[...]

        def block(b, carry):
            rows = pl.ds(pl.multiple_of(b * D, D), D)

            drain(w_in.at[rows], sems.at[b])
            value, grad = gelu_both(nn(n2[...], w_in[rows, :]))
            fb = value.astype(BF)
            f[:, rows] = fb
            slope[:, rows] = grad.astype(BF)
            drain(w_back.at[rows], sems.at[4 + b])
            acc[...] += nn(fb, w_back[rows, :])
            return carry

        lax.fori_loop(0, FF // D, block, 0)
        e[...] = acc[...].astype(BF)

    return call(
        body, "enc_ffn", [meta, h1, n2, *in_arrays, *back_arrays], [SM, VM, VM] + [ANY] * (2 * n),
        [((ROW_LEN, FF), BF), ((ROW_LEN, FF), BF), ((ROW_LEN, D), BF)], [VM] * 3,
        [pltpu.VMEM((FF, D), BF), pltpu.VMEM((FF, D), BF), pltpu.VMEM((ROW_LEN, D), F32),
         pltpu.SemaphoreType.DMA((8,))],
        us=15,
    )


PART = (GROUPS // 2, GROUP, D)


def enc_hidden_grad(meta, de, slope, back_sets):
    arrays, plan = plan_of(back_sets)
    n = len(arrays)

    def body(meta, de, slope, *rest):
        parts, rest = rest[:n], rest[n:]
        du, other, w, sems = rest
        start_fetch(meta, parts, plan, back_items(0), w, sems)
        for b in range(FF // D):
            cols = slice(b * D, (b + 1) * D)
            drain(w.at[cols], sems.at[b])
            value = (slope[:, cols].astype(F32) * nt(de[...], w[cols, :])).astype(BF)
            du[:, cols] = value

            @pl.when(meta[1] != b // 2)
            def _():
                other[:, (b % 2) * D : (b % 2 + 1) * D] = value

    return call(
        body, "enc_hidden_grad", [meta, de, slope, *arrays], [SM, VM, VM] + [ANY] * n,
        [((ROW_LEN, FF), BF), ((ROW_LEN, FF // 2), BF)], [VM, VM],
        [pltpu.VMEM((FF, D), BF), pltpu.SemaphoreType.DMA((4,))],
        us=8,
    )


def enc_w_back_grad(meta, de, de_got, f, f_got):
    half = D // 2

    def body(meta, de, de_got, f, f_got, keep_a, send_a, keep_b, send_b, mine, buf, sems):
        mine[...] = de[:, pl.ds(pl.multiple_of(meta[1] * half, TILE), half)]
        for b in range(FF // D):
            cols = slice(b * D, (b + 1) * D)
            at = b % 2
            if b >= 2:
                drain(buf.at[at], sems.at[at])
            buf[at] = (tn(f[:, cols], mine[...]) + tn(f_got[:, cols], de_got[...])).astype(BF)
            for k in range(D // GROUP):
                group, piece = b * (D // GROUP // 4) + k // 4, k % 4
                keep, send = (keep_a, send_a) if piece < 2 else (keep_b, send_b)
                start_store(meta, buf.at[at, pl.ds(k * GROUP, GROUP)], group, piece // 2, keep, send, sems.at[at],
                            pl.ds((piece % 2) * half, half))
        drain(buf.at[0], sems.at[0])
        drain(buf.at[1], sems.at[1])

    return call(
        body, "enc_w_back_grad", [meta, de, de_got, f, f_got], [SM] + [VM] * 4,
        [(PART, BF)] * 4, [ANY] * 4,
        [pltpu.VMEM((ROW_LEN, half), BF), pltpu.VMEM((2, D, half), BF), pltpu.SemaphoreType.DMA((2,))],
        us=7,
    )


def enc_w_in_grad(meta, du, du_got, n2, n2_got):
    def body(meta, du, du_got, n2, n2_got, keep_a, send_a, keep_b, send_b, buf, sems):
        for b in range(2):
            cols = pl.ds(pl.multiple_of(meta[1] * (FF // 2) + b * D, TILE), D)
            buf[b] = (tn(n2[...], du[:, cols]) + tn(n2_got[...], du_got[:, b * D : (b + 1) * D])).astype(BF)
            keep, send = (keep_a, send_a) if b == 0 else (keep_b, send_b)
            for g in range(GROUPS):
                start_store(meta, buf.at[b, pl.ds(g * GROUP, GROUP)], g, b, keep, send, sems.at[b])
        drain(buf.at[0], sems.at[0])
        drain(buf.at[1], sems.at[1])

    return call(
        body, "enc_w_in_grad", [meta, du, du_got, n2, n2_got], [SM] + [VM] * 4,
        [(PART, BF)] * 4, [ANY] * 4,
        [pltpu.VMEM((2, D, D), BF), pltpu.SemaphoreType.DMA((2,))],
        us=7,
    )


def enc_ffn_back(meta, du, h1, de, gains, in_sets):
    arrays, plan = plan_of(in_sets)
    n = len(arrays)

    def body(meta, du, h1, de, gains, *rest):
        parts, rest = rest[:n], rest[n:]
        dh1, da, dgain, w, acc, sems = rest
        start_fetch(meta, parts, plan, in_items(0), w, sems)
        for k, b in enumerate((0, 2, 1, 3)):
            cols = slice(b * D, (b + 1) * D)
            drain(w.at[cols], sems.at[b])
            part = nt(du[:, cols], w[cols, :])
            acc[...] = part if k == 0 else acc[...] + part
        dv, dg = rms_back(h1[...], gains[1:2, :], acc[...])
        total = de[...].astype(F32) + dv
        dh1[...] = total
        da[...] = total.astype(BF)
        dgain[...] = dg

    rows = (ROW_LEN, D)
    return call(
        body, "enc_ffn_back", [meta, du, h1, de, gains, *arrays], [SM, VM, VM, VM, VM] + [ANY] * n,
        [(rows, F32), (rows, BF), ((1, D), F32)], [VM, VM, VM],
        [pltpu.VMEM((FF, D), BF), pltpu.VMEM(rows, F32), pltpu.SemaphoreType.DMA((4,))],
        us=8,
    )


def enc_attention_back(meta, da, q, k, v, lse, segr, segc, windows, sets):
    arrays, plan = plan_of(sets)
    n = len(arrays)
    wide = 2 * TILE

    def body(meta, da, q, k, v, lse, segr, segc, windows, *rest):
        parts, rest = rest[:n], rest[n:]
        dq, dk, dv, diag, other, w, dc, tiles, sums, kacc, vacc, sem = rest
        start_fetch(meta, parts, plan, [(0, GROUP, lambda core, g: GROUP * g)], w, sem, only=0)
        fill_bias(windows, tiles, True)
        drain(w, sem)
        dc[...] = nt(da[...], w[...]).astype(BF)
        row = lax.broadcasted_iota(jnp.int32, (TILE, TILE), 0)
        col = lax.broadcasted_iota(jnp.int32, (TILE, TILE), 1)
        flip = (row + col == TILE - 1).astype(F32)

        def pair(pr, carry):
            cols = pl.ds(pl.multiple_of(pr * TILE, TILE), TILE)
            for hh in range(2):
                h = 2 * pr + hh
                lanes = pair_lanes(hh)
                km, vm = masked(k[:, cols], lanes), masked(v[:, cols], lanes)
                sums[...] = jnp.zeros_like(sums)
                for ib in range(ROW_LEN // wide):
                    rows = slice(ib * wide, (ib + 1) * wide)
                    same = segc[...] == segr[:, rows]
                    qp, dcp = q[rows, cols], dc[rows, cols]
                    bias = jnp.concatenate([
                        jnp.concatenate([
                            tiles[h, min(max(jb - (2 * ib + i), -2), 2) + 2] for i in range(2)
                        ], axis=1) for jb in range(ROW_LEN // TILE)
                    ], axis=0)
                    s = jnp.where(same, nt(km, qp) + bias, MASKED)
                    prob = jnp.exp(s - lse[pl.ds(h, 1), rows])
                    dprob = nt(vm, dcp)
                    inner = jnp.sum(prob * dprob, axis=0, keepdims=True)
                    ds = (prob * (dprob - inner)).astype(BF)
                    dvp = nn(prob.astype(BF), masked(dcp, lanes))
                    dkp = nn(ds, masked(qp, lanes))
                    dqp = tn(ds, km)
                    if hh == 0 and ib == 0:
                        vacc[...], kacc[...] = dvp, dkp
                    else:
                        vacc[...] += dvp
                        kacc[...] += dkp
                    if hh == 0:
                        dq[rows, cols] = dqp.astype(BF)
                    else:
                        dq[rows, cols] = dq[rows, cols] + dqp.astype(BF)
                    for jb in range(ROW_LEN // TILE):
                        for i in range(2):
                            d = min(max(jb - (2 * ib + i), -2), 2) + 2
                            sums[d] += ds[jb * TILE : (jb + 1) * TILE, i * TILE : (i + 1) * TILE].astype(F32)
                for d in range(5):
                    if d in (0, 4):
                        line = jnp.sum(sums[d], axis=0, keepdims=True)
                        diag[h, d : d + 1, :] = jnp.concatenate([line, jnp.zeros_like(line)], axis=1)
                    else:
                        turned = lax.dot_general(
                            flip, sums[d], (((1,), (0,)), ((), ())),
                            precision=lax.Precision.HIGHEST, preferred_element_type=F32,
                        )
                        wider = jnp.concatenate([turned, jnp.zeros_like(turned)], axis=1)
                        rolled = pltpu.roll(wider, 1, 1, stride=1, stride_axis=0)
                        diag[h, d : d + 1, :] = jnp.sum(rolled, axis=0, keepdims=True)
            dk[:, cols] = kacc[...].astype(BF)
            dv[:, cols] = vacc[...].astype(BF)
            return carry

        lax.fori_loop(0, HEADS // 2, pair, 0)

        @pl.when(meta[1] == 0)
        def _():
            other[0] = dk[...]
            other[1] = dv[...]

        @pl.when(meta[1] != 0)
        def _():
            other[0] = dq[...]
            other[1] = da[...]

    rows = (ROW_LEN, D)
    return call(
        body, "enc_attention_back", [meta, da, q, k, v, lse, segr, segc, windows, *arrays],
        [SM] + [VM] * 8 + [ANY] * n,
        [(rows, BF), (rows, BF), (rows, BF), ((HEADS, 5, 2 * TILE), F32), ((2,) + rows, BF)], [VM] * 5,
        [pltpu.VMEM((D, D), BF), pltpu.VMEM(rows, BF), pltpu.VMEM((HEADS, 5, TILE, TILE), F32),
         pltpu.VMEM((5, TILE, TILE), F32), pltpu.VMEM((ROW_LEN, TILE), F32), pltpu.VMEM((ROW_LEN, TILE), F32),
         pltpu.SemaphoreType.DMA],
        us=25,
    )


def enc_square_grads(meta, n1, n1_got, c, c_got, dq, dk, dv, da, got):
    def body(meta, n1, n1_got, c, c_got, dq, dk, dv, da, got, keep_a, send_a, keep_b, send_b, buf, sems):
        for core, (one, left, left_got, two) in enumerate(((dq, c, c_got, da), (dk, n1, n1_got, dv))):

            @pl.when(meta[1] == core)
            def _():
                buf[0] = (tn(n1[...], one[...]) + tn(n1_got[...], got[0])).astype(BF)
                for g in range(GROUPS):
                    start_store(meta, buf.at[0, pl.ds(g * GROUP, GROUP)], g, 0, keep_a, send_a, sems.at[0])
                buf[1] = (tn(left[...], two[...]) + tn(left_got[...], got[1])).astype(BF)
                for g in range(GROUPS):
                    start_store(meta, buf.at[1, pl.ds(g * GROUP, GROUP)], g, 1, keep_b, send_b, sems.at[1])

        drain(buf.at[0], sems.at[0])
        drain(buf.at[1], sems.at[1])

    return call(
        body, "enc_square_grads", [meta, n1, n1_got, c, c_got, dq, dk, dv, da, got], [SM] + [VM] * 9,
        [(PART, BF)] * 4, [ANY] * 4,
        [pltpu.VMEM((2, D, D), BF), pltpu.SemaphoreType.DMA((2,))],
        us=6,
    )


def enc_input_grad(meta, dq, dk, dv, x, dh1, gains, a_sets, b_sets):
    a_arrays, a_plan = plan_of(a_sets)
    b_arrays, b_plan = plan_of(b_sets)
    n = len(a_arrays)

    def body(meta, dq, dk, dv, x, dh1, gains, *rest):
        a_parts, b_parts, rest = rest[:n], rest[n : 2 * n], rest[2 * n :]
        keep, send, dgain, w, sem = rest
        start_fetch(meta, a_parts, a_plan, [(0, GROUP, lambda core, g: core * D + GROUP * g)], w, sem)
        start_fetch(meta, b_parts, b_plan, [(0, GROUP, lambda core, g: 2 * D + GROUP * g)], w, sem, only=1)
        drain(w, sem)
        total = nt(dq[...], w[0:D, :]) + nt(dk[...], w[D : 2 * D, :]) + nt(dv[...], w[2 * D :, :])
        dx, dg = rms_back(x[...].astype(F32), gains[0:1, :], total)
        out = (dh1[...] + dx).astype(BF)
        dgain[...] = dg
        half = D // 2

        @pl.when(meta[1] == 0)
        def _():
            keep[...] = out[:, :half]
            send[...] = out[:, half:]

        @pl.when(meta[1] != 0)
        def _():
            keep[...] = out[:, half:]
            send[...] = out[:, :half]

    return call(
        body, "enc_input_grad", [meta, dq, dk, dv, x, dh1, gains, *a_arrays, *b_arrays],
        [SM] + [VM] * 6 + [ANY] * (2 * n),
        [((ROW_LEN, D // 2), BF), ((ROW_LEN, D // 2), BF), ((1, D), F32)], [VM] * 3,
        [pltpu.VMEM((3 * D, D), BF), pltpu.SemaphoreType.DMA],
        us=8,
    )


def spread_heads(value):
    return jnp.concatenate([masked(value, head_lanes(h)) for h in range(HEADS)], axis=0)


def join_heads(value):
    total = jnp.zeros((8, D), F32)
    for h in range(HEADS):
        total = total + masked(value[8 * h : 8 * h + 8, :], head_lanes(h))
    return total


def own_rows(meta):
    row = lax.broadcasted_iota(jnp.int32, (8, 1), 0)
    return (row >= 4 * meta[1]) & (row < 4 * meta[1] + 4)


def start_self(meta, own, got, dst, sem):
    half = D // 2
    pltpu.make_async_copy(own, dst.at[pl.ds(pl.multiple_of(meta[1] * half, 16), half)], sem).start()
    pltpu.make_async_copy(got, dst.at[pl.ds(pl.multiple_of((1 - meta[1]) * half, 16), half)], sem).start()


def dec_before(meta, z, d_out, gains, self_own, self_got, sets):
    arrays, plan = plan_of(sets)
    n = len(arrays)

    def body(meta, z, d_out, gains, self_own, self_got, *rest):
        parts, rest = rest[:n], rest[n:]
        m1, sv, z1, m2, qc, qk, gm, w_self, w, sems = rest
        start_self(meta, self_own, self_got, w_self, sems.at[0])
        start_fetch(meta, parts, plan, [(0, GROUP, lambda core, g: core * D + GROUP * g)], w, sems.at[1])
        zf = z[...].astype(F32)
        gm[...] = jnp.where(own_rows(meta), d_out[...].astype(F32), 0.0).astype(BF)
        m1v = rms(zf, gains[2:3, :]).astype(BF)
        drain(w_self, sems.at[0])
        drain(w, sems.at[1])
        svv = nn(m1v, w_self[:, :D]).astype(BF)
        z1v = zf + nn(svv, w_self[:, D:])
        m2v = rms(z1v, gains[0:1, :]).astype(BF)
        qcv = nn(m2v, w[0:D, :]).astype(BF)
        qk[...] = nt(spread_heads(qcv), w[D:, :]).astype(BF)
        m1[...], sv[...], z1[...], m2[...], qc[...] = m1v, svv, z1v, m2v, qcv

    rows = (8, D)
    return call(
        body, "dec_before", [meta, z, d_out, gains, self_own, self_got, *arrays],
        [SM, VM, VM, VM, ANY, ANY] + [ANY] * n,
        [(rows, BF), (rows, BF), (rows, F32), (rows, BF), (rows, BF), ((8 * HEADS, D), BF), (rows, BF)], [VM] * 7,
        [pltpu.VMEM((D, 2 * D), BF), pltpu.VMEM((2 * D, D), BF), pltpu.SemaphoreType.DMA((2,))],
        us=6,
    )


def dec_core(meta, e, segr, qk, qc, z1, g, gw, gains, sets, in_sets, in_sets_b):
    arrays, plan = plan_of(sets)
    in_arrays, in_plan = plan_of(in_sets)
    in_arrays_b, in_plan_b = plan_of(in_sets_b)
    n = len(arrays)

    def body(meta, e, segr, qk, qc, z1, g, gw, gains, *rest):
        parts, ins, ins_b, rest = rest[:n], rest[n : 2 * n], rest[2 * n : 3 * n], rest[3 * n :]
        de, cc, z2, m3, fc, duc, da2, dz2, dcc, edt, ebar, dgain, de_other, pairs_other, w, w_in, sems = rest
        start_fetch(meta, parts, plan, [(0, GROUP, lambda core, g: core * D + GROUP * g)], w, sems.at[0])
        start_fetch(meta, ins, in_plan, [(GROUP, GROUP, square_row(0))], w_in, sems.at[1])
        start_fetch(meta, ins_b, in_plan_b, [(GROUP, GROUP, square_row(1))], w_in, sems.at[1])
        pairs = lax.broadcasted_iota(jnp.int32, (8 * HEADS, 1), 0)
        owner = segr[...] == jnp.bitwise_and(pairs, 7) - 4 * meta[1]
        t = jnp.where(owner, nt(qk[...], e[...]), MASKED)
        ex = jnp.where(owner, jnp.exp(t - jnp.max(t, axis=-1, keepdims=True)), 0.0)
        tot = jnp.sum(ex, axis=-1, keepdims=True)
        prob = ex * (1.0 / jnp.where(tot > 0.0, tot, 1.0))
        pc = prob.astype(BF)
        ebv = nn(pc, e[...]).astype(BF)
        ebar[...] = ebv
        drain(w, sems.at[0])
        ccv = join_heads(nn(ebv, w[D:, :])).astype(BF)
        z2v = z1[...] + nn(ccv, w[0:D, :])
        m3v = rms(z2v, gains[1:2, :]).astype(BF)
        drain(w_in, sems.at[1])
        dm3 = jnp.zeros((8, D), F32)
        own = own_rows(meta)
        for b in range(FF // D):
            cols = slice(b * D, (b + 1) * D)
            value, slope = gelu_both(nn(m3v, w_in[cols, :]))
            fc[:, cols] = jnp.where(own, value, 0.0).astype(BF)
            ducv = jnp.where(own, slope * gw[:, cols].astype(F32), 0.0).astype(BF)
            duc[:, cols] = ducv
            dm3 = dm3 + nt(ducv, w_in[cols, :])
        back, dg = rms_back(z2v, gains[1:2, :], dm3)
        dz2v = g[...].astype(F32) + back
        da2v = dz2v.astype(BF)
        dccv = nt(da2v, w[0:D, :]).astype(BF)
        dvw = nt(spread_heads(dccv), w[D:, :]).astype(BF)
        dprob = nt(dvw, e[...])
        dt = (prob * (dprob - jnp.sum(prob * dprob, axis=-1, keepdims=True))).astype(BF)
        de[...] = tn(jnp.concatenate([pc, dt], axis=0), jnp.concatenate([dvw, qk[...]], axis=0)).astype(BF)
        edt[...] = nn(dt, e[...]).astype(BF)
        cc[...], m3[...], da2[...], dz2[...], dcc[...], dgain[...] = ccv, m3v, da2v, dz2v, dccv, dg
        z2[...] = jnp.where(own, z2v, 0.0)
        half = D // 2
        pairs_other[8 * HEADS + 8 :, :] = jnp.zeros((8, D), BF)

        @pl.when(meta[1] == 0)
        def _():
            de_other[...] = de[:, half:]
            pairs_other[: 8 * HEADS, :] = ebv
            pairs_other[8 * HEADS : 8 * HEADS + 8, :] = dccv

        @pl.when(meta[1] != 0)
        def _():
            de_other[...] = de[:, :half]
            pairs_other[: 8 * HEADS, :] = edt[...]
            pairs_other[8 * HEADS : 8 * HEADS + 8, :] = qc[...]

    rows, spread = (8, D), (8 * HEADS, D)
    return call(
        body, "dec_core", [meta, e, segr, qk, qc, z1, g, gw, gains, *arrays, *in_arrays, *in_arrays_b],
        [SM] + [VM] * 8 + [ANY] * (3 * n),
        [((ROW_LEN, D), BF), (rows, BF), (rows, F32), (rows, BF), ((8, FF), BF), ((8, FF), BF), (rows, BF),
         (rows, F32), (rows, BF), (spread, BF), (spread, BF), ((1, D), F32),
         ((ROW_LEN, D // 2), BF), ((8 * HEADS + 16, D), BF)], [VM] * 14,
        [pltpu.VMEM((2 * D, D), BF), pltpu.VMEM((FF, D), BF), pltpu.SemaphoreType.DMA((2,))],
        us=10,
    )


def dec_after(meta, z, z1, dz2, qc, dcc, edt, ebar, got, gains, self_own, self_got, sets):
    arrays, plan = plan_of(sets)
    n = len(arrays)

    def body(meta, z, z1, dz2, qc, dcc, edt, ebar, got, gains, self_own, self_got, *rest):
        parts, rest = rest[:n], rest[n:]
        dqc, ds1, dsv, dec_grad, dg_attn, dg_self, keep, send, w_self, w, buf, sems = rest
        start_fetch(meta, parts, plan, [(0, GROUP, lambda core, g: core * D + GROUP * g)], w, sems.at[1])
        start_self(meta, self_own, self_got, w_self, sems.at[0])
        zero = meta[1] == 0
        left = jnp.concatenate([jnp.where(zero, edt[...], ebar[...]), got[: 8 * HEADS, :]], axis=0)
        right = jnp.where(zero, qc[...], dcc[...])
        right = jnp.concatenate([spread_heads(right), spread_heads(got[8 * HEADS : 8 * HEADS + 8, :])], axis=0)
        buf[...] = tn(left, right).astype(BF)
        for grp in range(GROUPS):
            start_store(meta, buf.at[pl.ds(grp * GROUP, GROUP)], grp, 0, keep, send, sems.at[3])
        drain(w, sems.at[1])
        dqv = join_heads(nn(edt[...], w[D:, :])).astype(BF)
        back, dg = rms_back(z1[...], gains[0:1, :], nt(dqv, w[0:D, :]))
        dz1 = dz2[...] + back
        ds1v = dz1.astype(BF)
        drain(w_self, sems.at[0])
        dsvv = nt(ds1v, w_self[:, D:]).astype(BF)
        back0, dg0 = rms_back(z[...].astype(F32), gains[2:3, :], nt(dsvv, w_self[:, :D]))
        own = own_rows(meta)
        dec_grad[...] = jnp.where(own, dz1 + back0, 0.0).astype(BF)
        dqc[...], ds1[...], dsv[...], dg_attn[...], dg_self[...] = dqv, ds1v, dsvv, dg, dg0
        drain(buf, sems.at[3])

    rows = (8, D)
    return call(
        body, "dec_after",
        [meta, z, z1, dz2, qc, dcc, edt, ebar, got, gains, self_own, self_got, *arrays],
        [SM] + [VM] * 9 + [ANY] * (2 + n),
        [(rows, BF)] * 4 + [((1, D), F32)] * 2 + [(PART, BF)] * 2, [VM] * 6 + [ANY] * 2,
        [pltpu.VMEM((D, 2 * D), BF), pltpu.VMEM((2 * D, D), BF), pltpu.VMEM((D, D), BF),
         pltpu.SemaphoreType.DMA((4,))],
        us=6,
    )


def dec_weight_grads(place, left, right, g_all, w_back, rows, self_rows):
    def body(place, left, right, g_all, w_back, dec_q, dec_o, dec_i, dec_b, self_v, self_o, y):
        half = left.shape[1]
        chip, core = place[0], place[1]
        chips = D // rows

        def cut(at, width):
            parts = []
            while width:
                ref, first = (left, at) if at < half else (right, at - half)
                count = min(width, half - first)
                parts.append(ref[:, first : first + count])
                at, width = at + count, width - count
            return parts[0] if len(parts) == 1 else jnp.concatenate(parts, axis=1)

        def picked(at, first, count, width=D):
            row = lax.broadcasted_iota(jnp.int32, (count, width), 0) + first
            col = lax.broadcasted_iota(jnp.int32, (count, width), 1)
            return nt((row == col).astype(F32).astype(BF), cut(at * D, width)).astype(BF)

        first, first_self = chip * rows, (core * chips + chip) * self_rows
        m1, sv, m2, cc, m3, da2, dqc, ds1, dsv, duc, fc = list(range(10)) + [13]
        dec_q[...] = nn(picked(m2, first, rows), cut(dqc * D, D))
        dec_o[...] = nn(picked(cc, first, rows), cut(da2 * D, D))
        dec_i[...] = nn(picked(m3, first, rows), cut(duc * D, FF))
        self_v[...] = nn(picked(m1, first_self, self_rows), cut(dsv * D, D))
        self_o[...] = nn(picked(sv, first_self, self_rows), cut(ds1 * D, D))
        hidden = picked(fc, 4 * first, 4 * rows, FF)
        dec_b[...] = nn(hidden, g_all[...])
        y[...] = tn(hidden, w_back[...]).astype(BF)

    return call(
        body, "dec_weight_grads", [place, left, right, g_all, w_back], [SM, VM, VM, VM, VM],
        [((rows, D), F32), ((rows, D), F32), ((rows, FF), F32), ((4 * rows, D), F32), ((self_rows, D), F32),
         ((self_rows, D), F32), (g_all.shape, BF)], [VM] * 7,
        [], us=5,
    )


def pieces(w_query, w_key, w_value, w_out, w_in, w_back):
    ins = [w_in[:, b * D : (b + 1) * D] for b in range(4)]
    backs = [w_back[b * GROUP : (b + 1) * GROUP] for b in range(4)]
    return jnp.stack([
        jnp.concatenate([w_query, w_out] + ins[:2] + backs[:2]), jnp.concatenate([w_key, w_value] + ins[2:] + backs[2:])
    ])


def per_device(
    enc_in, dec_in, segment, d_out, attn_gain, w_query, w_key, w_value, w_out, ffn_gain, w_in, w_back,
    self_gain, self_value, self_out, rel_table,
):
    core, chip = lax.axis_index("section"), lax.axis_index("dp")
    chips = lax.axis_size("dp")
    rows = w_query.shape[1]
    first = core == 0
    pre = low_bits(rows)
    meta = jnp.stack([chip >> pre, core]).astype(jnp.int32)
    self_rows = self_value.shape[0]
    at_self = (core * chips + chip) * self_rows

    small = jnp.zeros((8, D), BF)
    small = lax.dynamic_update_slice(small, jnp.concatenate([attn_gain, ffn_gain]), (0, chip * rows))
    small = lax.dynamic_update_slice(small, self_gain[None], (2, at_self))
    small = jnp.concatenate([jnp.concatenate([self_value, self_out], axis=1), jnp.concatenate([d_out, small], axis=1)])
    small = lax.all_gather(small, "dp")

    both = pieces(*[filled(w[0], pre, chip, 0) for w in (w_query, w_key, w_value, w_out, w_in, w_back)])
    kept = lax.dynamic_index_in_dim(both, core, 0, False)
    got = across(lax.dynamic_index_in_dim(both, 1 - core, 0, False))
    enc_piece, dec_piece = jnp.where(first, kept, got), jnp.where(first, got, kept)

    def block(piece, *numbers):
        return jnp.concatenate([piece[k * GROUP : (k + 1) * GROUP] for k in numbers])

    sq, wide = Chain(enc_piece[: 2 * GROUP], pre), Chain(enc_piece[2 * GROUP :], pre)
    dec = Chain(block(dec_piece, 0, 2, 1, 3), pre)

    windows = jnp.einsum(
        "adtb,bh->hadt", window_onehots(), rel_table, precision=lax.Precision.HIGHEST
    ).reshape(HEADS, 6, 2 * TILE)
    x = lax.dynamic_index_in_dim(enc_in, core, 0, False)
    seg = lax.dynamic_index_in_dim(segment, core, 0, False)
    segr, segc = seg[None, :], seg[:, None]

    sq.step(Z1)
    done = sq.step(Z0)
    sa, sb = sq.split(GROUP)
    gate_chains(done, sa, sb, wide)
    done = sa.step(X) + sb.step(Y) + wide.step(Z1)
    gate_chains(done, sa, sb, wide)
    done = sa.last(Y) + sb.last(X) + wide.step(Z0) + sa.cross() + sb.cross()
    wa, wb = wide.split(2 * GROUP)
    gate_chains(done, wa, wb, dec)
    done = wa.step(X) + wb.step(Y) + dec.step(Z1) + sa.cross_last() + sb.cross_last()
    wa.held, wb.held, dec.held, x = gate(done, wa.held, wb.held, dec.held, x)

    g_all = small[:, self_rows:, :D].reshape(8 * chips, D)
    gw = lax.all_gather(nt(w_back[0], g_all), "dp").reshape(FF, 8 * chips)
    gw = lax.dynamic_slice_in_dim(gw, 8 * chip, 8, 1).T
    gw_got = across(gw)
    gw = jnp.where(first, gw_got, gw)
    self_own = small[:, :self_rows].reshape(chips * self_rows, 2 * D)
    gains_own = jnp.sum(small[:, self_rows:, D:].astype(F32), axis=0)
    self_got, gains_got = across(self_own), across(gains_own)
    gains0, gains1 = jnp.where(first, gains_own, gains_got), jnp.where(first, gains_got, gains_own)
    gains1 = jnp.where(jnp.arange(8)[:, None] == 2, gains0 + gains1, gains1)

    n1, q, k, v, c, h1, n2, lse = enc_attention(meta, x, gains0, segr, segc, windows, sa.sets(), sb.sets())
    done = wa.last(Y) + wb.last(X) + dec.step(Z0) + wa.cross() + wb.cross() + [h1]
    da_, db_ = dec.split(2 * GROUP)
    da_.held, db_.held, wa.last_got, wb.last_got, n1, c, n2 = gate(
        done, da_.held, db_.held, wa.last_got, wb.last_got, n1, c, n2
    )
    n1_got, c_got, n2_got = across(n1), across(c), across(n2)
    done = da_.step(X) + db_.step(Y) + wa.cross_last() + wb.cross_last() + [n1_got, c_got, n2_got]
    da_.held, db_.held, h1 = gate(done, da_.held, db_.held, h1)
    f, slope, e = enc_ffn(meta, h1, n2, wa.sets(), wb.sets())
    done = da_.last(Y) + db_.last(X) + da_.cross() + db_.cross() + [e, gw]
    da_.last_got, db_.last_got = gate(done, da_.last_got, db_.last_got)
    f_got = across(f)
    z = gate(da_.cross_last() + db_.cross_last(), dec_in)
    d1a, d1b = da_.sets(), db_.sets()
    m1, sv, z1, m2, qc, qk, gm = dec_before(meta, z, d_out, gains1, self_own, self_got, d1a)
    de, cc, z2, m3, fc, duc, da2, dz2, dcc, edt, ebar, dg_ffn1, de_other, pairs_other = dec_core(
        meta, e, segr, qk, qc, z1, gm, gw, gains1, d1b, d1a, d1b
    )

    def two(parts):
        return Sum(parts[0], parts[1], pre), Sum(parts[2], parts[3], pre)

    de_got, pairs_got = across(de_other), across(pairs_other)
    du, du_other = enc_hidden_grad(meta, de, slope, wb.sets())
    de_got, pairs_got, du_other = gate([de_got, pairs_got, du], de_got, pairs_got, du_other)
    du_got = across(du_other)
    back_a, back_b = two(enc_w_back_grad(meta, de, de_got, f, f_got))
    edt, back_a.send, back_b.send = gate([back_a.mine], edt, back_a.send, back_b.send)
    done = back_a.step(Y) + back_b.step(X)
    dqc, ds1, dsv, dec_grad, dg_attn1, dg_self, k_keep, k_send = dec_after(
        meta, dec_in, z1, dz2, qc, dcc, edt, ebar, pairs_got, gains1, self_own, self_got, d1a
    )
    h1, dqc = gate([dqc], h1, dqc)
    acts = jnp.concatenate([m1, sv, m2, cc, m3, da2, dqc, ds1, dsv, duc, fc], axis=1)
    width = acts.shape[1] // 2
    acts_got = across(lax.dynamic_slice_in_dim(acts, (1 - core) * width, width, 1))
    own = (jnp.arange(8)[:, None] // 4) == core
    acts = jnp.where(own, lax.dynamic_slice_in_dim(acts, core * width, width, 1), acts_got)
    acts = lax.all_gather(acts, "dp").reshape(8 * chips, width)
    dh1, da, dg_ffn0 = enc_ffn_back(meta, du, h1, de, gains0, wa.sets())
    n2, back_a.mine, back_b.mine = gate(done + [da, du_got], n2, back_a.mine, back_b.mine)
    done = back_a.step(X) + back_b.step(Y)
    in_a, in_b = two(enc_w_in_grad(meta, du, du_got, n2, n2_got))
    in_a.mine, in_a.send = jnp.concatenate([in_a.mine, k_keep], axis=1), jnp.concatenate([in_a.send, k_send], axis=1)
    da, in_a.send, in_b.send = gate([in_a.mine], da, in_a.send, in_b.send)
    done += in_a.step(Y) + in_b.step(X)
    dq, dk, dv, diag, other = enc_attention_back(meta, da, q, k, v, lse, segr, segc, windows, sb.sets())
    backs = merged([back_a, back_b])
    dq, other, in_a.mine, in_b.mine, backs.mine = gate(done + [dq], dq, other, in_a.mine, in_b.mine, backs.mine)
    got = across(other)
    done = in_a.step(X) + in_b.step(Y) + backs.step(Z0)
    keep, send, dg_attn0 = enc_input_grad(meta, dq, dk, dv, x, dh1, gains0, sa.sets(), sb.sets())
    dq, got = gate([got, dg_attn0], dq, got)
    square_a, square_b = two(enc_square_grads(meta, n1, n1_got, c, c_got, dq, dk, dv, da, got))
    ins = merged([in_a, in_b])
    acts, send, z2, ins.mine, backs.mine, square_a.send, square_b.send = gate(
        done + [square_a.mine], acts, send, z2, ins.mine, backs.mine, square_a.send, square_b.send
    )
    done = square_a.step(Y) + square_b.step(X) + ins.step(Z0) + backs.step(Z1)

    theirs = across(acts)
    dec_q, dec_o, dec_i, dec_b, g_self_value, g_self_out, y = dec_weight_grads(
        jnp.stack([chip, core]), jnp.where(first, acts, theirs), jnp.where(first, theirs, acts),
        g_all, w_back[0], rows, self_rows,
    )
    z2 = z2 + across(z2)
    square_a.mine, square_b.mine, ins.mine, y = gate(done + [dec_q], square_a.mine, square_b.mine, ins.mine, y)
    done = square_a.step(X) + square_b.step(Y) + ins.step(Z1)
    squares = merged([square_a, square_b])
    squares.mine = gate(done, squares.mine)
    done = squares.step(Z0)
    y = jnp.sum(lax.all_to_all(y.reshape(chips, 8, D), "dp", 0, 0).astype(F32), axis=0)
    squares.mine = gate(done, squares.mine)
    squares.step(Z1)
    backs_sum, ins_sum, square_sum = backs.total(), ins.total(), squares.total()
    dec_out = (z2 + y).astype(BF)
    dec_out = jnp.where(first, across(dec_out), dec_out)
    mine = chip * rows

    table = jnp.einsum("hdt,dtb->bh", diag, diagonal_onehots(), precision=lax.Precision.HIGHEST)
    little = jnp.concatenate([
        dg_attn0, dg_ffn0, dg_attn1, dg_ffn1, dg_self,
        jnp.pad(table.reshape(1, -1), ((0, 0), (0, D - BUCKETS * HEADS))), jnp.zeros((18, D), F32),
    ])
    little = jnp.sum(gate(done, lax.all_gather(little + across(little), "dp")), axis=0)
    g_rel_table = little[5, : BUCKETS * HEADS].reshape(BUCKETS, HEADS)

    def cut(index, at, count):
        return lax.dynamic_slice_in_dim(little[index], at, count, 0)

    g_attn_gain = cut(jnp.where(first, 0, 2), mine, rows)[None]
    g_ffn_gain = cut(jnp.where(first, 1, 3), mine, rows)[None]
    g_self_gain = cut(4, at_self, self_rows)

    backs_got, ins_got, square_got = [across(v.astype(BF)).astype(F32) for v in (backs_sum, ins_sum, square_sum)]

    def group(value, index):
        return value[index * GROUP : (index + 1) * GROUP]

    def placed(enc_value, dec_value):
        return jnp.where(first, narrowed(enc_value, pre, chip), dec_value)[None]

    g_w_query = placed(group(square_sum, 0), dec_q)
    g_w_out = placed(group(square_sum, 1), dec_o)
    g_w_key = narrowed(jnp.where(first, group(square_got, 0), group(ins_got, 1)), pre, chip)[None]
    g_w_value = narrowed(jnp.where(first, group(square_got, 1), group(ins_sum, 1)), pre, chip)[None]
    g_w_in = placed(
        jnp.concatenate([group(ins_sum, 0), group(ins_sum, 2), group(ins_got, 0), group(ins_got, 2)], axis=1), dec_i
    )
    half = D // 2
    tall = [
        jnp.concatenate([group(v, i)[:, j * half : (j + 1) * half] for i in range(2) for j in range(2)])
        for v in (backs_sum, backs_got)
    ]
    g_w_back = placed(jnp.concatenate(tall, axis=1), dec_b)

    other_half = across(send)
    enc_in_grad = jnp.where(first, jnp.stack([keep, other_half]), jnp.stack([other_half, keep]))
    dec_grad = dec_grad + across(dec_grad)
    half = D // 2
    dec_out = jnp.where(first, dec_out[:, :half], dec_out[:, half:])
    dec_in_grad = jnp.where(first, dec_grad[:, :half], dec_grad[:, half:])
    return (
        dec_out, enc_in_grad, dec_in_grad, g_attn_gain, g_w_query, g_w_key, g_w_value, g_w_out, g_ffn_gain,
        g_w_in, g_w_back, g_self_gain, g_self_value, g_self_out, g_rel_table,
    )


def solution(mesh):
    return jax.shard_map(
        per_device,
        mesh=mesh,
        in_specs=(
            P("dp", None, None),
            P("dp", None),
            P("dp", None),
            P("dp", None),
            P("section", "dp"),
            P("section", "dp", None),
            P("section", "dp", None),
            P("section", "dp", None),
            P("section", "dp", None),
            P("section", "dp"),
            P("section", "dp", None),
            P("section", "dp", None),
            P(("section", "dp")),
            P(("section", "dp"), None),
            P(("section", "dp"), None),
            P(),
        ),
        out_specs=(
            P("dp", "section"),
            P("dp", None, "section"),
            P("dp", "section"),
            P("section", "dp"),
            P("section", "dp", None),
            P("section", "dp", None),
            P("section", "dp", None),
            P("section", "dp", None),
            P("section", "dp"),
            P("section", "dp", None),
            P("section", "dp", None),
            P(("section", "dp")),
            P(("section", "dp"), None),
            P(("section", "dp"), None),
            P(),
        ),
        check_vma=False,
    )
```

time: 611 us -> 444 us (0.73)
  waiting for transfers between devices: 332 us -> 161 us
  starting transfers between devices: 77.2 us -> 59 us
  between operations: 2.54 us -> 15.6 us
  other arithmetic: 24.9 us -> 36.3 us
    ppermute x62 -> x36, waiting for transfers between devices: 330 us -> 152 us  [along(): return lax.ppermute(value, 'dp', [(i, i ^ 1 << bit) for i in range(count)])]
    ppermute x62 -> x36, starting transfers between devices: 69 us -> 47.6 us  [along(): return lax.ppermute(value, 'dp', [(i, i ^ 1 << bit) for i in range(count)])]
    concatenate x21 -> x16, other arithmetic: 0.8 us -> 8.99 us  [the longest x10 7.07 us: step(): self.held = jnp.concatenate([self.held, got], axis=0)]
    ppermute x40 -> x34, waiting for transfers between devices: 1.52 us -> 8.96 us  [across(): return lax.ppermute(value, 'section', [(0, 1), (1, 0)])]
    pallas_call x11 -> x13, Pallas kernels: 133 us -> 136 us  [call(): pl.pallas_call(body, name=name, in_specs=[whole(s) for s in spaces], out_...]
    convert_element_type x16 -> x12, other arithmetic: 12.5 us -> 9.03 us  [added(): return (left.astype(F32) + right.astype(F32)).astype(kind)]
    unnamed x146 -> x148, local copies, waits for them, and re-layouts: 16.2 us -> 16.1 us
  transfers between devices with their start and end apart: 102 -> 75, of which waited for: 52 -> 31; matrix products, arithmetic and copies ran while one was open for 7% -> 12% of each run, Pallas kernels for 9% -> 31%
where the time goes in v2:
time: 444 us; the launch traced here: 438 us
  waiting for transfers between devices  161 us (36%)
  Pallas kernels  136 us (31%)
  starting transfers between devices  59 us (13%)
  other arithmetic  36.3 us (8%)
  local copies, waits for them, and re-layouts  26.7 us (6%)
  between operations  15.6 us (4%)
    ppermute x36, waiting for transfers between devices, along(): return lax.ppermute(value, 'dp', [(i, i ^ 1 << bit) for i in range(count)])  152 us
    pallas_call x13, Pallas kernels, call(): pl.pallas_call(body, name=name, in_specs=[whole(s) for s in spaces], out_...  136 us
    ppermute x36, starting transfers between devices, along(): return lax.ppermute(value, 'dp', [(i, i ^ 1 << bit) for i in range(count)])  47.6 us
    unnamed x148, local copies, waits for them, and re-layouts  16.1 us
    convert_element_type x12, other arithmetic, added(): return (left.astype(F32) + right.astype(F32)).astype(kind)  9.03 us
    ppermute x34, waiting for transfers between devices, across(): return lax.ppermute(value, 'section', [(0, 1), (1, 0)])  8.96 us
  transfers between devices with their start and end apart: 75, of which 31 were waited for; matrix products, arithmetic and copies ran while one was open for 12% of the time, Pallas kernels for 31%

profile of v2, /device:TPU:0, one launch (start us, length us, event | category | flops | bytes accessed | tf_op | source)
XLA Modules:
  0.0 438.3 jit_solution(11927336539888537980)
XLA Ops:
  15.5 4.0 collective-permute-start.1
  20.1 6.8 %collective-permute-done.1 = bf16[1,96,768]{2,1,0:T(8,128)(2,1)S(1)} collective-permute-done((bf16[1,96,768]{2,1,0:T(8,128)(2,1)S(1)}, bf16[1,96,768]{2,1,0:T(8,128)(2,1)S(1)}, u32[]{:S(2)}, u32[]{:S(2)}) %collective-permute-start.1) | collective-permute-done | bytes 147488 | tf_op jit(solution)/shard_map/ppermute | solution.py:67
  28.4 7.2 %collective-permute-done.2 = bf16[2,96,768]{2,1,0:T(8,128)(2,1)} collective-permute-done((bf16[2,96,768]{2,1,0:T(8,128)(2,1)S(1)}, bf16[2,96,768]{2,1,0:T(8,128)(2,1)}, u32[]{:S(2)}, u32[]{:S(2)}) %collective-permute-start.2) | collective-permute-done | bytes 294944 | tf_op jit(solution)/shard_map/ppermute | solution.py:67
  39.5 3.0 collective-permute-start.5
  42.5 2.6 collective-permute-done.3
  45.8 11.1 %collective-permute-done.5 = bf16[1,192,768]{2,1,0:T(8,128)(2,1)S(1)} collective-permute-done((bf16[1,192,768]{2,1,0:T(8,128)(2,1)S(1)}, bf16[1,192,768]{2,1,0:T(8,128)(2,1)S(1)}, u32[]{:S(2)}, u32[]{:S(2)}) %collective-permute-start.5) | collective-permute-done | bytes 294944 | tf_op jit(solution)/shard_map/ppermute | solution.py:67
  59.1 16.4 %collective-permute-done.6 = bf16[2,192,768]{2,1,0:T(8,128)(2,1)S(1)} collective-permute-done((bf16[2,192,768]{2,1,0:T(8,128)(2,1)S(1)}, bf16[2,192,768]{2,1,0:T(8,128)(2,1)S(1)}, u32[]{:S(2)}, u32[]{:S(2)}) %collective-permute-start.6) | collective-permute-done | bytes 589856 | tf_op jit(solution)/shard_map/ppermute | solution.py:67
  78.1 3.4 collective-permute-start.13
  85.8 17.0 %collective-permute-done.13 = bf16[1,192,768]{2,1,0:T(8,128)(2,1)S(1)} collective-permute-done((bf16[1,192,768]{2,1,0:T(8,128)(2,1)S(1)}, bf16[1,192,768]{2,1,0:T(8,128)(2,1)S(1)}, u32[]{:S(2)}, u32[]{:S(2)}) %collective-permute-start.13) | collective-permute-done | bytes 294944 | tf_op jit(solution)/shard_map/ppermute | solution.py:67
  102.8 2.2 pad_maximum_fusion.rest_0_
  105.0 2.3 pad_maximum_fusion.1.rest_4_.rest_0_
  111.1 1.8 convolution_bitcast_fusion
  114.2 6.8 %collective-permute-done.16 = bf16[2,192,768]{2,1,0:T(8,128)(2,1)S(1)} collective-permute-done((bf16[2,192,768]{2,1,0:T(8,128)(2,1)S(1)}, bf16[2,192,768]{2,1,0:T(8,128)(2,1)S(1)}, u32[]{:S(2)}, u32[]{:S(2)}) %collective-permute-start.16) | collective-permute-done | bytes 589856 | tf_op jit(solution)/shard_map/ppermute | solution.py:67
  122.9 20.3 %enc_attention.1 = (bf16[512,768]{1,0:T(8,128)(2,1)}, bf16[512,768]{1,0:T(8,128)(2,1)}, bf16[512,768]{1,0:T(8,128)(2,1)}, bf16[512,768]{1,0:T(8,128)(2,1)}, bf16...) custom-call(s32[2]{0:T(128)} %pad_add_fusion.meta, ...), custom_call_target="tpu_custom_call" | custom-call | flops 22000001024 | bytes 20000000 | tf_op jit(solution)/shard_map/enc_attention/pallas_call | solution.py:305
  143.3 3.6 collective-permute-start.23
  147.5 14.6 %collective-permute-done.22 = bf16[4,96,768]{2,1,0:T(8,128)(2,1)S(1)} collective-permute-done((bf16[4,96,768]{2,1,0:T(8,128)(2,1)S(1)}, bf16[4,96,768]{2,1,0:T(8,128)(2,1)S(1)}, u32[]{:S(2)}, u32[]{:S(2)}) %collective-permute-start.22) | collective-permute-done | bytes 589856 | tf_op jit(solution)/shard_map/ppermute | solution.py:67
  162.1 3.3 collective-permute-done.23
  169.3 2.4 collective-permute-start.29
  171.9 1.9 constant_dynamic-slice_fusion.2
  174.2 15.9 %enc_ffn.1 = (bf16[512,3072]{1,0:T(8,128)(2,1)}, bf16[512,3072]{1,0:T(8,128)(2,1)}, bf16[512,768]{1,0:T(8,128)(2,1)}) custom-call(s32[2]{0:T(128)} %pad_add_fusion.meta, f32[512,768]{1,0:T(8,128)} %get-tuple-element.212.h1, bf16[512,768]{1,0:T(8,128)(2,1)} %get-tuple-element.218.n2, bf16[8,96,768]{2,1,0:T(8,128)(2,1)} %pad_maximum_fusion.rest_0_, ...), custom_call_target="tpu_custom_call" | custom-call | flops 16499999744 | bytes 15000000 | tf_op jit(solution)/shard_map/enc_ffn/pallas_call | solution.py:305
  190.8 6.7 %collective-permute-done.30.rest_1_.rest_9_ = bf16[8,96,768]{2,1,0:T(8,128)(2,1)} collective-permute-done((bf16[8,96,768]{2,1,0:T(8,128)(2,1)}, bf16[8,96,768]{2,1,0:T(8,128)(2,1)}, u32[]{:S(2)}, u32[]{:S(2)}) %collective-permute-start.30) | collective-permute-done | bytes 1179680 | tf_op jit(solution)/shard_map/ppermute | solution.py:67
  201.4 3.4 collective-permute-done.34.rest_3_.rest_7_
  204.8 5.1 %dec_before.1 = (bf16[8,768]{1,0:T(8,128)(2,1)}, bf16[8,768]{1,0:T(8,128)(2,1)}, f32[8,768]{1,0:T(8,128)}, bf16[8,768]{1,0:T(8,128)(2,1)}, bf16[8,768]{1,0:T(8,1...) custom-call(s32[2]{0:T(128)} %pad_add_fusion.meta, bf16[8,768]{1,0:T(8,128)(2,1)} %z.2, bf16[8,768]{1,0:T(8,128)(2,1)} %d_out.1, ...), custom_call_target="tpu_custom_call" | custom-call | flops 6600000000 | bytes 6000000 | tf_op jit(solution)/shard_map/dec_before/pallas_call | solution.py:305
  209.9 9.7 %dec_core.1 = (bf16[512,768]{1,0:T(8,128)(2,1)}, bf16[8,768]{1,0:T(8,128)(2,1)}, f32[8,768]{1,0:T(8,128)}, bf16[8,768]{1,0:T(8,128)(2,1)}, bf16[8,3072]{1,0:T(8,...) custom-call(s32[2]{0:T(128)} %pad_add_fusion.meta, ...), custom_call_target="tpu_custom_call" | custom-call | flops 11000000512 | bytes 10000000 | tf_op jit(solution)/shard_map/dec_core/pallas_call | solution.py:305
  220.3 10.9 %enc_hidden_grad.1 = (bf16[512,3072]{1,0:T(8,128)(2,1)}, bf16[512,1536]{1,0:T(8,128)(2,1)}) custom-call(s32[2]{0:T(128)} %pad_add_fusion.meta, bf16[512,768]{1,0:T(8,128)(2,1)} %get-tuple-element.192.de, bf16[512,3072]{1,0:T(8,128)(2,1)} %get-tuple-element.195.slope, bf16[8,96,768]{2,1,0:T(8,128)(2,1)} %pad_maximum_fusion.1.rest_4_.rest_0_, ...), custom_call_target="tpu_custom_call" | custom-call | flops 8800000000 | bytes 8000000 | tf_op jit(solution)/shard_map/enc_hidden_grad/pallas_call | solution.py:305
  232.1 8.1 %enc_w_back_grad.1 = (bf16[8,48,768]{2,1,0:T(8,128)(2,1)}, bf16[8,48,768]{2,1,0:T(8,128)(2,1)}, bf16[8,48,768]{2,1,0:T(8,128)(2,1)}, bf16[8,48,768]{2,1,0:T(8,128)(2,1)}) custom-call(s32[2]{0:T(128)} %pad_add_fusion.meta, bf16[512,768]{1,0:T(8,128)(2,1)} %get-tuple-element.192.de, bf16[512,384]{1,0:T(8,128)(2,1)} %copy-done.58, ...), custom_call_target="tpu_custom_call" | custom-call | flops 7699999744 | bytes 7000000 | tf_op jit(solution)/shard_map/enc_w_back_grad/pallas_call | solution.py:305
  240.3 5.7 %dec_after.1 = (bf16[8,768]{1,0:T(8,128)(2,1)}, bf16[8,768]{1,0:T(8,128)(2,1)}, bf16[8,768]{1,0:T(8,128)(2,1)}, bf16[8,768]{1,0:T(8,128)(2,1)}, f32[1,768]{1,0:T...) custom-call(s32[2]{0:T(128)} %pad_add_fusion.meta, bf16[8,768]{1,0:T(8,128)(2,1)} %z.2, ...), custom_call_target="tpu_custom_call" | custom-call | flops 6600000000 | bytes 6000000 | tf_op jit(solution)/shard_map/dec_after/pallas_call | solution.py:305
  248.8 1.7 collective-permute-start.42
  250.6 2.0 collective-permute-start.43
  252.6 10.0 %enc_ffn_back.1 = (f32[512,768]{1,0:T(8,128)}, bf16[512,768]{1,0:T(8,128)(2,1)}, f32[1,768]{1,0:T(1,128)}) custom-call(s32[2]{0:T(128)} %pad_add_fusion.meta, bf16[512,3072]{1,0:T(8,128)(2,1)} %get-tuple-element.197.du, f32[512,768]{1,0:T(8,128)} %get-tuple-element.212.h1, bf16[512,768]{1,0:T(8,128)(2,1)} %get-tuple-element.192.de, ...), custom_call_target="tpu_custom_call" | custom-call | flops 8800000000 | bytes 8000000 | tf_op jit(solution)/shard_map/enc_ffn_back/pallas_call | solution.py:305
  266.8 1.7 collective-permute-start.44
  269.9 6.6 %enc_w_in_grad.1 = (bf16[8,48,768]{2,1,0:T(8,128)(2,1)}, bf16[8,48,768]{2,1,0:T(8,128)(2,1)}, bf16[8,48,768]{2,1,0:T(8,128)(2,1)}, bf16[8,48,768]{2,1,0:T(8,128)(2,1)}) custom-call(s32[2]{0:T(128)} %pad_add_fusion.meta, bf16[512,3072]{1,0:T(8,128)(2,1)} %get-tuple-element.197.du, bf16[512,1536]{1,0:T(8,128)(2,1)} %collective-permute-done.41.du_got, ...), custom_call_target="tpu_custom_call" | custom-call | flops 7699999744 | bytes 7000000 | tf_op jit(solution)/shard_map/enc_w_in_grad/pallas_call | solution.py:305
  281.2 23.8 %enc_attention_back.1 = (bf16[512,768]{1,0:T(8,128)(2,1)}, bf16[512,768]{1,0:T(8,128)(2,1)}, bf16[512,768]{1,0:T(8,128)(2,1)}, f32[12,5,256]{2,1,0:T(8,128)}, bf16[2,512,768]{2,1,0:T(8,128)(2,1)}) custom-call(s32[2]{0:T(128)} %pad_add_fusion.meta, bf16[512,768]{1,0:T(8,128)(2,1)} %get-tuple-element.224.da, bf16[512,768]{1,0:T(8,128)(2,1)} %get-tuple-element.225.q, ...), custom_call_target="tpu_custom_call" | custom-call | flops 27499999232 | bytes 25000000 | tf_op jit(solution)/shard_map/enc_attention_back/pallas_call | solution.py:305
  308.3 4.6 %collective-permute-done.46 = bf16[8,96,768]{2,1,0:T(8,128)(2,1)} collective-permute-done((bf16[8,96,768]{2,1,0:T(8,128)(2,1)}, bf16[8,96,768]{2,1,0:T(8,128)(2,1)}, u32[]{:S(2)}, u32[]{:S(2)}) %collective-permute-start.46) | collective-permute-done | bytes 1179680 | tf_op jit(solution)/shard_map/ppermute | solution.py:67
  312.9 7.9 %enc_input_grad.1 = (bf16[512,384]{1,0:T(8,128)(2,1)}, bf16[512,384]{1,0:T(8,128)(2,1)}, f32[1,768]{1,0:T(1,128)}) custom-call(s32[2]{0:T(128)} %pad_add_fusion.meta, bf16[512,768]{1,0:T(8,128)(2,1)} %get-tuple-element.247.dq, bf16[512,768]{1,0:T(8,128)(2,1)} %get-tuple-element.237.dk, bf16[512,768]{1,0:T(8,128)(2,1)} %get-tuple-element.238.dv, ...), custom_call_target="tpu_custom_call" | custom-call | flops 8800000000 | bytes 8000000 | tf_op jit(solution)/shard_map/enc_input_grad/pallas_call | solution.py:305
  324.0 2.6 collective-permute-start.50
  329.7 7.1 %enc_square_grads.1 = (bf16[8,48,768]{2,1,0:T(8,128)(2,1)}, bf16[8,48,768]{2,1,0:T(8,128)(2,1)}, bf16[8,48,768]{2,1,0:T(8,128)(2,1)}, bf16[8,48,768]{2,1,0:T(8,128)(2,1)}) custom-call(s32[2]{0:T(128)} %pad_add_fusion.meta, bf16[512,768]{1,0:T(8,128)(2,1)} %get-tuple-element.169.n1, bf16[512,768]{1,0:T(8,128)(2,1)} %collective-permute-done.26.n1_got, ...), custom_call_target="tpu_custom_call" | custom-call | flops 6600000000 | bytes 6000000 | tf_op jit(solution)/shard_map/enc_square_grads/pallas_call | solution.py:305
  337.5 6.3 %collective-permute-done.49 = bf16[4,96,768]{2,1,0:T(8,128)(2,1)} collective-permute-done((bf16[4,96,768]{2,1,0:T(8,128)(2,1)S(1)}, bf16[4,96,768]{2,1,0:T(8,128)(2,1)}, u32[]{:S(2)}, u32[]{:S(2)}) %collective-permute-start.49) | collective-permute-done | bytes 589856 | tf_op jit(solution)/shard_map/ppermute | solution.py:67
  349.2 9.0 %collective-permute-done.57 = bf16[1,96,768]{2,1,0:T(8,128)(2,1)S(1)} collective-permute-done((bf16[1,96,768]{2,1,0:T(8,128)(2,1)S(1)}, bf16[1,96,768]{2,1,0:T(8,128)(2,1)S(1)}, u32[]{:S(2)}, u32[]{:S(2)}) %collective-permute-start.57) | collective-permute-done | bytes 147488 | tf_op jit(solution)/shard_map/ppermute | solution.py:67
  363.9 2.1 broadcast_select_fusion
  366.0 5.0 %dec_weight_grads.1 = (f32[48,768]{1,0:T(8,128)}, f32[48,768]{1,0:T(8,128)}, f32[48,3072]{1,0:T(8,128)}, f32[192,768]{1,0:T(8,128)}, f32[24,768]{1,0:T(8,128)}, ...) custom-call(s32[2]{0:T(128)} %pad_add_fusion.1.place, bf16[128,6528]{1,0:T(8,128)(2,1)} %get-tuple-element.318.left, ...), custom_call_target="tpu_custom_call" | custom-call | flops 5500000256 | bytes 5000000 | tf_op jit(solution)/shard_map/dec_weight_grads/pallas_call | solution.py:305
  371.1 6.1 %collective-permute-done.54 = bf16[8,48,768]{2,1,0:T(8,128)(2,1)} collective-permute-done((bf16[8,48,768]{2,1,0:T(8,128)(2,1)S(1)}, bf16[8,48,768]{2,1,0:T(8,128)(2,1)}, u32[]{:S(2)}, u32[]{:S(2)}) %collective-permute-start.54) | collective-permute-done | bytes 589856 | tf_op jit(solution)/shard_map/ppermute | solution.py:67
  377.1 1.7 collective-permute-done.55
  379.7 4.1 all-to-all-start
  384.9 2.9 collective-permute-start.64
  393.2 12.9 %collective-permute-done.64 = bf16[1,144,768]{2,1,0:T(8,128)(2,1)S(1)} collective-permute-done((bf16[1,144,768]{2,1,0:T(8,128)(2,1)S(1)}, bf16[1,144,768]{2,1,0:T(8,128)(2,1)S(1)}, u32[]{:S(2)}, u32[]{:S(2)}) %collective-permute-start.64) | collective-permute-done | bytes 221216 | tf_op jit(solution)/shard_map/ppermute | solution.py:67
  411.2 7.5 %collective-permute-done.65 = bf16[2,96,768]{2,1,0:T(8,128)(2,1)S(1)} collective-permute-done((bf16[2,96,768]{2,1,0:T(8,128)(2,1)}, bf16[2,96,768]{2,1,0:T(8,128)(2,1)S(1)}, u32[]{:S(2)}, u32[]{:S(2)}) %collective-permute-start.65) | collective-permute-done | bytes 294944 | tf_op jit(solution)/shard_map/ppermute | solution.py:67
  422.5 6.7 %collective-permute-done.66 = bf16[1,96,768]{2,1,0:T(8,128)(2,1)S(1)} collective-permute-done((bf16[1,96,768]{2,1,0:T(8,128)(2,1)S(1)}, bf16[1,96,768]{2,1,0:T(8,128)(2,1)S(1)}, u32[]{:S(2)}, u32[]{:S(2)}) %collective-permute-start.66) | collective-permute-done | bytes 147488 | tf_op jit(solution)/shard_map/ppermute | solution.py:67
  (367 shorter events, 94.3 us)
Async XLA Ops:
  7.2 103.8 %all-gather.9.cloned.1.call-start = ((), (), s32[]{:S(2)}) async-start(), calls=%async_computation.1 | async-start | bytes 1671168 | tf_op jit(solution)/shard_map/all_gather | solution.py:906
  28.4 143.5 %all-gather.11.cloned.1.call-start = ((), (), s32[]{:S(2)}) async-start(), calls=%async_computation.2 | async-start | bytes 1671168 | tf_op jit(solution)/shard_map/all_gather | solution.py:939
  39.5 17.4 %collective-permute-start.5 = (bf16[1,192,768]{2,1,0:T(8,128)(2,1)S(1)}, bf16[1,192,768]{2,1,0:T(8,128)(2,1)S(1)}, u32[]{:S(2)}, u32[]{:S(2)}) collective-permute-start(bf16[1,192,768]{2,1,0:T(8,128)(2,1)S(1)} %slice_bitcast_fusion), channel_id=1, source_target_pairs={{0,8},{1,9},{2,10},{3,11},{4,12},{5,13},{6,14},{7,15},{8,0},{9,1},... | collective-permute-start | bytes 884744 | tf_op jit(solution)/shard_map/ppermute | solution.py:67
  57.0 18.5 %collective-permute-start.6 = (bf16[2,192,768]{2,1,0:T(8,128)(2,1)S(1)}, bf16[2,192,768]{2,1,0:T(8,128)(2,1)S(1)}, u32[]{:S(2)}, u32[]{:S(2)}) collective-permute-start(bf16[2,192,768]{2,1,0:T(8,128)(2,1)S(1)} %pad_maximum_fusion.9), channel_id=1, source_target_pairs={{0,4},{1,5},{2,6},{3,7},{4,0},{5,1},{6,2},{7,3},{8,12},{9,13},{10,... | collective-permute-start | bytes 1769480 | tf_op jit(solution)/shard_map/ppermute | solution.py:67
  57.5 18.2 %collective-permute-start.9 = (bf16[8,48,768]{2,1,0:T(8,128)(2,1)S(1)}, bf16[8,48,768]{2,1,0:T(8,128)(2,1)S(1)}, u32[]{:S(2)}, u32[]{:S(2)}) collective-permute-start(bf16[8,48,768]{2,1,0:T(8,128)(2,1)S(1)} %pad_maximum_fusion.7.rest_0_), channel_id=1, source_target_pairs={{0,16},{16,0},{1,17},{17,1},{2,18},{18,2},{3,19},{19,3},{4,20},{20... | collective-permute-start | bytes 1769480 | tf_op jit(solution)/shard_map/ppermute | solution.py:62
  57.5 18.1 %collective-permute-start.7 = (bf16[8,48,768]{2,1,0:T(8,128)(2,1)S(1)}, bf16[8,48,768]{2,1,0:T(8,128)(2,1)}, u32[]{:S(2)}, u32[]{:S(2)}) collective-permute-start(bf16[8,48,768]{2,1,0:T(8,128)(2,1)S(1)} %pad_maximum_fusion.7.rest_0_), channel_id=1, source_target_pairs={{0,2},{1,3},{2,0},{3,1},{4,6},{5,7},{6,4},{7,5},{8,10},{9,11},{10,... | collective-permute-start | bytes 1769480 | tf_op jit(solution)/shard_map/ppermute | solution.py:67
  58.2 17.5 %collective-permute-start.10 = (bf16[8,48,768]{2,1,0:T(8,128)(2,1)S(1)}, bf16[8,48,768]{2,1,0:T(8,128)(2,1)S(1)}, u32[]{:S(2)}, u32[]{:S(2)}) collective-permute-start(bf16[8,48,768]{2,1,0:T(8,128)(2,1)S(1)} %pad_maximum_fusion.8.rest_4_.rest_0_), channel_id=1, source_target_pairs={{0,16},{16,0},{1,17},{17,1},{2,18},{18,2},{3,19},{19,3},{4,20},{20... | collective-permute-start | bytes 1769480 | tf_op jit(solution)/shard_map/ppermute | solution.py:62
  58.3 18.5 %collective-permute-start.8 = (bf16[8,48,768]{2,1,0:T(8,128)(2,1)S(1)}, bf16[8,48,768]{2,1,0:T(8,128)(2,1)}, u32[]{:S(2)}, u32[]{:S(2)}) collective-permute-start(bf16[8,48,768]{2,1,0:T(8,128)(2,1)S(1)} %pad_maximum_fusion.8.rest_4_.rest_0_), channel_id=1, source_target_pairs={{0,1},{1,0},{2,3},{3,2},{4,5},{5,4},{6,7},{7,6},{8,9},{9,8},{10,11... | collective-permute-start | bytes 1769480 | tf_op jit(solution)/shard_map/ppermute | solution.py:67
  76.8 26.0 %collective-permute-start.11 = (bf16[4,96,768]{2,1,0:T(8,128)(2,1)S(1)}, bf16[4,96,768]{2,1,0:T(8,128)(2,1)}, u32[]{:S(2)}, u32[]{:S(2)}) collective-permute-start(bf16[4,96,768]{2,1,0:T(8,128)(2,1)S(1)} %get-tuple-element.154), channel_id=1, source_target_pairs={{0,1},{1,0},{2,3},{3,2},{4,5},{5,4},{6,7},{7,6},{8,9},{9,8},{10,11... | collective-permute-start | bytes 1769480 | tf_op jit(solution)/shard_map/ppermute | solution.py:67
  78.1 24.6 %collective-permute-start.13 = (bf16[1,192,768]{2,1,0:T(8,128)(2,1)S(1)}, bf16[1,192,768]{2,1,0:T(8,128)(2,1)S(1)}, u32[]{:S(2)}, u32[]{:S(2)}) collective-permute-start(bf16[1,192,768]{2,1,0:T(8,128)(2,1)S(1)} %maximum_bitcast_fusion), channel_id=1, source_target_pairs={{0,8},{1,9},{2,10},{3,11},{4,12},{5,13},{6,14},{7,15},{8,0},{9,1},... | collective-permute-start | bytes 884744 | tf_op jit(solution)/shard_map/ppermute | solution.py:67
  81.5 23.5 %collective-permute-start.12 = (bf16[4,96,768]{2,1,0:T(8,128)(2,1)S(1)}, bf16[4,96,768]{2,1,0:T(8,128)(2,1)}, u32[]{:S(2)}, u32[]{:S(2)}) collective-permute-start(bf16[4,96,768]{2,1,0:T(8,128)(2,1)S(1)} %get-tuple-element.155), channel_id=1, source_target_pairs={{0,2},{1,3},{2,0},{3,1},{4,6},{5,7},{6,4},{7,5},{8,10},{9,11},{10,... | collective-permute-start | bytes 1769480 | tf_op jit(solution)/shard_map/ppermute | solution.py:67
  82.8 24.5 %collective-permute-start.14 = (bf16[8,48,768]{2,1,0:T(8,128)(2,1)}, bf16[8,48,768]{2,1,0:T(8,128)(2,1)}, u32[]{:S(2)}, u32[]{:S(2)}) collective-permute-start(bf16[8,48,768]{2,1,0:T(8,128)(2,1)} %collective-permute-done.7.rest_1_), channel_id=1, source_target_pairs={{0,16},{16,0},{1,17},{17,1},{2,18},{18,2},{3,19},{19,3},{4,20},{20... | collective-permute-start | bytes 1769480 | tf_op jit(solution)/shard_map/ppermute | solution.py:62
  82.8 24.5 %collective-permute-start.15 = (bf16[8,48,768]{2,1,0:T(8,128)(2,1)}, bf16[8,48,768]{2,1,0:T(8,128)(2,1)}, u32[]{:S(2)}, u32[]{:S(2)}) collective-permute-start(bf16[8,48,768]{2,1,0:T(8,128)(2,1)} %collective-permute-done.8.rest_5_.rest_1_), channel_id=1, source_target_pairs={{0,16},{16,0},{1,17},{17,1},{2,18},{18,2},{3,19},{19,3},{4,20},{20... | collective-permute-start | bytes 1769480 | tf_op jit(solution)/shard_map/ppermute | solution.py:62
  108.0 35.2 %collective-permute-start.20 = (bf16[8,96,768]{2,1,0:T(8,128)(2,1)}, bf16[8,96,768]{2,1,0:T(8,128)(2,1)}, u32[]{:S(2)}, u32[]{:S(2)}) collective-permute-start(bf16[8,96,768]{2,1,0:T(8,128)(2,1)} %pad_maximum_fusion.rest_0_), channel_id=1, source_target_pairs={{0,16},{16,0},{1,17},{17,1},{2,18},{18,2},{3,19},{19,3},{4,20},{20... | collective-permute-start | bytes 3538952 | tf_op jit(solution)/shard_map/ppermute | solution.py:62
  108.0 35.2 %collective-permute-start.17 = (bf16[8,96,768]{2,1,0:T(8,128)(2,1)}, bf16[8,96,768]{2,1,0:T(8,128)(2,1)}, u32[]{:S(2)}, u32[]{:S(2)}) collective-permute-start(bf16[8,96,768]{2,1,0:T(8,128)(2,1)} %pad_maximum_fusion.rest_0_), channel_id=1, source_target_pairs={{0,2},{1,3},{2,0},{3,1},{4,6},{5,7},{6,4},{7,5},{8,10},{9,11},{10,... | collective-permute-start | bytes 3538952 | tf_op jit(solution)/shard_map/ppermute | solution.py:67
  109.3 34.0 %collective-permute-start.21 = (bf16[8,96,768]{2,1,0:T(8,128)(2,1)}, bf16[8,96,768]{2,1,0:T(8,128)(2,1)}, u32[]{:S(2)}, u32[]{:S(2)}) collective-permute-start(bf16[8,96,768]{2,1,0:T(8,128)(2,1)} %pad_maximum_fusion.1.rest_4_.rest_0_), channel_id=1, source_target_pairs={{0,16},{16,0},{1,17},{17,1},{2,18},{18,2},{3,19},{19,3},{4,20},{20... | collective-permute-start | bytes 3538952 | tf_op jit(solution)/shard_map/ppermute | solution.py:62
  109.5 33.7 %collective-permute-start.18 = (bf16[8,96,768]{2,1,0:T(8,128)(2,1)}, bf16[8,96,768]{2,1,0:T(8,128)(2,1)}, u32[]{:S(2)}, u32[]{:S(2)}) collective-permute-start(bf16[8,96,768]{2,1,0:T(8,128)(2,1)} %pad_maximum_fusion.1.rest_4_.rest_0_), channel_id=1, source_target_pairs={{0,1},{1,0},{2,3},{3,2},{4,5},{5,4},{6,7},{7,6},{8,9},{9,8},{10,11... | collective-permute-start | bytes 3538952 | tf_op jit(solution)/shard_map/ppermute | solution.py:67
  112.9 230.9 %all-gather.13.cloned.1.call-start = ((), (), s32[]{:S(2)}) async-start(), calls=%async_computation.3 | async-start | bytes 1775616 | tf_op jit(solution)/shard_map/all_gather | solution.py:988
  143.2 18.8 %collective-permute-start.22 = (bf16[4,96,768]{2,1,0:T(8,128)(2,1)S(1)}, bf16[4,96,768]{2,1,0:T(8,128)(2,1)S(1)}, u32[]{:S(2)}, u32[]{:S(2)}) collective-permute-start(bf16[4,96,768]{2,1,0:T(8,128)(2,1)S(1)} %get-tuple-element.165), channel_id=1, source_target_pairs={{0,1},{1,0},{2,3},{3,2},{4,5},{5,4},{6,7},{7,6},{8,9},{9,8},{10,11... | collective-permute-start | bytes 1769480 | tf_op jit(solution)/shard_map/ppermute | solution.py:67
  143.3 22.0 %collective-permute-start.23 = (bf16[4,96,768]{2,1,0:T(8,128)(2,1)S(1)}, bf16[4,96,768]{2,1,0:T(8,128)(2,1)S(1)}, u32[]{:S(2)}, u32[]{:S(2)}) collective-permute-start(bf16[4,96,768]{2,1,0:T(8,128)(2,1)S(1)} %get-tuple-element.166), channel_id=1, source_target_pairs={{0,2},{1,3},{2,0},{3,1},{4,6},{5,7},{6,4},{7,5},{8,10},{9,11},{10,... | collective-permute-start | bytes 1769480 | tf_op jit(solution)/shard_map/ppermute | solution.py:67
  147.0 21.8 %collective-permute-start.24 = (bf16[8,96,768]{2,1,0:T(8,128)(2,1)}, bf16[8,96,768]{2,1,0:T(8,128)(2,1)}, u32[]{:S(2)}, u32[]{:S(2)}) collective-permute-start(bf16[8,96,768]{2,1,0:T(8,128)(2,1)} %collective-permute-done.17.rest_1_), channel_id=1, source_target_pairs={{0,16},{16,0},{1,17},{17,1},{2,18},{18,2},{3,19},{19,3},{4,20},{20... | collective-permute-start | bytes 3538952 | tf_op jit(solution)/shard_map/ppermute | solution.py:62
  147.0 21.8 %collective-permute-start.25 = (bf16[8,96,768]{2,1,0:T(8,128)(2,1)}, bf16[8,96,768]{2,1,0:T(8,128)(2,1)}, u32[]{:S(2)}, u32[]{:S(2)}) collective-permute-start(bf16[8,96,768]{2,1,0:T(8,128)(2,1)} %collective-permute-done.18.rest_5_.rest_1_), channel_id=1, source_target_pairs={{0,16},{16,0},{1,17},{17,1},{2,18},{18,2},{3,19},{19,3},{4,20},{20... | collective-permute-start | bytes 3538952 | tf_op jit(solution)/shard_map/ppermute | solution.py:62
  147.5 21.0 %collective-permute-start.26 = (bf16[512,768]{1,0:T(8,128)(2,1)}, bf16[512,768]{1,0:T(8,128)(2,1)}, u32[]{:S(2)}, u32[]{:S(2)}) collective-permute-start(bf16[512,768]{1,0:T(8,128)(2,1)} %get-tuple-element.169.n1), channel_id=1, source_target_pairs={{0,16},{16,0},{1,17},{17,1},{2,18},{18,2},{3,19},{19,3},{4,20},{20... | collective-permute-start | bytes 2359304 | tf_op jit(solution)/shard_map/ppermute | solution.py:62
  168.8 22.0 %collective-permute-start.32 = (bf16[8,96,768]{2,1,0:T(8,128)(2,1)}, bf16[8,96,768]{2,1,0:T(8,128)(2,1)}, u32[]{:S(2)}, u32[]{:S(2)}) collective-permute-start(bf16[8,96,768]{2,1,0:T(8,128)(2,1)} %pad_maximum_fusion.3.rest_0_.rest_8_), channel_id=1, source_target_pairs={{0,16},{16,0},{1,17},{17,1},{2,18},{18,2},{3,19},{19,3},{4,20},{20... | collective-permute-start | bytes 3538952 | tf_op jit(solution)/shard_map/ppermute | solution.py:62
  169.1 28.4 %collective-permute-start.30 = (bf16[8,96,768]{2,1,0:T(8,128)(2,1)}, bf16[8,96,768]{2,1,0:T(8,128)(2,1)}, u32[]{:S(2)}, u32[]{:S(2)}) collective-permute-start(bf16[8,96,768]{2,1,0:T(8,128)(2,1)} %pad_maximum_fusion.3.rest_0_.rest_8_), channel_id=1, source_target_pairs={{0,1},{1,0},{2,3},{3,2},{4,5},{5,4},{6,7},{7,6},{8,9},{9,8},{10,11... | collective-permute-start | bytes 3538952 | tf_op jit(solution)/shard_map/ppermute | solution.py:67
  169.1 28.4 %collective-permute-start.31 = (bf16[8,96,768]{2,1,0:T(8,128)(2,1)S(1)}, bf16[8,96,768]{2,1,0:T(8,128)(2,1)}, u32[]{:S(2)}, u32[]{:S(2)}) collective-permute-start(bf16[8,96,768]{2,1,0:T(8,128)(2,1)S(1)} %pad_maximum_fusion.2.rest_0_.rest_4_), channel_id=1, source_target_pairs={{0,16},{16,0},{1,17},{17,1},{2,18},{18,2},{3,19},{19,3},{4,20},{20... | collective-permute-start | bytes 3538952 | tf_op jit(solution)/shard_map/ppermute | solution.py:62
  169.3 28.9 %collective-permute-start.29 = (bf16[8,96,768]{2,1,0:T(8,128)(2,1)S(1)}, bf16[8,96,768]{2,1,0:T(8,128)(2,1)}, u32[]{:S(2)}, u32[]{:S(2)}) collective-permute-start(bf16[8,96,768]{2,1,0:T(8,128)(2,1)S(1)} %pad_maximum_fusion.2.rest_0_.rest_4_), channel_id=1, source_target_pairs={{0,2},{1,3},{2,0},{3,1},{4,6},{5,7},{6,4},{7,5},{8,10},{9,11},{10,... | collective-permute-start | bytes 3538952 | tf_op jit(solution)/shard_map/ppermute | solution.py:67
  174.2 16.0 %collective-permute-start.33 = (f32[8,3072]{1,0:T(8,128)S(1)}, f32[8,3072]{1,0:T(8,128)S(1)}, u32[]{:S(2)}, u32[]{:S(2)}) collective-permute-start(f32[8,3072]{1,0:T(8,128)S(1)} %bitcast.125), channel_id=1, source_target_pairs={{0,16},{16,0},{1,17},{17,1},{2,18},{18,2},{3,19},{19,3},{4,20},{20... | collective-permute-start | bytes 294920 | tf_op jit(solution)/shard_map/ppermute | solution.py:62
  200.4 31.2 %collective-permute-start.39 = (bf16[512,3072]{1,0:T(8,128)(2,1)}, bf16[512,3072]{1,0:T(8,128)(2,1)}, u32[]{:S(2)}, u32[]{:S(2)}) collective-permute-start(bf16[512,3072]{1,0:T(8,128)(2,1)} %get-tuple-element.199.f), channel_id=1, source_target_pairs={{0,16},{16,0},{1,17},{17,1},{2,18},{18,2},{3,19},{19,3},{4,20},{20... | collective-permute-start | bytes 9437192 | tf_op jit(solution)/shard_map/ppermute | solution.py:62
  231.3 34.7 %collective-permute-start.41 = (bf16[512,1536]{1,0:T(8,128)(2,1)}, bf16[512,1536]{1,0:T(8,128)(2,1)}, u32[]{:S(2)}, u32[]{:S(2)}) collective-permute-start(bf16[512,1536]{1,0:T(8,128)(2,1)} %get-tuple-element.214), channel_id=1, source_target_pairs={{0,16},{16,0},{1,17},{17,1},{2,18},{18,2},{3,19},{19,3},{4,20},{20... | collective-permute-start | bytes 4718600 | tf_op jit(solution)/shard_map/ppermute | solution.py:62
  246.0 16.6 %collective-permute-start.60 = (bf16[8,768]{1,0:T(8,128)(2,1)}, bf16[8,768]{1,0:T(8,128)(2,1)S(1)}, u32[]{:S(2)}, u32[]{:S(2)}) collective-permute-start(bf16[8,768]{1,0:T(8,128)(2,1)} %get-tuple-element.264), channel_id=1, source_target_pairs={{0,16},{16,0},{1,17},{17,1},{2,18},{18,2},{3,19},{19,3},{4,20},{20... | collective-permute-start | bytes 36872 | tf_op jit(solution)/shard_map/ppermute | solution.py:62
  248.8 15.6 %collective-permute-start.42 = (bf16[8,48,768]{2,1,0:T(8,128)(2,1)}, bf16[8,48,768]{2,1,0:T(8,128)(2,1)S(1)}, u32[]{:S(2)}, u32[]{:S(2)}) collective-permute-start(bf16[8,48,768]{2,1,0:T(8,128)(2,1)} %get-tuple-element.216), channel_id=1, source_target_pairs={{0,2},{1,3},{2,0},{3,1},{4,6},{5,7},{6,4},{7,5},{8,10},{9,11},{10,... | collective-permute-start | bytes 1769480 | tf_op jit(solution)/shard_map/ppermute | solution.py:67
  263.4 147.7 %all-gather.15.cloned.1.call-start = ((), (), s32[]{:S(2)}) async-start(), calls=%async_computation.4 | async-start | bytes 1253376 | tf_op jit(solution)/shard_map/all_gather | solution.py:1034
  266.8 39.5 %collective-permute-start.44 = (bf16[4,48,768]{2,1,0:T(8,128)(2,1)}, bf16[4,48,768]{2,1,0:T(8,128)(2,1)}, u32[]{:S(2)}, u32[]{:S(2)}) collective-permute-start(bf16[4,48,768]{2,1,0:T(8,128)(2,1)} %get-tuple-element.337), channel_id=1, source_target_pairs={{0,1},{1,0},{2,3},{3,2},{4,5},{5,4},{6,7},{7,6},{8,9},{9,8},{10,11... | collective-permute-start | bytes 884744 | tf_op jit(solution)/shard_map/ppermute | solution.py:67
  269.5 37.9 %collective-permute-start.45 = (bf16[4,48,768]{2,1,0:T(8,128)(2,1)}, bf16[4,48,768]{2,1,0:T(8,128)(2,1)}, u32[]{:S(2)}, u32[]{:S(2)}) collective-permute-start(bf16[4,48,768]{2,1,0:T(8,128)(2,1)} %get-tuple-element.335), channel_id=1, source_target_pairs={{0,2},{1,3},{2,0},{3,1},{4,6},{5,7},{6,4},{7,5},{8,10},{9,11},{10,... | collective-permute-start | bytes 884744 | tf_op jit(solution)/shard_map/ppermute | solution.py:67
  279.3 29.0 %collective-permute-start.47 = (bf16[8,48,768]{2,1,0:T(8,128)(2,1)}, bf16[8,48,768]{2,1,0:T(8,128)(2,1)S(1)}, u32[]{:S(2)}, u32[]{:S(2)}) collective-permute-start(bf16[8,48,768]{2,1,0:T(8,128)(2,1)} %get-tuple-element.235), channel_id=1, source_target_pairs={{0,1},{1,0},{2,3},{3,2},{4,5},{5,4},{6,7},{7,6},{8,9},{9,8},{10,11... | collective-permute-start | bytes 1769480 | tf_op jit(solution)/shard_map/ppermute | solution.py:67
  279.5 33.4 %collective-permute-start.46 = (bf16[8,96,768]{2,1,0:T(8,128)(2,1)}, bf16[8,96,768]{2,1,0:T(8,128)(2,1)}, u32[]{:S(2)}, u32[]{:S(2)}) collective-permute-start(bf16[8,96,768]{2,1,0:T(8,128)(2,1)} %pad_maximum_fusion.4), channel_id=1, source_target_pairs={{0,2},{1,3},{2,0},{3,1},{4,6},{5,7},{6,4},{7,5},{8,10},{9,11},{10,... | collective-permute-start | bytes 3538952 | tf_op jit(solution)/shard_map/ppermute | solution.py:67
  312.9 16.8 %collective-permute-start.48 = (bf16[2,512,768]{2,1,0:T(8,128)(2,1)}, bf16[2,512,768]{2,1,0:T(8,128)(2,1)}, u32[]{:S(2)}, u32[]{:S(2)}) collective-permute-start(bf16[2,512,768]{2,1,0:T(8,128)(2,1)} %get-tuple-element.245), channel_id=1, source_target_pairs={{0,16},{16,0},{1,17},{17,1},{2,18},{18,2},{3,19},{19,3},{4,20},{20... | collective-permute-start | bytes 4718600 | tf_op jit(solution)/shard_map/ppermute | solution.py:62
  321.8 22.6 %collective-permute-start.61 = (f32[24,768]{1,0:T(8,128)S(1)}, f32[24,768]{1,0:T(8,128)S(1)}, u32[]{:S(2)}, u32[]{:S(2)}) collective-permute-start(f32[24,768]{1,0:T(8,128)S(1)} %concatenate.126), channel_id=1, source_target_pairs={{0,16},{16,0},{1,17},{17,1},{2,18},{18,2},{3,19},{19,3},{4,20},{20... | collective-permute-start | bytes 221192 | tf_op jit(solution)/shard_map/ppermute | solution.py:62
  343.8 20.2 %collective-permute-start.53 = (bf16[128,6528]{1,0:T(8,128)(2,1)}, bf16[128,6528]{1,0:T(8,128)(2,1)S(1)}, u32[]{:S(2)}, u32[]{:S(2)}) collective-permute-start(bf16[128,6528]{1,0:T(8,128)(2,1)} %all-gather.13.cloned.1.call-done), channel_id=1, source_target_pairs={{0,16},{16,0},{1,17},{17,1},{2,18},{18,2},{3,19},{19,3},{4,20},{20... | collective-permute-start | bytes 5013512 | tf_op jit(solution)/shard_map/ppermute | solution.py:62
  346.2 61.2 %collective-permute-start.52 = (f32[8,768]{1,0:T(8,128)}, f32[8,768]{1,0:T(8,128)}, u32[]{:S(2)}, u32[]{:S(2)}) collective-permute-start(f32[8,768]{1,0:T(8,128)} %get-tuple-element.252), channel_id=1, source_target_pairs={{0,16},{16,0},{1,17},{17,1},{2,18},{18,2},{3,19},{19,3},{4,20},{20... | collective-permute-start | bytes 73736 | tf_op jit(solution)/shard_map/ppermute | solution.py:62
  348.1 23.0 %collective-permute-start.56 = (bf16[2,144,768]{2,1,0:T(8,128)(2,1)S(1)}, bf16[2,144,768]{2,1,0:T(8,128)(2,1)}, u32[]{:S(2)}, u32[]{:S(2)}) collective-permute-start(bf16[2,144,768]{2,1,0:T(8,128)(2,1)S(1)} %get-tuple-element.321), channel_id=1, source_target_pairs={{0,4},{1,5},{2,6},{3,7},{4,0},{5,1},{6,2},{7,3},{8,12},{9,13},{10,... | collective-permute-start | bytes 1327112 | tf_op jit(solution)/shard_map/ppermute | solution.py:67
  360.6 16.5 %collective-permute-start.54 = (bf16[8,48,768]{2,1,0:T(8,128)(2,1)S(1)}, bf16[8,48,768]{2,1,0:T(8,128)(2,1)}, u32[]{:S(2)}, u32[]{:S(2)}) collective-permute-start(bf16[8,48,768]{2,1,0:T(8,128)(2,1)S(1)} %copy-done.56), channel_id=1, source_target_pairs={{0,2},{1,3},{2,0},{3,1},{4,6},{5,7},{6,4},{7,5},{8,10},{9,11},{10,... | collective-permute-start | bytes 1769480 | tf_op jit(solution)/shard_map/ppermute | solution.py:67
  361.5 17.3 %collective-permute-start.55 = (bf16[8,48,768]{2,1,0:T(8,128)(2,1)S(1)}, bf16[8,48,768]{2,1,0:T(8,128)(2,1)S(1)}, u32[]{:S(2)}, u32[]{:S(2)}) collective-permute-start(bf16[8,48,768]{2,1,0:T(8,128)(2,1)S(1)} %copy-done.55), channel_id=1, source_target_pairs={{0,1},{1,0},{2,3},{3,2},{4,5},{5,4},{6,7},{7,6},{8,9},{9,8},{10,11... | collective-permute-start | bytes 1769480 | tf_op jit(solution)/shard_map/ppermute | solution.py:67
  379.7 27.7 %all-to-all-start = ((bf16[16,8,768]{2,1,0:T(8,128)(2,1)}), bf16[16,8,768]{2,1,0:T(8,128)(2,1)S(1)}, u32[]{:S(2)}, u32[]{:S(2)}) async-start(bf16[16,8,768]{2,1,0:T(8,128)(2,1)} %bitcast.131), calls=%async_computation | async-start | bytes 393216 | tf_op jit(solution)/shard_map/all_to_all | solution.py:1021
  384.9 21.2 %collective-permute-start.64 = (bf16[1,144,768]{2,1,0:T(8,128)(2,1)S(1)}, bf16[1,144,768]{2,1,0:T(8,128)(2,1)S(1)}, u32[]{:S(2)}, u32[]{:S(2)}) collective-permute-start(bf16[1,144,768]{2,1,0:T(8,128)(2,1)S(1)} %add_convert_fusion.19), channel_id=1, source_target_pairs={{0,8},{1,9},{2,10},{3,11},{4,12},{5,13},{6,14},{7,15},{8,0},{9,1},... | collective-permute-start | bytes 663560 | tf_op jit(solution)/shard_map/ppermute | solution.py:67
  389.0 18.2 %collective-permute-start.62 = (bf16[4,48,768]{2,1,0:T(8,128)(2,1)S(1)}, bf16[4,48,768]{2,1,0:T(8,128)(2,1)S(1)}, u32[]{:S(2)}, u32[]{:S(2)}) collective-permute-start(bf16[4,48,768]{2,1,0:T(8,128)(2,1)S(1)} %get-tuple-element.328), channel_id=1, source_target_pairs={{0,1},{1,0},{2,3},{3,2},{4,5},{5,4},{6,7},{7,6},{8,9},{9,8},{10,11... | collective-permute-start | bytes 884744 | tf_op jit(solution)/shard_map/ppermute | solution.py:67
  390.7 16.6 %collective-permute-start.63 = (bf16[4,48,768]{2,1,0:T(8,128)(2,1)S(1)}, bf16[4,48,768]{2,1,0:T(8,128)(2,1)S(1)}, u32[]{:S(2)}, u32[]{:S(2)}) collective-permute-start(bf16[4,48,768]{2,1,0:T(8,128)(2,1)S(1)} %get-tuple-element.330), channel_id=1, source_target_pairs={{0,2},{1,3},{2,0},{3,1},{4,6},{5,7},{6,4},{7,5},{8,10},{9,11},{10,... | collective-permute-start | bytes 884744 | tf_op jit(solution)/shard_map/ppermute | solution.py:67
  (89 other events, 788.1 us)
Sparse Core Ops, SparseCore 0:
  28.5 74.4 all-gather.8
  113.0 58.7 all-gather.10
  263.5 56.3 all-gather.12
  345.1 60.3 all-gather.14
